TPU v7x, 128 devices: a whole 4x4x4 slice. The times are simulated.
128 devices in a mesh: row: 4 (over x_hi, core), reader: 32 (over x_lo, z, y).
Axes of the slice: x: 4 (x_hi: 2, x_lo: 2; x = x_hi * 2 + x_lo), y: 4, z: 4, core: 2. Of those that a mesh axis runs over, the one named last changes fastest.
Arguments:
- records: bfloat16 [4, 32, 256, 4096], P('row', None, 'reader'), may hold values from -6 to 6
- lengths: int32 [4, 32], replicated, may hold values from 1 to 256, as said below
- assignment: int32 [4, 32], replicated, may hold values from 0 to 31, as said below
- segment_ids: int32 [4, 32, 256], replicated, may hold values from 0 to 11, never falling along the last dimension, each value on 1 to 64 neighbouring positions
- norm_gain: float32 [4096], replicated, may hold values from 0.6 to 6
- w_qkv: bfloat16 [4096, 4, 1280], P('reader', 'row'), may hold values from -0.09375 to 0.09375
- w_out: bfloat16 [4096, 4, 1024], P('reader', 'row'), may hold values from -0.09375 to 0.09375
- score_weights: float32 [4096], replicated, may hold values from -0.09375 to 0.09375
Outputs:
- hidden_out: bfloat16 [28672, 4096], P('reader', 'row')
- record_scores: float32 [32, 4], P('reader')
Inputs may be any that keep to these rules, and one draw needn't show every extreme that they name: `assignment`: each row names every scorer shard exactly once. For every scorer shard the lengths of the records that name it, one from each row, sum to 896; some record has 256. `segment_ids`: along a record the document numbers never fall.
All inputs are finite; a program needn't handle non-finite values.
Results may differ from a plain program's by a relative error of at most 0.015.
The roundings to bfloat16 on the way count: a program that leaves them out, or rounds other values in their place, can miss the bound.
Values may be sent and summed in bfloat16 or wider, within the bound.
No kernel may reach another device: no remote copies, remote signals or barrier semaphores. Data moves between devices by JAX's collectives and lax.ppermute only.
A program may use at most 128 MiB of HBM per device.

v0:
```python
import math

import jax
import jax.numpy as jnp
from jax import lax
from jax.sharding import PartitionSpec as P

HS = 128
GROUP = 8
RECLEN = 256


ROPE_BASE = 500000.0


def rotary(values, cosine, sine):
    half = values.shape[-1] // 2
    shape = (values.shape[0],) + (1,) * (values.ndim - 2) + (half,)
    cosine = cosine.reshape(shape)
    sine = sine.reshape(shape)
    first = values[..., :half]
    second = values[..., half:]
    return jnp.concatenate(
        [first * cosine - second * sine, second * cosine + first * sine], axis=-1
    )


def masked_softmax(logits, allowed):
    held = jnp.where(allowed, logits, -1e30)
    top = jnp.max(held, axis=-1, keepdims=True)
    weights = jnp.where(allowed, jnp.exp(held - top), 0.0)
    return weights / jnp.sum(weights, axis=-1, keepdims=True)


def on_device(records, lengths, assignment, segment_ids, norm_gain, w_qkv, w_out, score_weights):
    row_count = lax.axis_size("row")
    reader_count = lax.axis_size("reader")
    row_index = lax.axis_index("row")
    reader_index = lax.axis_index("reader")
    slot_count = records.shape[2]
    width = records.shape[3]
    local_heads = w_qkv.shape[1]
    tok_rows = row_count * RECLEN - RECLEN // 2
    row_ids = jnp.arange(row_count, dtype=jnp.int32)
    chosen = jnp.argmax(assignment == reader_index, axis=1)
    record_lens = jnp.take_along_axis(lengths, chosen[:, None], axis=1)[:, 0]
    ends = jnp.cumsum(record_lens)
    starts = ends - record_lens
    place = jnp.arange(tok_rows, dtype=jnp.int32)
    owner = jnp.sum((place[:, None] >= ends[None, :-1]).astype(jnp.int32), axis=1)
    matches = owner[:, None] == row_ids[None, :]
    within = place - jnp.sum(jnp.where(matches, starts[None, :], 0), axis=1)
    picked = jnp.sum(jnp.where(matches, chosen[None, :], 0), axis=1)
    segs = segment_ids[owner, picked, within]
    own_assign = lax.dynamic_index_in_dim(assignment, row_index, 0, keepdims=False)
    readers = jnp.arange(reader_count, dtype=jnp.int32)
    outgoing = jnp.argmax(own_assign[None, :] == readers[:, None], axis=1)
    send_block = records[0][outgoing]
    arrived = lax.all_to_all(send_block, "reader", split_axis=0, concat_axis=0, tiled=True)
    own_record = arrived.reshape(1, reader_count * slot_count, width)
    gathered = lax.all_gather(own_record, "row", axis=0, tiled=True)
    packed = gathered.reshape(row_count * RECLEN, width)[owner * RECLEN + within]
    packed_f = packed.astype(jnp.float32)
    scale = lax.rsqrt(jnp.mean(packed_f * packed_f, axis=1, keepdims=True) + 1e-05)
    normed = (packed_f * scale * norm_gain).astype(jnp.bfloat16)
    full_qkv, full_out = (
        lax.all_gather(w_qkv, "reader", axis=0, tiled=True),
        lax.all_gather(w_out, "reader", axis=0, tiled=True),
    )
    projected = jnp.dot(normed, full_qkv.reshape(width, -1), preferred_element_type=jnp.float32)
    projected = projected.reshape(tok_rows, local_heads, GROUP + 2, HS)
    inv_freq = ROPE_BASE ** (-(jnp.arange(HS // 2, dtype=jnp.float32) * 2.0 / HS))
    angle = within.astype(jnp.float32)[:, None] * inv_freq[None, :]
    cosine = jnp.cos(angle)
    sine = jnp.sin(angle)
    queries = rotary(projected[:, :, :GROUP], cosine, sine).astype(jnp.bfloat16)
    keys = rotary(projected[:, :, GROUP], cosine, sine).astype(jnp.bfloat16)
    values = projected[:, :, GROUP + 1].astype(jnp.bfloat16)
    allowed = (
        (owner[:, None] == owner[None, :])
        & (segs[:, None] == segs[None, :])
        & (place[None, :] <= place[:, None])
    )
    logits = jnp.einsum("qhgd,khd->hgqk", queries, keys, preferred_element_type=jnp.float32) * (
        1.0 / math.sqrt(HS)
    )
    probs = masked_softmax(logits, allowed[None, None]).astype(jnp.bfloat16)
    mixed = jnp.einsum("hgqk,khd->qhgd", probs, values, preferred_element_type=jnp.float32).astype(
        jnp.bfloat16
    )
    mixed_flat = mixed.reshape(tok_rows, local_heads * GROUP * HS)
    partial_value = jnp.einsum(
        "tj,dj->td", mixed_flat, full_out.reshape(width, -1), preferred_element_type=jnp.float32
    )
    summed = lax.psum_scatter(
        partial_value.astype(jnp.bfloat16), "row", scatter_dimension=1, tiled=True
    ).astype(jnp.float32)
    col_width = width // row_count
    packed_cols = lax.dynamic_slice_in_dim(packed_f, row_index * col_width, col_width, 1)
    total = packed_cols + summed
    hidden_out = total.astype(jnp.bfloat16)
    score_cols = lax.dynamic_slice_in_dim(score_weights, row_index * col_width, col_width, 0)
    token_scores = jnp.dot(total, score_cols, precision=lax.Precision.HIGHEST)
    record_part = jnp.dot(
        token_scores, matches.astype(jnp.float32), precision=lax.Precision.HIGHEST
    )
    record_total = lax.psum(record_part, "row")
    record_scores = (record_total / record_lens.astype(jnp.float32))[None, :]
    return (hidden_out, record_scores)


def solution(mesh):
    in_specs = (
        P("row", None, "reader", None),
        P(),
        P(),
        P(),
        P(),
        P("reader", "row", None),
        P("reader", "row", None),
        P(),
    )
    out_specs = (P("reader", "row"), P("reader", None))
    return jax.shard_map(
        on_device, mesh=mesh, in_specs=in_specs, out_specs=out_specs, check_vma=False
    )
```

profile of v0, /device:TPU:1, one launch (start us, length us, event | category | flops | bytes accessed | tf_op | source)
XLA Modules:
  0.0 561.5 jit_solution(11207179706539714900)
XLA Ops:
  7.2 0.0 copy-start
  7.2 0.0 copy-start.4
  7.2 0.0 copy-start.2
  7.2 0.0 all-gather.4.cloned.1.call-start
  7.3 0.8 dynamic-slice_bitcast_fusion
  8.1 0.6 iota_reduce_fusion
  8.7 0.0 copy-done
  8.8 2.0 gather_fusion
  10.8 36.0 %all_to_all.5 = bf16[32,8,4096]{2,1,0:T(8,128)(2,1)} all-to-all(bf16[32,8,4096]{2,1,0:T(8,128)(2,1)} %gather_fusion), channel_id=1, replica_groups=mesh['row'=4,'reader'=32] {'reader'}, dimensions={0} | all-to-all | bytes 4194304 | tf_op jit(solution)/shard_map/all_to_all | solution.py:59
  46.8 0.0 all-gather.4.cloned.1.call-update
  46.8 0.0 all-gather.6.cloned.1.call-start
  46.9 0.7 all-gather.6.cloned.1.call-update
  47.6 0.0 all-gather.8.cloned.1.call-start
  47.6 0.7 all-gather.8.cloned.1.call-update
  48.3 0.0 reduce-scatter.2.cloned.1.call-start
  48.4 0.6 iota_reduce_fusion.1
  49.1 0.6 gather_fusion.3
  49.7 0.2 reduce-window.4
  49.9 0.1 convert_reduce_fusion
  50.0 0.1 select_reduce_fusion
  50.1 0.1 fusion.55
  50.2 0.0 copy-done.3
  50.2 9.0 %gather_fusion.2 = s32[896]{0:T(1024)S(1)} fusion(s32[4,32,256]{2,1,0:T(8,128)S(1)} %copy-done.3, s32[896]{0:T(1024)S(1)} %get-tuple-element.6), kind=kCustom, calls=%fused_computation.2 | custom fusion | bytes 17920 | tf_op jit(solution)/shard_map/gather | solution.py:54
  59.2 0.9 multiply_cosine_fusion
  60.1 1.2 fusion.15
  61.3 48.4 %all-gather.4.cloned.1.call-done = bf16[4,256,4096]{2,1,0:T(8,128)(2,1)} async-done(((bf16[1,256,4096]{2,1,0:T(8,128)(2,1)}), bf16[4,256,4096]{2,1,0:T(8,128)(2,1)}) %all-gather.4.cloned.1.call-update) | async-done | bytes 8388624 | tf_op jit(solution)/shard_map/all_gather | solution.py:61
  109.7 19.4 %gather_fusion.1 = bf16[896,4096]{1,0:T(8,128)(2,1)} fusion(bf16[1024,4096]{1,0:T(8,128)(2,1)} %bitcast.91, s32[1024]{0:T(1024)S(1)} %pad_clamp_fusion), kind=kCustom, calls=%fused_computation.1 | custom fusion | bytes 14683648 | tf_op jit(solution)/shard_map/gather | solution.py:62
  129.2 4.6 multiply_reduce_fusion
  133.8 130.7 %all-gather.6.cloned.1.call-done = bf16[4096,1,1280]{2,0,1:T(8,128)(2,1)} async-done(((bf16[128,1,1280]{2,0,1:T(8,128)(2,1)}), bf16[4096,1,1280]{2,0,1:T(8,128)(2,1)}) %all-gather.6.cloned.1.call-update) | async-done | bytes 10485776 | tf_op jit(solution)/shard_map/all_gather | solution.py:67
  264.6 14.3 %copy.22 = bf16[1280,4096]{1,0:T(8,128)(2,1)} copy(bf16[1280,4096]{0,1:T(8,128)(2,1)} %bitcast.92) | data formatting | bytes 20971520 | tf_op jit(solution)/shard_map/dot_general | solution.py:70
  278.9 15.1 %fusion.18 = f32[896,1,10,128]{0,3,2,1:T(8,128)S(1)} fusion(bf16[10,128,4096]{2,1,0:T(8,128)(2,1)} %bitcast.93, f32[4096]{0:T(1024)S(1)} %copy-done.5, f32[896]{0:T(1024)S(1)} %add_rsqrt_fusion, bf16[896,4096]{1,0:T(8,128)(2,1)} %gather_fusion.1), kind=kOutput, calls=%fused_computation.26 | convolution fusion | flops 9409921024 | bytes 22433280 | tf_op jit(solution)/shard_map/dot_general | solution.py:70
  294.0 0.9 fusion.44
  294.9 0.5 fusion.29
  295.5 11.1 %fusion = (f32[8,896]{1,0:T(8,128)S(1)}, f32[896,896,8]{1,0,2:T(8,128)}) fusion(pred[896,896]{0,1:T(8,128)(4,1)S(1)} %fusion.15, bf16[896,8,64]{0,2,1:T(8,128)(2,1)S(1)} %get-tuple-element.11, bf16[896,8,64]{0,2,1:T(8,128)(2,1)S(1)} %get-tuple-element.10, bf16[896,64]{0,1:T(8,128)(2,1)S(1)} %get-tuple-element.13, bf16[896,64]{0,1:T(8,128)(2,1)S(1)} %get-tuple-element.12), kind=kOutput, calls=%fused_computation.7 | convolution fusion | flops 1667556352 | bytes 28585984 | tf_op jit(solution)/shard_map/qhgd,khd->hgqk/dot_general | solution.py:84
  306.6 12.1 %fusion.1 = f32[8,896]{1,0:T(8,128)S(1)} fusion(f32[896,896,8]{1,0,2:T(8,128)} %get-tuple-element.17, f32[8,896]{1,0:T(8,128)S(1)} %get-tuple-element.16, pred[896,896]{0,1:T(8,128)(4,1)S(1)} %fusion.15), kind=kLoop, calls=%fused_computation.8 | loop fusion | flops 32105472 | bytes 26550272 | tf_op jit(solution)/shard_map/reduce_sum | solution.py:32
  318.6 14.9 %fusion.25 = bf16[128,8,896]{2,0,1:T(8,128)(2,1)} fusion(f32[8,896]{1,0:T(8,128)S(1)} %fusion.1, f32[8,896]{1,0:T(8,128)S(1)} %get-tuple-element.16, f32[896,896,8]{1,0,2:T(8,128)} %get-tuple-element.17, pred[896,896]{0,1:T(8,128)(4,1)S(1)} %fusion.15, f32[896,1,10,128]{0,3,2,1:T(8,128)S(1)} %fusion.18), kind=kOutput, calls=%fused_computation.33 | convolution fusion | flops 1683619840 | bytes 28614656 | tf_op jit(solution)/shard_map/hgqk,khd->qhgd/dot_general | solution.py:88
  333.5 97.7 %all-gather.8.cloned.1.call-done = bf16[4096,1,1024]{2,0,1:T(8,128)(2,1)} async-done(((bf16[128,1,1024]{2,0,1:T(8,128)(2,1)}), bf16[4096,1,1024]{2,0,1:T(8,128)(2,1)}) %all-gather.8.cloned.1.call-update) | async-done | bytes 8388624 | tf_op jit(solution)/shard_map/all_gather | solution.py:68
  431.2 12.6 %fusion.12 = bf16[896,4096]{1,0:T(8,128)(2,1)} fusion(bf16[896,1024]{0,1:T(8,128)(2,1)} %bitcast.96, bf16[4096,1,1024]{2,0,1:T(8,128)(2,1)} %all-gather.8.cloned.1.call-done), kind=kOutput, calls=%fused_computation.20 | convolution fusion | flops 7519862784 | bytes 17563648 | tf_op jit(solution)/shard_map/tj,dj->td/dot_general | solution.py:92
  443.8 0.0 reduce-scatter.2.cloned.1.call-update
  443.9 0.0 dynamic-slice-start
  443.9 0.0 copy-start.1
  443.9 10.4 %convert_element_type.57 = f32[896,4096]{1,0:T(8,128)} convert(bf16[896,4096]{1,0:T(8,128)(2,1)} %gather_fusion.1) | non-fusion elementwise | flops 3670016 | bytes 22020096 | tf_op jit(solution)/shard_map/convert_element_type | solution.py:63
  454.3 82.3 %reduce-scatter.2.cloned.1.call-done = bf16[896,1024]{1,0:T(8,128)(2,1)} async-done(((bf16[896,4096]{1,0:T(8,128)(2,1)}), bf16[896,1024]{1,0:T(8,128)(2,1)}) %reduce-scatter.2.cloned.1.call-update) | async-done | bytes 1835024 | tf_op jit(solution)/shard_map/reduce_scatter | solution.py:95
  536.7 5.9 %fusion.28 = f32[896,1]{0,1:T(1,128)S(1)} fusion(f32[1024,1]{0,1:T(1,128)S(1)} %bitcast.95, bf16[896,1024]{1,0:T(8,128)(2,1)} %reduce-scatter.2.cloned.1.call-done, f32[896,4096]{1,0:T(8,128)} %convert_element_type.57, s32[]{:T(128)} %select_n.96), kind=kOutput, calls=%fused_computation.34 | convolution fusion | flops 12845056 | bytes 5513216 | tf_op jit(solution)/shard_map/dot_general | solution.py:103
  542.6 0.1 convolution_bitcast_fusion
  542.7 7.2 %psum.7 = f32[4]{0:T(128)S(1)} all-reduce(f32[4]{0:T(128)S(1)} %convolution_bitcast_fusion), channel_id=1, replica_groups=mesh['row'=4,'reader'=32] {'row'}, use_global_device_ids=true, to_apply=%region_10.11 | all-reduce | flops 4 | bytes 32 | tf_op jit(solution)/shard_map/psum | solution.py:107
  549.9 0.5 fusion.57
  550.4 4.5 fusion.17
  (21 shorter events, 0.1 us)
Async XLA Ops:
  7.2 1.6 copy-start
  7.2 41.2 %copy-start.4 = (s32[4,32]{1,0:T(4,128)S(1)}, s32[4,32]{1,0:T(4,128)}, u32[]{:S(2)}) copy-start(s32[4,32]{1,0:T(4,128)} %param.10) | copy-start | bytes 1540
  7.2 41.9 %copy-start.2 = (s32[4,32]{1,0:T(4,128)S(1)}, s32[4,32]{1,0:T(4,128)}, u32[]{:S(2)}) copy-start(s32[4,32]{1,0:T(4,128)} %param.9) | copy-start | bytes 1540
  7.2 43.0 %copy-start.3 = (s32[4,32,256]{2,1,0:T(8,128)S(1)}, s32[4,32,256]{2,1,0:T(8,128)}, u32[]{:S(2)}) copy-start(s32[4,32,256]{2,1,0:T(8,128)} %param.11) | copy-start | bytes 393220
  7.2 102.5 %all-gather.4.cloned.1.call-start = ((), (), s32[]{:S(2)}) async-start(), calls=%async_computation.2 | async-start | bytes 10485760 | tf_op jit(solution)/shard_map/all_gather | solution.py:61
  46.8 217.7 %all-gather.6.cloned.1.call-start = ((), (), s32[]{:S(2)}) async-start(), calls=%async_computation.3 | async-start | bytes 10813440 | tf_op jit(solution)/shard_map/all_gather | solution.py:67
  47.6 383.6 %all-gather.8.cloned.1.call-start = ((), (), s32[]{:S(2)}) async-start(), calls=%async_computation.4 | async-start | bytes 8650752 | tf_op jit(solution)/shard_map/all_gather | solution.py:68
  48.3 488.3 %reduce-scatter.2.cloned.1.call-start = ((), (), s32[]{:S(2)}) async-start(), calls=%async_computation.5 | async-start | bytes 9175040 | tf_op jit(solution)/shard_map/reduce_scatter | solution.py:95
  264.6 14.3 %copy-start.5 = (f32[4096]{0:T(1024)S(1)}, f32[4096]{0:T(1024)}, u32[]{:S(2)}) copy-start(f32[4096]{0:T(1024)} %param.12) | copy-start | bytes 49156
  443.9 92.8 %dynamic-slice-start = ((f32[4096]{0:T(1024)}, s32[]{:T(128)}), f32[1024]{0:T(1024)S(1)}, s32[]{:S(2)}) async-start(f32[4096]{0:T(1024)} %param.15, s32[]{:T(128)} %select_n.96), calls=%async_computation.6 | async-start | bytes 8704 | tf_op jit(solution)/shard_map/dynamic_slice | solution.py:102
  443.9 111.0 %copy-start.1 = (bf16[1,32,8,4096]{3,2,1,0:T(8,128)(2,1)S(1)}, bf16[1,32,8,4096]{3,2,1,0:T(8,128)(2,1)}, u32[]{:S(2)}) copy-start(bf16[1,32,8,4096]{3,2,1,0:T(8,128)(2,1)} %param.8) | copy-start | bytes 6291460
Sparse Core Ops, SparseCore 0:
  47.0 62.7 all-gather.3
  111.4 153.1 all-gather.5
  266.2 164.9 all-gather.7
  444.0 92.6 reduce-scatter.1
where the time goes:
time: 562 us; the launch traced here: 561 us
  waiting for transfers between devices  361 us (64%)
  matrix products  59.7 us (11%)
  local copies, waits for them, and re-layouts  46.4 us (8%)
  blocking collectives  43.2 us (8%)
  other arithmetic  37.4 us (7%)
  between operations  14 us (2%)
    all_gather x1, waiting for transfers between devices, on_device(): lax.all_gather(w_qkv, 'reader', axis=0, tiled=True)  131 us
    all_gather x1, waiting for transfers between devices, on_device(): lax.all_gather(w_out, 'reader', axis=0, tiled=True)  97.7 us
    reduce_scatter x1, waiting for transfers between devices, on_device(): lax.psum_scatter(partial_value.astype(jnp.bfloat16), 'row', scatter_dimen...  82.3 us
    all_gather x1, waiting for transfers between devices, on_device(): gathered = lax.all_gather(own_record, 'row', axis=0, tiled=True)  48.4 us
    all_to_all x1, blocking collectives, on_device(): lax.all_to_all(send_block, 'reader', split_axis=0, concat_axis=0, tiled=T...  36 us
    gather x1, local copies, waits for them, and re-layouts, on_device(): gathered.reshape(row_count * RECLEN, width)[owner * RECLEN + within]  19.4 us
    dot_general x1, matrix products, on_device(): jnp.dot(normed, full_qkv.reshape(width, -1), preferred_element_type=jnp.f...  15.1 us
    dot_general x1, matrix products, on_device(): jnp.einsum('hgqk,khd->qhgd', probs, values, preferred_element_type=jnp.fl...  14.9 us
  transfers between devices with their start and end apart: 4, of which 4 were waited for; matrix products, arithmetic and copies ran while one was open for 21% of the time, Pallas kernels for 0%

commit v1 on v0

v1 whole, which is shorter than its diff:
```python
import math

import jax
import jax.numpy as jnp
from jax import lax
from jax.experimental import pallas as pl
from jax.experimental.pallas import tpu as pltpu
from jax.sharding import Mesh, PartitionSpec as P

HS = 128
GROUP = 8
RECLEN = 256
WIDTH = 4096
TOK = 896
QKV = (GROUP + 2) * HS
HEADS = GROUP * HS
COLS = WIDTH // 4
ROPE_BASE = 500000.0
BLK = 128
VMEM_LIMIT = 56 * 1024 * 1024

CORE_ZY = ("co", "z", "y")


def ring(axis, size, step):
    return lambda v: lax.ppermute(v, axis, [(i, (i + step) % size) for i in range(size)])


def plane_perm(step, first):
    pairs = []
    for co in range(2):
        for z in range(4):
            for y in range(4):
                along_y = (co == 0) == first
                z2, y2 = (z, (y + step) % 4) if along_y else ((z + step) % 4, y)
                pairs.append((co * 16 + z * 4 + y, co * 16 + z2 * 4 + y2))
    return lambda v: lax.ppermute(v, CORE_ZY, pairs)


def plane_gather_first(block):
    one = plane_perm(1, True)(block)
    three = plane_perm(-1, True)(block)
    two = plane_perm(2, True)(block)
    return jnp.concatenate([block, one, two, three], axis=0)


def plane_gather_second(line):
    half = line.shape[0] // 2
    one = plane_perm(1, False)(line)
    three = plane_perm(-1, False)(line)
    two_a = plane_perm(1, False)(one[:half])
    two_b = plane_perm(-1, False)(three[half:])
    return [line, one, three, two_a, two_b]


def piece_of(a, b, rows):
    if b == 0:
        return 0, a * rows
    if b == 1:
        return 1, a * rows
    if b == 3:
        return 2, a * rows
    return (3, a * rows) if a < 2 else (4, (a - 2) * rows)


def order_kernel(outgoing_ref, records_ref, out_ref, sems):
    copies = [
        pltpu.make_async_copy(records_ref.at[outgoing_ref[j]], out_ref.at[j], sems.at[j])
        for j in range(32)
    ]
    for copy in copies:
        copy.start()
    for copy in copies:
        copy.wait()


def order_records(outgoing, records):
    return pl.pallas_call(
        order_kernel,
        out_shape=jax.ShapeDtypeStruct(records.shape, records.dtype),
        in_specs=[
            pl.BlockSpec(memory_space=pltpu.SMEM),
            pl.BlockSpec(memory_space=pl.ANY),
        ],
        out_specs=pl.BlockSpec(memory_space=pl.ANY),
        scratch_shapes=[pltpu.SemaphoreType.DMA((32,))],
        cost_estimate=pl.CostEstimate(flops=0, bytes_accessed=4 << 20, transcendentals=0),
        name="order_records",
    )(outgoing, records)


def attend_kernel(
    offs_ref, xa_ref, xb_ref, gain_ref, cos_ref, sin_ref, segq_ref, segk_ref, *rest
):
    pieces = rest[:10]
    out_ref, w_ref, normed_ref, proj_ref, sems = rest[10:]
    copies = []
    for side in range(2):
        for a in range(4):
            for b in range(4):
                which, row = piece_of(a, b, BLK)
                n = side * 16 + a * 4 + b
                dst = pl.multiple_of(offs_ref[n], BLK)
                copies.append(
                    pltpu.make_async_copy(
                        pieces[side * 5 + which].at[pl.ds(row, BLK)],
                        w_ref.at[pl.ds(dst, BLK)],
                        sems.at[n],
                    )
                )
    for copy in copies:
        copy.start()
    gain = gain_ref[...]
    for part, x_ref in enumerate((xa_ref, xb_ref)):

        @pl.loop(0, RECLEN // 16)
        def _(i, part=part, x_ref=x_ref):
            row = pl.multiple_of(i * 16, 16)
            x = x_ref[pl.ds(row, 16), :].astype(jnp.float32)
            scale = lax.rsqrt(jnp.mean(x * x, axis=1, keepdims=True) + 1e-05)
            out_row = pl.multiple_of(part * RECLEN + i * 16, 16)
            normed_ref[pl.ds(out_row, 16), :] = (x * scale * gain).astype(jnp.bfloat16)

    for copy in copies:
        copy.wait()

    @pl.loop(0, QKV // 256)
    def _(n):
        col = pl.multiple_of(n * 256, 256)
        proj_ref[:, pl.ds(col, 256)] = jnp.dot(
            normed_ref[...], w_ref[:, pl.ds(col, 256)], preferred_element_type=jnp.float32
        )

    cosine = cos_ref[...]
    sine = sin_ref[...]
    place_q = lax.broadcasted_iota(jnp.int32, (RECLEN, RECLEN), 0)
    place_k = lax.broadcasted_iota(jnp.int32, (RECLEN, RECLEN), 1)
    scaling = 1.0 / math.sqrt(HS)
    for part in range(2):
        rows = pl.ds(part * RECLEN, RECLEN)
        allowed = (segq_ref[part] == segk_ref[part]) & (place_k <= place_q)
        key = proj_ref[rows, GROUP * HS : (GROUP + 1) * HS]
        key = (key * cosine + pltpu.roll(key, HS // 2, 1) * sine).astype(jnp.bfloat16)
        value = proj_ref[rows, (GROUP + 1) * HS : (GROUP + 2) * HS].astype(jnp.bfloat16)

        @pl.loop(0, GROUP)
        def _(g, rows=rows, allowed=allowed, key=key, value=value):
            col = pl.multiple_of(g * HS, HS)
            query = proj_ref[rows, pl.ds(col, HS)]
            query = (query * cosine + pltpu.roll(query, HS // 2, 1) * sine).astype(jnp.bfloat16)
            logits = (
                lax.dot_general(
                    query, key, (((1,), (1,)), ((), ())), preferred_element_type=jnp.float32
                )
                * scaling
            )
            held = jnp.where(allowed, logits, -1e30)
            top = jnp.max(held, axis=-1, keepdims=True)
            weights = jnp.where(allowed, jnp.exp(held - top), 0.0)
            probs = (weights / jnp.sum(weights, axis=-1, keepdims=True)).astype(jnp.bfloat16)
            out_ref[rows, pl.ds(col, HS)] = jnp.dot(
                probs, value, preferred_element_type=jnp.float32
            ).astype(jnp.bfloat16)


def attend(offs, xa, xb, gain, cosine, sine, segq, segk, pieces):
    vmem = pl.BlockSpec(memory_space=pltpu.VMEM)
    return pl.pallas_call(
        attend_kernel,
        out_shape=jax.ShapeDtypeStruct((2 * RECLEN, HEADS), jnp.bfloat16),
        in_specs=[pl.BlockSpec(memory_space=pltpu.SMEM)]
        + [vmem] * 7
        + [pl.BlockSpec(memory_space=pl.ANY)] * 10,
        out_specs=vmem,
        scratch_shapes=[
            pltpu.VMEM((WIDTH, QKV), jnp.bfloat16),
            pltpu.VMEM((2 * RECLEN, WIDTH), jnp.bfloat16),
            pltpu.VMEM((2 * RECLEN, QKV), jnp.float32),
            pltpu.SemaphoreType.DMA((32,)),
        ],
        compiler_params=pltpu.CompilerParams(vmem_limit_bytes=VMEM_LIMIT),
        cost_estimate=pl.CostEstimate(
            flops=2 * 512 * WIDTH * QKV, bytes_accessed=32 << 20, transcendentals=1 << 20
        ),
        name="attend",
    )(offs, xa, xb, gain, cosine, sine, segq, segk, *pieces)


def project_kernel(head, offs_ref, mixed_ref, *rest):
    pieces = rest[:5]
    away_ref, kept_ref, w_ref, sems = rest[5:]
    copies = []
    for a in range(4):
        for b in range(4):
            which, row = piece_of(a, b, 2 * BLK)
            n = a * 4 + b
            dst = pl.multiple_of(offs_ref[n], BLK)
            copies.append(
                pltpu.make_async_copy(
                    pieces[which].at[pl.ds(row + head * BLK, BLK)],
                    w_ref.at[pl.ds(dst, BLK)],
                    sems.at[n],
                )
            )
    for copy in copies:
        copy.start()
    for copy in copies:
        copy.wait()
    for part, out_ref in enumerate((away_ref, kept_ref)):

        @pl.loop(0, COLS // 256)
        def _(n, part=part, out_ref=out_ref):
            row = pl.multiple_of(part * COLS + n * 256, 256)
            col = pl.multiple_of(n * 256, 256)
            out_ref[:, pl.ds(col, 256)] = lax.dot_general(
                mixed_ref[...],
                w_ref[pl.ds(row, 256), :],
                (((1,), (1,)), ((), ())),
                preferred_element_type=jnp.float32,
            ).astype(jnp.bfloat16)


def project(offs, mixed, pieces, head):
    vmem = pl.BlockSpec(memory_space=pltpu.VMEM)
    tokens = mixed.shape[0]
    return pl.pallas_call(
        lambda *refs: project_kernel(head, *refs),
        out_shape=[jax.ShapeDtypeStruct((tokens, COLS), jnp.bfloat16)] * 2,
        in_specs=[pl.BlockSpec(memory_space=pltpu.SMEM), vmem]
        + [pl.BlockSpec(memory_space=pl.ANY)] * 5,
        out_specs=[vmem, vmem],
        scratch_shapes=[
            pltpu.VMEM((2 * COLS, HEADS), jnp.bfloat16),
            pltpu.SemaphoreType.DMA((16,)),
        ],
        compiler_params=pltpu.CompilerParams(vmem_limit_bytes=VMEM_LIMIT),
        cost_estimate=pl.CostEstimate(
            flops=2 * tokens * HEADS * 2 * COLS, bytes_accessed=10 << 20, transcendentals=0
        ),
        name=f"project_{head}",
    )(offs, mixed, *pieces)


def finish_kernel(meta_ref, *refs):
    x_refs = refs[:4]
    near_ref, near_in_ref = refs[4:6]
    far_refs = refs[6:8]
    far_in_refs = refs[8:10]
    weight_ref, hidden_ref, score_ref, acc_ref = refs[10:]
    weight = weight_ref[...]
    place = lax.broadcasted_iota(jnp.int32, (RECLEN, 1), 0)
    lane = lax.broadcasted_iota(jnp.int32, (1, 128), 1)
    token = lax.broadcasted_iota(jnp.int32, (TOK, RECLEN), 0)
    slot = lax.broadcasted_iota(jnp.int32, (TOK, RECLEN), 1)
    scores = jnp.zeros((1, 128), jnp.float32)
    for i in range(4):
        row, start, length = meta_ref[i], meta_ref[4 + i], meta_ref[8 + i]
        mine = pl.ds(i * RECLEN, RECLEN)
        theirs = pl.ds((i ^ 1) * RECLEN, RECLEN)
        far = pl.ds((i % 2) * RECLEN, RECLEN)
        far_in = pl.ds((1 - i % 2) * RECLEN, RECLEN)
        total = (
            x_refs[i][...].astype(jnp.float32)
            + near_ref[mine, :].astype(jnp.float32)
            + near_in_ref[theirs, :].astype(jnp.float32)
            + far_refs[i // 2][far, :].astype(jnp.float32)
            + far_in_refs[i // 2][far_in, :].astype(jnp.float32)
        )
        token_score = jnp.sum(total * weight, axis=1, keepdims=True)
        score = jnp.sum(jnp.where(place < length, token_score, 0.0), axis=0, keepdims=True)
        scores = scores + jnp.where(lane == row, score, 0.0)
        pick = ((token - slot == start) & (slot < length)).astype(jnp.bfloat16)
        moved = jnp.dot(pick, total.astype(jnp.bfloat16), preferred_element_type=jnp.float32)
        if i == 0:
            acc_ref[...] = moved
        else:
            acc_ref[...] += moved
    hidden_ref[...] = acc_ref[...].astype(jnp.bfloat16)
    score_ref[...] = scores


def finish(meta, records, near, near_in, fars, fars_in, weight):
    def whole(a):
        return pl.BlockSpec(a.shape, lambda i, m: (0,) * a.ndim)

    slices = pl.BlockSpec((RECLEN, COLS), lambda i, m: (0, m[12]))
    return pl.pallas_call(
        finish_kernel,
        out_shape=[
            jax.ShapeDtypeStruct((TOK, COLS), jnp.bfloat16),
            jax.ShapeDtypeStruct((1, 128), jnp.float32),
        ],
        grid_spec=pltpu.PrefetchScalarGridSpec(
            num_scalar_prefetch=1,
            grid=(1,),
            in_specs=[slices] * 4
            + [whole(near), whole(near_in)]
            + [whole(f) for f in (*fars, *fars_in)]
            + [pl.BlockSpec((1, COLS), lambda i, m: (0, m[12]))],
            out_specs=[
                pl.BlockSpec((TOK, COLS), lambda i, m: (0, 0)),
                pl.BlockSpec((1, 128), lambda i, m: (0, 0)),
            ],
            scratch_shapes=[pltpu.VMEM((TOK, COLS), jnp.float32)],
        ),
        compiler_params=pltpu.CompilerParams(vmem_limit_bytes=VMEM_LIMIT),
        cost_estimate=pl.CostEstimate(
            flops=2 * TOK * 4 * RECLEN * COLS, bytes_accessed=16 << 20, transcendentals=0
        ),
        name="finish",
    )(meta, *records, near, near_in, *fars, *fars_in, weight)


def on_device(records, lengths, assignment, segment_ids, norm_gain, w_qkv, w_out, score_weights):
    xh, co, xl, z, y = (lax.axis_index(a) for a in ("xh", "co", "xl", "z", "y"))
    row_index = xh * 2 + co
    reader_index = xl * 16 + z * 4 + y
    swap_xl, swap_xh, swap_co = ring("xl", 2, 1), ring("xh", 2, 1), ring("co", 2, 1)
    rec_ids = jnp.arange(32, dtype=jnp.int32)

    own_assign = lax.dynamic_index_in_dim(assignment, row_index, 0, keepdims=False)
    outgoing = jnp.sum(
        jnp.where(own_assign[None, :] == rec_ids[:, None], rec_ids[None, :], 0), axis=1
    )
    send_block = order_records(outgoing, records.reshape(32, 8, WIDTH))
    arrived = lax.all_to_all(
        send_block, ("xl", "z", "y"), split_axis=0, concat_axis=0, tiled=True
    )
    own_record = arrived.reshape(RECLEN, WIDTH)
    peer_record = swap_co(own_record)
    far_record = swap_xh(own_record)
    far_peer_record = swap_co(far_record)
    slots = [own_record, peer_record, far_record, far_peer_record]

    chosen = assignment == reader_index
    row_order = jnp.stack(
        [row_index, row_index + 1 - 2 * co, row_index + 2 - 4 * xh, 3 - row_index]
    )
    pick_row = row_order[:, None] == jnp.arange(4, dtype=jnp.int32)[None, :]
    lens = jnp.sum(jnp.where(chosen, lengths, 0), axis=1)
    segs = jnp.sum(jnp.where(chosen[:, :, None], segment_ids, 0), axis=1)
    local_lens = jnp.sum(jnp.where(pick_row, lens[None, :], 0), axis=1)
    before = jnp.arange(4, dtype=jnp.int32)[None, :] < row_order[:, None]
    local_starts = jnp.sum(jnp.where(before, lens[None, :], 0), axis=1)
    local_segs = jnp.sum(jnp.where(pick_row[:, :, None], segs[None], 0), axis=1)
    segq = local_segs[:, :, None]
    segk = local_segs[:, None, :]
    meta = jnp.concatenate([row_order, local_starts, local_lens, row_index[None]])

    inv_freq = ROPE_BASE ** (-(jnp.arange(HS // 2, dtype=jnp.float32) * 2.0 / HS))
    angle = jnp.arange(RECLEN, dtype=jnp.float32)[:, None] * inv_freq[None, :]
    cosine = jnp.cos(angle)
    sine = jnp.sin(angle)
    cosine = jnp.concatenate([cosine, cosine], axis=1)
    sine = jnp.concatenate([-sine, sine], axis=1)

    w_own = w_qkv.reshape(BLK, QKV)
    w_peer = swap_xl(w_own)
    qkv_pieces = plane_gather_second(plane_gather_first(w_own)) + plane_gather_second(
        plane_gather_first(w_peer)
    )

    o_own = w_out.reshape(BLK, HEADS)
    o_peer = swap_xl(o_own)
    here = xl == xh
    o_near = jnp.where(here, o_own, o_peer)
    o_far = swap_xh(jnp.where(here, o_peer, o_own))
    out_pieces = plane_gather_second(
        plane_gather_first(jnp.concatenate([o_near, o_far], axis=0))
    )

    steps_a = jnp.arange(4, dtype=jnp.int32)[:, None]
    steps_b = jnp.arange(4, dtype=jnp.int32)[None, :]
    src_z = jnp.where(co == 0, z - steps_b, z - steps_a) & 3
    src_y = jnp.where(co == 0, y - steps_a, y - steps_b) & 3
    plane = (src_z * 4 + src_y).reshape(16)
    qkv_offs = BLK * jnp.concatenate([xl * 16 + plane, (1 - xl) * 16 + plane])
    kept = ((src_z // 2) == co).astype(jnp.int32)
    out_offs = (kept * COLS + (src_z & 1) * (4 * BLK) + src_y * BLK).reshape(16)

    gain = norm_gain[None, :]
    mixed_a = attend(
        qkv_offs, slots[0], slots[1], gain, cosine, sine, segq[:2], segk[:2], qkv_pieces
    )
    mixed_b = attend(
        qkv_offs, slots[2], slots[3], gain, cosine, sine, segq[2:], segk[2:], qkv_pieces
    )
    far_b = swap_xh(mixed_a)
    far_a = swap_xh(mixed_b)
    near_away, near_kept = project(
        out_offs, jnp.concatenate([mixed_a, mixed_b], axis=0), out_pieces, 0
    )
    near_in = swap_co(near_away)
    away_b, kept_b = project(out_offs, far_b, out_pieces, 1)
    in_b = swap_co(away_b)
    away_a, kept_a = project(out_offs, far_a, out_pieces, 1)
    in_a = swap_co(away_a)
    hidden_out, scores = finish(
        meta, slots, near_kept, near_in, (kept_a, kept_b), (in_a, in_b), score_weights[None, :]
    )
    scores = lax.psum(scores[0, :4], ("xh", "co"))
    record_scores = (scores / lens.astype(jnp.float32))[None, :]
    return (hidden_out, record_scores)


def solution(mesh):
    fine = Mesh(mesh.devices.reshape(2, 2, 2, 4, 4), ("xh", "co", "xl", "z", "y"))
    row, reader = ("xh", "co"), ("xl", "z", "y")
    in_specs = (
        P(row, None, reader, None),
        P(),
        P(),
        P(),
        P(),
        P(reader, row, None),
        P(reader, row, None),
        P(),
    )
    out_specs = (P(reader, row), P(reader, None))
    return jax.shard_map(
        on_device, mesh=fine, in_specs=in_specs, out_specs=out_specs, check_vma=False
    )
```

time: 562 us -> 346 us (0.62)
  waiting for transfers between devices: 361 us -> 101 us
  Pallas kernels: 0 us -> 151 us
  matrix products: 59.7 us -> 0 us
  starting transfers between devices: 0.16 us -> 52 us
  blocking collectives: 43.2 us -> 6.64 us
  other arithmetic: 37.4 us -> 8.1 us
  local copies, waits for them, and re-layouts: 46.4 us -> 25.8 us
  between operations: 14 us -> 0.97 us
    all_gather x3 -> x0, waiting for transfers between devices: 277 us -> none  [the longest x1 131 us: on_device(): lax.all_gather(w_qkv, 'reader', axis=0, tiled=True)]
    pallas_call x0 -> x7, Pallas kernels: none -> 151 us  [the longest x1 65.6 us: order_records(): pl.pallas_call(order_kernel, out_shape=jax.ShapeDtypeStruct(records.shape...]
    ppermute x0 -> x32, waiting for transfers between devices: none -> 101 us  [the longest x21 63.3 us: plane_perm(): return lambda v: lax.ppermute(v, CORE_ZY, pairs)]
    reduce_scatter x1 -> x0, waiting for transfers between devices: 82.3 us -> none  [on_device(): lax.psum_scatter(partial_value.astype(jnp.bfloat16), 'row', scatter_dimen...]
    dot_general x6 -> x0, matrix products: 59.7 us -> none  [the longest x1 15.1 us: on_device(): jnp.dot(normed, full_qkv.reshape(width, -1), preferred_element_type=jnp.f...]
    ppermute x0 -> x32, starting transfers between devices: none -> 41.9 us  [the longest x21 25.7 us: plane_perm(): return lambda v: lax.ppermute(v, CORE_ZY, pairs)]
    all_to_all x1 -> x0, blocking collectives: 36 us -> none  [on_device(): lax.all_to_all(send_block, 'reader', split_axis=0, concat_axis=0, tiled=T...]
    gather x4 -> x0, local copies, waits for them, and re-layouts: 31.1 us -> none  [the longest x1 19.4 us: on_device(): gathered.reshape(row_count * RECLEN, width)[owner * RECLEN + within]]
  transfers between devices with their start and end apart: 4 -> 33, of which waited for: 4 -> 16; matrix products, arithmetic and copies ran while one was open for 21% -> 7% of each run, Pallas kernels for 0% -> 22%
where the time goes in v1:
time: 346 us; the launch traced here: 345 us
  Pallas kernels  151 us (44%)
  waiting for transfers between devices  101 us (29%)
  starting transfers between devices  52 us (15%)
  local copies, waits for them, and re-layouts  25.8 us (7%)
  other arithmetic  8.1 us (2%)
  blocking collectives  6.64 us (2%)
    pallas_call x1, Pallas kernels, order_records(): pl.pallas_call(order_kernel, out_shape=jax.ShapeDtypeStruct(records.shape...  65.6 us
    ppermute x21, waiting for transfers between devices, plane_perm(): return lambda v: lax.ppermute(v, CORE_ZY, pairs)  63.3 us
    pallas_call x2, Pallas kernels, attend(): pl.pallas_call(attend_kernel, out_shape=jax.ShapeDtypeStruct((2 * RECLEN,...  48.9 us
    ppermute x11, waiting for transfers between devices, ring(): lax.ppermute(v, axis, [(i, (i + step) % size) for i in range(size)])  37.2 us
    pallas_call x3, Pallas kernels, project(): pl.pallas_call(lambda *refs: project_kernel(head, *refs), out_shape=[jax....  27.8 us
    ppermute x21, starting transfers between devices, plane_perm(): return lambda v: lax.ppermute(v, CORE_ZY, pairs)  25.7 us
    ppermute x11, starting transfers between devices, ring(): lax.ppermute(v, axis, [(i, (i + step) % size) for i in range(size)])  16.2 us
    unnamed x40, local copies, waits for them, and re-layouts  11.3 us
  transfers between devices with their start and end apart: 33, of which 16 were waited for; matrix products, arithmetic and copies ran while one was open for 7% of the time, Pallas kernels for 22%

profile of v1, /device:TPU:1, one launch (start us, length us, event | category | flops | bytes accessed | tf_op | source)
XLA Modules:
  0.0 344.8 jit_solution(16750229355823678962)
XLA Ops:
  2.0 65.6 %order_records.1 = bf16[32,8,4096]{2,1,0:T(8,128)(2,1)} custom-call(s32[32]{0:T(128)} %select_reduce_fusion.2.outgoing_ref, bf16[32,8,4096]{2,1,0:T(8,128)(2,1)} %bitcast.23), custom_call_target="tpu_custom_call" | custom-call | bytes 4194304 | tf_op jit(solution)/shard_map/order_records/pallas_call | solution.py:78
  67.6 10.1 %all-to-all-start = ((bf16[32,8,4096]{2,1,0:T(8,128)(2,1)}), bf16[32,8,4096]{2,1,0:T(8,128)(2,1)}, u32[]{:S(2)}, u32[]{:S(2)}) async-start(bf16[32,8,4096]{2,1,0:T(8,128)(2,1)} %order_records.1), calls=%async_computation | async-start | bytes 4194304 | tf_op jit(solution)/shard_map/all_to_all | solution.py:326
  77.7 1.2 collective-permute-start.18
  78.9 2.5 collective-permute-start.5
  82.8 24.1 %collective-permute-done.18 = bf16[128,1024]{1,0:T(8,128)(2,1)S(1)} collective-permute-done((bf16[128,1024]{1,0:T(8,128)(2,1)S(1)}, bf16[128,1024]{1,0:T(8,128)(2,1)S(1)}, u32[]{:S(2)}, u32[]{:S(2)}) %collective-permute-start.18) | collective-permute-done | bytes 262176 | tf_op jit(solution)/shard_map/ppermute | solution.py:26
  107.6 2.5 collective-permute-start.19
  110.9 1.1 collective-permute-start.6
  112.0 1.6 collective-permute-start.7
  114.0 1.2 collective-permute-start.11
  115.2 2.6 collective-permute-start.12
  117.8 1.7 constant_dynamic-update-slice_fusion.3
  119.5 1.3 collective-permute-done.19
  120.8 2.7 collective-permute-start.13
  123.5 1.5 collective-permute-done.11
  125.8 7.3 %collective-permute-done.12 = bf16[128,1280]{1,0:T(8,128)(2,1)S(1)} collective-permute-done((bf16[128,1280]{1,0:T(8,128)(2,1)}, bf16[128,1280]{1,0:T(8,128)(2,1)S(1)}, u32[]{:S(2)}, u32[]{:S(2)}) %collective-permute-start.12) | collective-permute-done | bytes 327712 | tf_op jit(solution)/shard_map/ppermute | solution.py:37
  135.0 2.8 collective-permute-start.1
  137.8 1.7 constant_dynamic-update-slice_fusion.rest_5_
  139.5 2.9 collective-permute-done.20
  142.4 1.9 collective-permute-start.14
  144.3 10.1 %collective-permute-done.21 = bf16[256,1024]{1,0:T(8,128)(2,1)S(1)} collective-permute-done((bf16[256,1024]{1,0:T(8,128)(2,1)S(1)}, bf16[256,1024]{1,0:T(8,128)(2,1)S(1)}, u32[]{:S(2)}, u32[]{:S(2)}) %collective-permute-start.21) | collective-permute-done | bytes 524320 | tf_op jit(solution)/shard_map/ppermute | solution.py:37
  156.8 6.0 %collective-permute-done.22 = bf16[256,1024]{1,0:T(8,128)(2,1)S(1)} collective-permute-done((bf16[256,1024]{1,0:T(8,128)(2,1)S(1)}, bf16[256,1024]{1,0:T(8,128)(2,1)S(1)}, u32[]{:S(2)}, u32[]{:S(2)}) %collective-permute-start.22) | collective-permute-done | bytes 524320 | tf_op jit(solution)/shard_map/ppermute | solution.py:37
  163.7 5.7 %collective-permute-start.23 = (bf16[1024,1024]{1,0:T(8,128)(2,1)}, bf16[1024,1024]{1,0:T(8,128)(2,1)S(1)}, u32[]{:S(2)}, u32[]{:S(2)}) collective-permute-start(bf16[1024,1024]{1,0:T(8,128)(2,1)} %constant_dynamic-update-slice_fusion.4.refs_2_), channel_id=1, source_target_pairs={{0,4},{1,5},{2,6},{3,7},{4,8},{5,9},{6,10},{7,11},{8,12},{9,13},{1... | collective-permute-start | bytes 6291464 | tf_op jit(solution)/shard_map/ppermute | solution.py:37
  170.0 9.4 %collective-permute-done.1.xa_ref.refs_2_ = bf16[256,4096]{1,0:T(8,128)(2,1)} collective-permute-done((bf16[256,4096]{1,0:T(8,128)(2,1)}, bf16[256,4096]{1,0:T(8,128)(2,1)}, u32[]{:S(2)}, u32[]{:S(2)}) %collective-permute-start.1) | collective-permute-done | bytes 2097184 | tf_op jit(solution)/shard_map/ppermute | solution.py:26
  179.3 5.6 %collective-permute-start.2 = (bf16[256,4096]{1,0:T(8,128)(2,1)}, bf16[256,4096]{1,0:T(8,128)(2,1)}, u32[]{:S(2)}, u32[]{:S(2)}) collective-permute-start(bf16[256,4096]{1,0:T(8,128)(2,1)} %collective-permute-done.1.xa_ref.refs_2_), channel_id=1, source_target_pairs={{0,32},{32,0},{1,33},{33,1},{2,34},{34,2},{3,35},{35,3},{4,36},{36... | collective-permute-start | bytes 6291464 | tf_op jit(solution)/shard_map/ppermute | solution.py:26
  185.1 1.1 slice.55
  186.2 22.7 %collective-permute-done.15.rest_7_ = bf16[512,1280]{1,0:T(8,128)(2,1)} collective-permute-done((bf16[512,1280]{1,0:T(8,128)(2,1)}, bf16[512,1280]{1,0:T(8,128)(2,1)}, u32[]{:S(2)}, u32[]{:S(2)}) %collective-permute-start.15) | collective-permute-done | bytes 1310752 | tf_op jit(solution)/shard_map/ppermute | solution.py:37
  212.0 1.1 slice.56
  213.2 1.1 slice.57
  214.3 1.1 slice.58
  215.5 4.4 %collective-permute-done.8.rest_3_ = bf16[256,1280]{1,0:T(8,128)(2,1)} collective-permute-done((bf16[256,1280]{1,0:T(8,128)(2,1)S(1)}, bf16[256,1280]{1,0:T(8,128)(2,1)}, u32[]{:S(2)}, u32[]{:S(2)}) %collective-permute-start.8) | collective-permute-done | bytes 655392 | tf_op jit(solution)/shard_map/ppermute | solution.py:37
  219.9 1.4 collective-permute-start.16
  221.3 1.3 collective-permute-start.17
  226.3 1.3 slice.61
  227.6 2.0 collective-permute-done.9.rest_4_
  229.6 1.3 collective-permute-done.16.rest_8_
  230.9 1.4 collective-permute-start.26
  232.3 4.3 %collective-permute-done.17.rest_9_ = bf16[256,1280]{1,0:T(8,128)(2,1)S(1)} collective-permute-done((bf16[256,1280]{1,0:T(8,128)(2,1)S(1)}, bf16[256,1280]{1,0:T(8,128)(2,1)S(1)}, u32[]{:S(2)}, u32[]{:S(2)}) %collective-permute-start.17) | collective-permute-done | bytes 655392 | tf_op jit(solution)/shard_map/ppermute | solution.py:37
  237.5 24.4 %attend.2 = bf16[512,1024]{1,0:T(8,128)(2,1)} custom-call(s32[32]{0:T(128)} %add_multiply_fusion.offs_ref, bf16[256,4096]{1,0:T(8,128)(2,1)} %bitcast.6.xa_ref.refs_0_, bf16[256,4096]{1,0:T(8,128)(2,1)} %collective-permute-done.xb_ref.refs_1_, f32[1,4096]{1,0:T(1,128)} %bitcast.31, f32[256,128]{1,0:T(8,128)} %get-tuple-element.37.cos_ref, ...), custom_call_target="tpu_custom_call" | custom-call | flops 5368709120 | bytes 33554432 | tf_op jit(solution)/shard_map/attend/pallas_call | solution.py:168
  262.9 24.4 %attend.3 = bf16[512,1024]{1,0:T(8,128)(2,1)} custom-call(s32[32]{0:T(128)} %add_multiply_fusion.offs_ref, bf16[256,4096]{1,0:T(8,128)(2,1)} %collective-permute-done.1.xa_ref.refs_2_, bf16[256,4096]{1,0:T(8,128)(2,1)} %collective-permute-done.2.xb_ref.refs_3_, f32[1,4096]{1,0:T(1,128)} %bitcast.32, f32[256,128]{1,0:T(8,128)} %get-tuple-element.37.cos_ref, ...), custom_call_target="tpu_custom_call" | custom-call | flops 5368709120 | bytes 33554432 | tf_op jit(solution)/shard_map/attend/pallas_call | solution.py:168
  287.3 2.7 pad_maximum_fusion.refs_1_
  290.1 2.1 collective-permute-start.28
  293.5 11.1 %project_0.1 = (bf16[1024,1024]{1,0:T(8,128)(2,1)}, bf16[1024,1024]{1,0:T(8,128)(2,1)}) custom-call(s32[16]{0:T(128)} %get-tuple-element.31.refs_0_, bf16[1024,1024]{1,0:T(8,128)(2,1)} %pad_maximum_fusion.refs_1_, bf16[1024,1024]{1,0:T(8,128)(2,1)} %constant_dynamic-update-slice_fusion.4.refs_2_, bf16[1024,1024]{1,0:T(8,128)(2,1)} %copy-done, ...), custom_call_target="tpu_custom_call" | custom-call | flops 4294967296 | bytes 10485760 | tf_op jit(solution)/shard_map/project_0/pallas_call | solution.py:226
  305.8 8.4 %project_1.3 = (bf16[512,1024]{1,0:T(8,128)(2,1)}, bf16[512,1024]{1,0:T(8,128)(2,1)}) custom-call(s32[16]{0:T(128)} %get-tuple-element.31.refs_0_, bf16[512,1024]{1,0:T(8,128)(2,1)} %copy-done.6, bf16[1024,1024]{1,0:T(8,128)(2,1)} %constant_dynamic-update-slice_fusion.4.refs_2_, bf16[1024,1024]{1,0:T(8,128)(2,1)} %copy-done, ...), custom_call_target="tpu_custom_call" | custom-call | flops 2147483648 | bytes 10485760 | tf_op jit(solution)/shard_map/project_1/pallas_call | solution.py:226
  315.7 8.3 %project_1.2 = (bf16[512,1024]{1,0:T(8,128)(2,1)}, bf16[512,1024]{1,0:T(8,128)(2,1)}) custom-call(s32[16]{0:T(128)} %get-tuple-element.31.refs_0_, bf16[512,1024]{1,0:T(8,128)(2,1)} %copy-done.7, bf16[1024,1024]{1,0:T(8,128)(2,1)} %constant_dynamic-update-slice_fusion.4.refs_2_, bf16[1024,1024]{1,0:T(8,128)(2,1)} %copy-done, ...), custom_call_target="tpu_custom_call" | custom-call | flops 2147483648 | bytes 10485760 | tf_op jit(solution)/shard_map/project_1/pallas_call | solution.py:226
  325.0 2.2 collective-permute-done.30.refs_8_
  327.2 1.3 copy-done.3
  328.5 8.5 %finish.1 = (bf16[896,1024]{1,0:T(8,128)(2,1)}, f32[1,128]{1,0:T(1,128)}) custom-call(s32[13]{0:T(128)} %concatenate.29.meta_ref, bf16[256,4096]{1,0:T(8,128)(2,1)} %bitcast.6.xa_ref.refs_0_, bf16[256,4096]{1,0:T(8,128)(2,1)} %collective-permute-done.xb_ref.refs_1_, bf16[256,4096]{1,0:T(8,128)(2,1)} %collective-permute-done.1.xa_ref.refs_2_, ...), custom_call_target="tpu_custom_call" | custom-call | flops 1879048192 | bytes 16777216 | tf_op jit(solution)/shard_map/finish/pallas_call | solution.py:287
  337.7 6.6 %psum.7 = f32[4]{0:T(128)S(1)} all-reduce(f32[4]{0:T(128)S(1)} %slice_bitcast_fusion), channel_id=1, replica_groups=mesh['xh'=2,'co'=2,'xl'=2,'z'=4,'y'=4] {'xh','co'}, use_global_device_ids=true, to_apply=%region_6.7 | all-reduce | flops 4 | bytes 32 | tf_op jit(solution)/shard_map/psum | solution.py:401
  (104 shorter events, 26.0 us)
Async XLA Ops:
  67.6 10.1 %copy-start.10 = (bf16[128,1,1024]{2,0,1:T(8,128)(2,1)S(1)}, bf16[128,1,1024]{2,0,1:T(8,128)(2,1)}, u32[]{:S(2)}) copy-start(bf16[128,1,1024]{2,0,1:T(8,128)(2,1)} %param.14) | copy-start | bytes 786436
  67.6 11.4 %copy-start.9 = (bf16[128,1,1280]{2,0,1:T(8,128)(2,1)S(1)}, bf16[128,1,1280]{2,0,1:T(8,128)(2,1)}, u32[]{:S(2)}) copy-start(bf16[128,1,1280]{2,0,1:T(8,128)(2,1)} %param.13) | copy-start | bytes 983044
  67.6 67.4 %all-to-all-start = ((bf16[32,8,4096]{2,1,0:T(8,128)(2,1)}), bf16[32,8,4096]{2,1,0:T(8,128)(2,1)}, u32[]{:S(2)}, u32[]{:S(2)}) async-start(bf16[32,8,4096]{2,1,0:T(8,128)(2,1)} %order_records.1), calls=%async_computation | async-start | bytes 4194304 | tf_op jit(solution)/shard_map/all_to_all | solution.py:326
  77.7 29.1 %collective-permute-start.18 = (bf16[128,1024]{1,0:T(8,128)(2,1)S(1)}, bf16[128,1024]{1,0:T(8,128)(2,1)S(1)}, u32[]{:S(2)}, u32[]{:S(2)}) collective-permute-start(bf16[128,1024]{1,0:T(8,128)(2,1)S(1)} %bitcast.29), channel_id=1, source_target_pairs={{0,16},{16,0},{1,17},{17,1},{2,18},{18,2},{3,19},{19,3},{4,20},{20... | collective-permute-start | bytes 786440 | tf_op jit(solution)/shard_map/ppermute | solution.py:26
  78.9 31.2 %collective-permute-start.5 = (bf16[128,1280]{1,0:T(8,128)(2,1)S(1)}, bf16[128,1280]{1,0:T(8,128)(2,1)S(1)}, u32[]{:S(2)}, u32[]{:S(2)}) collective-permute-start(bf16[128,1280]{1,0:T(8,128)(2,1)S(1)} %bitcast.24), channel_id=1, source_target_pairs={{0,3},{1,0},{2,1},{3,2},{4,7},{5,4},{6,5},{7,6},{8,11},{9,8},{10,9... | collective-permute-start | bytes 983048 | tf_op jit(solution)/shard_map/ppermute | solution.py:37
  81.4 28.7 %collective-permute-start.4 = (bf16[128,1280]{1,0:T(8,128)(2,1)S(1)}, bf16[128,1280]{1,0:T(8,128)(2,1)S(1)}, u32[]{:S(2)}, u32[]{:S(2)}) collective-permute-start(bf16[128,1280]{1,0:T(8,128)(2,1)S(1)} %bitcast.25), channel_id=1, source_target_pairs={{0,2},{1,3},{2,0},{3,1},{4,6},{5,7},{6,4},{7,5},{8,10},{9,11},{10,... | collective-permute-start | bytes 983048 | tf_op jit(solution)/shard_map/ppermute | solution.py:37
  81.9 28.9 %collective-permute-start.3 = (bf16[128,1280]{1,0:T(8,128)(2,1)S(1)}, bf16[128,1280]{1,0:T(8,128)(2,1)S(1)}, u32[]{:S(2)}, u32[]{:S(2)}) collective-permute-start(bf16[128,1280]{1,0:T(8,128)(2,1)S(1)} %bitcast.26), channel_id=1, source_target_pairs={{0,1},{1,2},{2,3},{3,0},{4,5},{5,6},{6,7},{7,4},{8,9},{9,10},{10,1... | collective-permute-start | bytes 983048 | tf_op jit(solution)/shard_map/ppermute | solution.py:37
  82.5 31.4 %collective-permute-start.10 = (bf16[128,1280]{1,0:T(8,128)(2,1)S(1)}, bf16[128,1280]{1,0:T(8,128)(2,1)}, u32[]{:S(2)}, u32[]{:S(2)}) collective-permute-start(bf16[128,1280]{1,0:T(8,128)(2,1)S(1)} %bitcast.27), channel_id=1, source_target_pairs={{0,16},{16,0},{1,17},{17,1},{2,18},{18,2},{3,19},{19,3},{4,20},{20... | collective-permute-start | bytes 983048 | tf_op jit(solution)/shard_map/ppermute | solution.py:26
  107.6 13.2 %collective-permute-start.19 = (bf16[128,1024]{1,0:T(8,128)(2,1)S(1)}, bf16[128,1024]{1,0:T(8,128)(2,1)S(1)}, u32[]{:S(2)}, u32[]{:S(2)}) collective-permute-start(bf16[128,1024]{1,0:T(8,128)(2,1)S(1)} %get-tuple-element.24), channel_id=1, source_target_pairs={{0,64},{64,0},{1,65},{65,1},{2,66},{66,2},{3,67},{67,3},{4,68},{68... | collective-permute-start | bytes 786440 | tf_op jit(solution)/shard_map/ppermute | solution.py:26
  110.9 44.3 %copy-start.4 = (bf16[512,1280]{1,0:T(8,128)(2,1)}, bf16[512,1280]{1,0:T(8,128)(2,1)S(1)}, u32[]{:S(2)}) copy-start(bf16[512,1280]{1,0:T(8,128)(2,1)S(1)} %pad_maximum_fusion.1.rest_0_) | copy-start | bytes 3932164
  110.9 58.5 %collective-permute-start.6 = (bf16[512,1280]{1,0:T(8,128)(2,1)S(1)}, bf16[512,1280]{1,0:T(8,128)(2,1)}, u32[]{:S(2)}, u32[]{:S(2)}) collective-permute-start(bf16[512,1280]{1,0:T(8,128)(2,1)S(1)} %pad_maximum_fusion.1.rest_0_), channel_id=1, source_target_pairs={{0,4},{1,5},{2,6},{3,7},{4,8},{5,9},{6,10},{7,11},{8,12},{9,13},{1... | collective-permute-start | bytes 3932168 | tf_op jit(solution)/shard_map/ppermute | solution.py:37
  112.0 57.4 %collective-permute-start.7 = (bf16[512,1280]{1,0:T(8,128)(2,1)S(1)}, bf16[512,1280]{1,0:T(8,128)(2,1)}, u32[]{:S(2)}, u32[]{:S(2)}) collective-permute-start(bf16[512,1280]{1,0:T(8,128)(2,1)S(1)} %pad_maximum_fusion.1.rest_0_), channel_id=1, source_target_pairs={{0,12},{1,13},{2,14},{3,15},{4,0},{5,1},{6,2},{7,3},{8,4},{9,5},{1... | collective-permute-start | bytes 3932168 | tf_op jit(solution)/shard_map/ppermute | solution.py:37
  114.0 11.1 %collective-permute-start.11 = (bf16[128,1280]{1,0:T(8,128)(2,1)}, bf16[128,1280]{1,0:T(8,128)(2,1)S(1)}, u32[]{:S(2)}, u32[]{:S(2)}) collective-permute-start(bf16[128,1280]{1,0:T(8,128)(2,1)} %collective-permute-done.10), channel_id=1, source_target_pairs={{0,1},{1,2},{2,3},{3,0},{4,5},{5,6},{6,7},{7,4},{8,9},{9,10},{10,1... | collective-permute-start | bytes 983048 | tf_op jit(solution)/shard_map/ppermute | solution.py:37
  115.2 17.9 %collective-permute-start.12 = (bf16[128,1280]{1,0:T(8,128)(2,1)}, bf16[128,1280]{1,0:T(8,128)(2,1)S(1)}, u32[]{:S(2)}, u32[]{:S(2)}) collective-permute-start(bf16[128,1280]{1,0:T(8,128)(2,1)} %collective-permute-done.10), channel_id=1, source_target_pairs={{0,2},{1,3},{2,0},{3,1},{4,6},{5,7},{6,4},{7,5},{8,10},{9,11},{10,... | collective-permute-start | bytes 983048 | tf_op jit(solution)/shard_map/ppermute | solution.py:37
  120.8 14.1 %collective-permute-start.13 = (bf16[128,1280]{1,0:T(8,128)(2,1)}, bf16[128,1280]{1,0:T(8,128)(2,1)}, u32[]{:S(2)}, u32[]{:S(2)}) collective-permute-start(bf16[128,1280]{1,0:T(8,128)(2,1)} %collective-permute-done.10), channel_id=1, source_target_pairs={{0,3},{1,0},{2,1},{3,2},{4,7},{5,4},{6,5},{7,6},{8,11},{9,8},{10,9... | collective-permute-start | bytes 983048 | tf_op jit(solution)/shard_map/ppermute | solution.py:37
  125.0 17.4 %collective-permute-start.20 = (bf16[256,1024]{1,0:T(8,128)(2,1)S(1)}, bf16[256,1024]{1,0:T(8,128)(2,1)S(1)}, u32[]{:S(2)}, u32[]{:S(2)}) collective-permute-start(bf16[256,1024]{1,0:T(8,128)(2,1)S(1)} %pad_maximum_fusion.2), channel_id=1, source_target_pairs={{0,1},{1,2},{2,3},{3,0},{4,5},{5,6},{6,7},{7,4},{8,9},{9,10},{10,1... | collective-permute-start | bytes 1572872 | tf_op jit(solution)/shard_map/ppermute | solution.py:37
  133.1 21.4 %collective-permute-start.21 = (bf16[256,1024]{1,0:T(8,128)(2,1)S(1)}, bf16[256,1024]{1,0:T(8,128)(2,1)S(1)}, u32[]{:S(2)}, u32[]{:S(2)}) collective-permute-start(bf16[256,1024]{1,0:T(8,128)(2,1)S(1)} %pad_maximum_fusion.2), channel_id=1, source_target_pairs={{0,2},{1,3},{2,0},{3,1},{4,6},{5,7},{6,4},{7,5},{8,10},{9,11},{10,... | collective-permute-start | bytes 1572872 | tf_op jit(solution)/shard_map/ppermute | solution.py:37
  135.0 34.9 %copy-start.12 = (s32[4,32]{1,0:T(4,128)S(1)}, s32[4,32]{1,0:T(4,128)}, u32[]{:S(2)}) copy-start(s32[4,32]{1,0:T(4,128)} %param.9) | copy-start | bytes 1540
  135.0 34.9 %copy-start.13 = (s32[4,32]{1,0:T(4,128)S(1)}, s32[4,32]{1,0:T(4,128)}, u32[]{:S(2)}) copy-start(s32[4,32]{1,0:T(4,128)} %param.10) | copy-start | bytes 1540
  135.0 50.0 %copy-start.11 = (s32[4,32,256]{2,1,0:T(8,128)S(1)}, s32[4,32,256]{2,1,0:T(8,128)}, u32[]{:S(2)}) copy-start(s32[4,32,256]{2,1,0:T(8,128)} %param.11) | copy-start | bytes 393220
  135.0 44.4 %collective-permute-start.1 = (bf16[256,4096]{1,0:T(8,128)(2,1)}, bf16[256,4096]{1,0:T(8,128)(2,1)}, u32[]{:S(2)}, u32[]{:S(2)}) collective-permute-start(bf16[256,4096]{1,0:T(8,128)(2,1)} %bitcast.6.xa_ref.refs_0_), channel_id=1, source_target_pairs={{0,64},{64,0},{1,65},{65,1},{2,66},{66,2},{3,67},{67,3},{4,68},{68... | collective-permute-start | bytes 6291464 | tf_op jit(solution)/shard_map/ppermute | solution.py:26
  142.4 27.1 %collective-permute-start.14 = (bf16[512,1280]{1,0:T(8,128)(2,1)}, bf16[512,1280]{1,0:T(8,128)(2,1)}, u32[]{:S(2)}, u32[]{:S(2)}) collective-permute-start(bf16[512,1280]{1,0:T(8,128)(2,1)} %constant_dynamic-update-slice_fusion.rest_5_), channel_id=1, source_target_pairs={{0,4},{1,5},{2,6},{3,7},{4,8},{5,9},{6,10},{7,11},{8,12},{9,13},{1... | collective-permute-start | bytes 3932168 | tf_op jit(solution)/shard_map/ppermute | solution.py:37
  154.4 8.4 %collective-permute-start.22 = (bf16[256,1024]{1,0:T(8,128)(2,1)S(1)}, bf16[256,1024]{1,0:T(8,128)(2,1)S(1)}, u32[]{:S(2)}, u32[]{:S(2)}) collective-permute-start(bf16[256,1024]{1,0:T(8,128)(2,1)S(1)} %pad_maximum_fusion.2), channel_id=1, source_target_pairs={{0,3},{1,0},{2,1},{3,2},{4,7},{5,4},{6,5},{7,6},{8,11},{9,8},{10,9... | collective-permute-start | bytes 1572872 | tf_op jit(solution)/shard_map/ppermute | solution.py:37
  163.7 56.2 %collective-permute-start.23 = (bf16[1024,1024]{1,0:T(8,128)(2,1)}, bf16[1024,1024]{1,0:T(8,128)(2,1)S(1)}, u32[]{:S(2)}, u32[]{:S(2)}) collective-permute-start(bf16[1024,1024]{1,0:T(8,128)(2,1)} %constant_dynamic-update-slice_fusion.4.refs_2_), channel_id=1, source_target_pairs={{0,4},{1,5},{2,6},{3,7},{4,8},{5,9},{6,10},{7,11},{8,12},{9,13},{1... | collective-permute-start | bytes 6291464 | tf_op jit(solution)/shard_map/ppermute | solution.py:37
  169.4 52.0 %collective-permute-start.24 = (bf16[1024,1024]{1,0:T(8,128)(2,1)}, bf16[1024,1024]{1,0:T(8,128)(2,1)}, u32[]{:S(2)}, u32[]{:S(2)}) collective-permute-start(bf16[1024,1024]{1,0:T(8,128)(2,1)} %constant_dynamic-update-slice_fusion.4.refs_2_), channel_id=1, source_target_pairs={{0,12},{1,13},{2,14},{3,15},{4,0},{5,1},{6,2},{7,3},{8,4},{9,5},{1... | collective-permute-start | bytes 6291464 | tf_op jit(solution)/shard_map/ppermute | solution.py:37
  169.4 39.5 %collective-permute-start.15 = (bf16[512,1280]{1,0:T(8,128)(2,1)}, bf16[512,1280]{1,0:T(8,128)(2,1)}, u32[]{:S(2)}, u32[]{:S(2)}) collective-permute-start(bf16[512,1280]{1,0:T(8,128)(2,1)} %constant_dynamic-update-slice_fusion.rest_5_), channel_id=1, source_target_pairs={{0,12},{1,13},{2,14},{3,15},{4,0},{5,1},{6,2},{7,3},{8,4},{9,5},{1... | collective-permute-start | bytes 3932168 | tf_op jit(solution)/shard_map/ppermute | solution.py:37
  169.5 67.1 %collective-permute-start = (bf16[256,4096]{1,0:T(8,128)(2,1)}, bf16[256,4096]{1,0:T(8,128)(2,1)}, u32[]{:S(2)}, u32[]{:S(2)}) collective-permute-start(bf16[256,4096]{1,0:T(8,128)(2,1)} %bitcast.6.xa_ref.refs_0_), channel_id=1, source_target_pairs={{0,32},{32,0},{1,33},{33,1},{2,34},{34,2},{3,35},{35,3},{4,36},{36... | collective-permute-start | bytes 6291464 | tf_op jit(solution)/shard_map/ppermute | solution.py:26
  179.3 83.5 %collective-permute-start.2 = (bf16[256,4096]{1,0:T(8,128)(2,1)}, bf16[256,4096]{1,0:T(8,128)(2,1)}, u32[]{:S(2)}, u32[]{:S(2)}) collective-permute-start(bf16[256,4096]{1,0:T(8,128)(2,1)} %collective-permute-done.1.xa_ref.refs_2_), channel_id=1, source_target_pairs={{0,32},{32,0},{1,33},{33,1},{2,34},{34,2},{3,35},{35,3},{4,36},{36... | collective-permute-start | bytes 6291464 | tf_op jit(solution)/shard_map/ppermute | solution.py:26
  208.9 10.9 %collective-permute-start.8 = (bf16[256,1280]{1,0:T(8,128)(2,1)S(1)}, bf16[256,1280]{1,0:T(8,128)(2,1)}, u32[]{:S(2)}, u32[]{:S(2)}) collective-permute-start(bf16[256,1280]{1,0:T(8,128)(2,1)S(1)} %slice.55), channel_id=1, source_target_pairs={{0,4},{1,5},{2,6},{3,7},{4,8},{5,9},{6,10},{7,11},{8,12},{9,13},{1... | collective-permute-start | bytes 1966088 | tf_op jit(solution)/shard_map/ppermute | solution.py:37
  219.9 9.7 %collective-permute-start.9 = (bf16[256,1280]{1,0:T(8,128)(2,1)S(1)}, bf16[256,1280]{1,0:T(8,128)(2,1)S(1)}, u32[]{:S(2)}, u32[]{:S(2)}) collective-permute-start(bf16[256,1280]{1,0:T(8,128)(2,1)S(1)} %slice.56), channel_id=1, source_target_pairs={{0,12},{1,13},{2,14},{3,15},{4,0},{5,1},{6,2},{7,3},{8,4},{9,5},{1... | collective-permute-start | bytes 1966088 | tf_op jit(solution)/shard_map/ppermute | solution.py:37
  219.9 7.7 %copy-start = (bf16[1024,1024]{1,0:T(8,128)(2,1)}, bf16[1024,1024]{1,0:T(8,128)(2,1)S(1)}, u32[]{:S(2)}) copy-start(bf16[1024,1024]{1,0:T(8,128)(2,1)S(1)} %collective-permute-done.23.refs_3_) | copy-start | bytes 6291460
  219.9 11.0 %collective-permute-start.16 = (bf16[256,1280]{1,0:T(8,128)(2,1)S(1)}, bf16[256,1280]{1,0:T(8,128)(2,1)S(1)}, u32[]{:S(2)}, u32[]{:S(2)}) collective-permute-start(bf16[256,1280]{1,0:T(8,128)(2,1)S(1)} %slice.57), channel_id=1, source_target_pairs={{0,4},{1,5},{2,6},{3,7},{4,8},{5,9},{6,10},{7,11},{8,12},{9,13},{1... | collective-permute-start | bytes 1966088 | tf_op jit(solution)/shard_map/ppermute | solution.py:37
  221.3 15.3 %collective-permute-start.17 = (bf16[256,1280]{1,0:T(8,128)(2,1)S(1)}, bf16[256,1280]{1,0:T(8,128)(2,1)S(1)}, u32[]{:S(2)}, u32[]{:S(2)}) collective-permute-start(bf16[256,1280]{1,0:T(8,128)(2,1)S(1)} %slice.58), channel_id=1, source_target_pairs={{0,12},{1,13},{2,14},{3,15},{4,0},{5,1},{6,2},{7,3},{8,4},{9,5},{1... | collective-permute-start | bytes 1966088 | tf_op jit(solution)/shard_map/ppermute | solution.py:37
  229.6 7.0 %copy-start.14 = (bf16[256,1280]{1,0:T(8,128)(2,1)}, bf16[256,1280]{1,0:T(8,128)(2,1)S(1)}, u32[]{:S(2)}) copy-start(bf16[256,1280]{1,0:T(8,128)(2,1)S(1)} %collective-permute-done.9.rest_4_) | copy-start | bytes 1966084
  229.6 62.6 %collective-permute-start.25 = (bf16[512,1024]{1,0:T(8,128)(2,1)}, bf16[512,1024]{1,0:T(8,128)(2,1)S(1)}, u32[]{:S(2)}, u32[]{:S(2)}) collective-permute-start(bf16[512,1024]{1,0:T(8,128)(2,1)} %slice.60), channel_id=1, source_target_pairs={{0,4},{1,5},{2,6},{3,7},{4,8},{5,9},{6,10},{7,11},{8,12},{9,13},{1... | collective-permute-start | bytes 3145736 | tf_op jit(solution)/shard_map/ppermute | solution.py:37
  230.9 5.7 %copy-start.15 = (bf16[256,1280]{1,0:T(8,128)(2,1)}, bf16[256,1280]{1,0:T(8,128)(2,1)S(1)}, u32[]{:S(2)}) copy-start(bf16[256,1280]{1,0:T(8,128)(2,1)S(1)} %collective-permute-done.16.rest_8_) | copy-start | bytes 1966084
  230.9 61.3 %collective-permute-start.26 = (bf16[512,1024]{1,0:T(8,128)(2,1)S(1)}, bf16[512,1024]{1,0:T(8,128)(2,1)S(1)}, u32[]{:S(2)}, u32[]{:S(2)}) collective-permute-start(bf16[512,1024]{1,0:T(8,128)(2,1)S(1)} %slice.61), channel_id=1, source_target_pairs={{0,12},{1,13},{2,14},{3,15},{4,0},{5,1},{6,2},{7,3},{8,4},{9,5},{1... | collective-permute-start | bytes 3145736 | tf_op jit(solution)/shard_map/ppermute | solution.py:37
  261.9 25.4 %copy-start.8 = (bf16[512,1024]{1,0:T(8,128)(2,1)S(1)}, bf16[512,1024]{1,0:T(8,128)(2,1)}, u32[]{:S(2)}) copy-start(bf16[512,1024]{1,0:T(8,128)(2,1)} %attend.2) | copy-start | bytes 3145732
  261.9 42.9 %collective-permute-start.29 = (bf16[512,1024]{1,0:T(8,128)(2,1)}, bf16[512,1024]{1,0:T(8,128)(2,1)S(1)}, u32[]{:S(2)}, u32[]{:S(2)}) collective-permute-start(bf16[512,1024]{1,0:T(8,128)(2,1)} %attend.2), channel_id=1, source_target_pairs={{0,64},{64,0},{1,65},{65,1},{2,66},{66,2},{3,67},{67,3},{4,68},{68... | collective-permute-start | bytes 3145736 | tf_op jit(solution)/shard_map/ppermute | solution.py:26
  290.1 24.7 %collective-permute-start.28 = (bf16[512,1024]{1,0:T(8,128)(2,1)}, bf16[512,1024]{1,0:T(8,128)(2,1)S(1)}, u32[]{:S(2)}, u32[]{:S(2)}) collective-permute-start(bf16[512,1024]{1,0:T(8,128)(2,1)} %attend.3), channel_id=1, source_target_pairs={{0,64},{64,0},{1,65},{65,1},{2,66},{66,2},{3,67},{67,3},{4,68},{68... | collective-permute-start | bytes 3145736 | tf_op jit(solution)/shard_map/ppermute | solution.py:26
  292.2 1.4 copy-start.2
  304.7 22.5 %collective-permute-start.27 = (bf16[1024,1024]{1,0:T(8,128)(2,1)}, bf16[1024,1024]{1,0:T(8,128)(2,1)S(1)}, u32[]{:S(2)}, u32[]{:S(2)}) collective-permute-start(bf16[1024,1024]{1,0:T(8,128)(2,1)} %get-tuple-element.11), channel_id=1, source_target_pairs={{0,32},{32,0},{1,33},{33,1},{2,34},{34,2},{3,35},{35,3},{4,36},{36... | collective-permute-start | bytes 6291464 | tf_op jit(solution)/shard_map/ppermute | solution.py:26
  304.8 1.0 copy-start.6
  314.2 10.8 %collective-permute-start.31 = (bf16[512,1024]{1,0:T(8,128)(2,1)}, bf16[512,1024]{1,0:T(8,128)(2,1)S(1)}, u32[]{:S(2)}, u32[]{:S(2)}) collective-permute-start(bf16[512,1024]{1,0:T(8,128)(2,1)} %get-tuple-element.15), channel_id=1, source_target_pairs={{0,32},{32,0},{1,33},{33,1},{2,34},{34,2},{3,35},{35,3},{4,36},{36... | collective-permute-start | bytes 3145736 | tf_op jit(solution)/shard_map/ppermute | solution.py:26
  314.7 1.0 copy-start.7
  324.1 3.1 collective-permute-start.30
  325.0 2.2 copy-start.5
  327.2 1.4 copy-start.3
  (2 other events, 1.8 us)

commit v2 on v1

v2 whole, which is shorter than its diff:
```python
import math

import jax
import jax.numpy as jnp
from jax import lax
from jax.experimental import pallas as pl
from jax.experimental.pallas import tpu as pltpu
from jax.sharding import Mesh, PartitionSpec as P

HS = 128
GROUP = 8
RECLEN = 256
WIDTH = 4096
TOK = 896
QKV = (GROUP + 2) * HS
HEADS = GROUP * HS
COLS = WIDTH // 4
ROPE_BASE = 500000.0
BLK = 128
QBLK = 256
ATTEND_VMEM = 16 << 20
SMALL_VMEM = 12 << 20
PROJECT_VMEM = 16 << 20
FINISH_VMEM = 28 << 20

CORE_ZY = ("co", "z", "y")


def ring(axis, size, step):
    return lambda v: lax.ppermute(v, axis, [(i, (i + step) % size) for i in range(size)])


def plane_perm(step, first):
    pairs = []
    for co in range(2):
        for z in range(4):
            for y in range(4):
                along_y = (co == 0) == first
                z2, y2 = (z, (y + step) % 4) if along_y else ((z + step) % 4, y)
                pairs.append((co * 16 + z * 4 + y, co * 16 + z2 * 4 + y2))
    return lambda v: lax.ppermute(v, CORE_ZY, pairs)


def stack_kernel(plan, *refs):
    out_ref = refs[-1]
    to = 0
    for which, row, rows in plan:
        out_ref[to : to + rows] = refs[which][row : row + rows]
        to += rows


def stack(arrays, plan, after=None):
    rows = sum(p[2] for p in plan)
    held = [] if after is None else after if isinstance(after, list) else [after]
    return pl.pallas_call(
        lambda *refs: stack_kernel(plan, *refs),
        out_shape=jax.ShapeDtypeStruct((rows, arrays[0].shape[1]), arrays[0].dtype),
        in_specs=[pl.BlockSpec(memory_space=pltpu.VMEM)] * len(arrays)
        + [pl.BlockSpec(memory_space=pl.ANY)] * len(held),
        out_specs=pl.BlockSpec(memory_space=pltpu.VMEM),
        compiler_params=pltpu.CompilerParams(vmem_limit_bytes=SMALL_VMEM),
        cost_estimate=pl.CostEstimate(flops=0, bytes_accessed=1 << 20, transcendentals=0),
        name="stack",
    )(*arrays, *held)


def plane_gather_first(block, groups, after=None):
    one = plane_perm(1, True)(block)
    three = plane_perm(-1, True)(block)
    two = plane_perm(2, True)(block)
    plan = [(i, g * BLK, BLK) for g in range(groups) for i in range(4)]
    return stack([block, one, two, three], plan, after)


def plane_gather_second(line):
    half = line.shape[0] // 2
    one = plane_perm(1, False)(line)
    three = plane_perm(-1, False)(line)
    two_a = plane_perm(1, False)(one[:half])
    two_b = plane_perm(-1, False)(three[half:])
    return [line, one, three, two_a, two_b]


def order_kernel(outgoing_ref, records_ref, *rest):
    out_ref, sems = rest[-2:]
    copies = [
        pltpu.make_async_copy(records_ref.at[outgoing_ref[j]], out_ref.at[j], sems.at[j])
        for j in range(32)
    ]
    for copy in copies:
        copy.start()
    for copy in copies:
        copy.wait()


def order_records(outgoing, records, after):
    return pl.pallas_call(
        order_kernel,
        out_shape=jax.ShapeDtypeStruct(records.shape, records.dtype),
        in_specs=[pl.BlockSpec(memory_space=pltpu.SMEM)]
        + [pl.BlockSpec(memory_space=pl.ANY)] * (1 + len(after)),
        out_specs=pl.BlockSpec(memory_space=pltpu.VMEM),
        scratch_shapes=[pltpu.SemaphoreType.DMA((32,))],
        cost_estimate=pl.CostEstimate(flops=0, bytes_accessed=4 << 20, transcendentals=0),
        name="order_records",
    )(outgoing, records, *after)


def normalize_kernel(offs_ref, xa_ref, xb_ref, gain_ref, normed_ref):
    for part, x_ref in enumerate((xa_ref, xb_ref)):

        @pl.loop(0, RECLEN // 32)
        def _(i, part=part, x_ref=x_ref):
            rows = pl.ds(pl.multiple_of(i * 32, 32), 32)
            into = pl.ds(pl.multiple_of(part * RECLEN + i * 32, 32), 32)
            x = x_ref[rows, :].astype(jnp.float32)
            scale = lax.rsqrt(jnp.mean(x * x, axis=1, keepdims=True) + 1e-05)
            for n in range(32):
                cols = pl.ds(pl.multiple_of(offs_ref[n], BLK), BLK)
                normed_ref[into, n * BLK : (n + 1) * BLK] = (
                    x_ref[rows, cols].astype(jnp.float32) * scale * gain_ref[:, cols]
                ).astype(jnp.bfloat16)


def normalize(offs, xa, xb, gain):
    vmem = pl.BlockSpec(memory_space=pltpu.VMEM)
    return pl.pallas_call(
        normalize_kernel,
        out_shape=jax.ShapeDtypeStruct((2 * RECLEN, WIDTH), jnp.bfloat16),
        in_specs=[pl.BlockSpec(memory_space=pltpu.SMEM)] + [vmem] * 3,
        out_specs=vmem,
        compiler_params=pltpu.CompilerParams(vmem_limit_bytes=SMALL_VMEM),
        cost_estimate=pl.CostEstimate(
            flops=2 * 512 * WIDTH, bytes_accessed=12 << 20, transcendentals=0
        ),
        name="normalize",
    )(offs, xa, xb, gain)


def attend_kernel(normed_ref, cos_ref, sin_ref, segq_ref, segk_ref, *rest):
    pieces = rest[:10]
    out_ref, proj_ref = rest[-2:]

    @pl.loop(0, QKV // 256)
    def _(n):
        cols = pl.ds(pl.multiple_of(n * 256, 256), 256)
        total, start = 0.0, 0
        for piece in pieces:
            stop = start + piece.shape[0]
            total += jnp.dot(
                normed_ref[:, start:stop], piece[:, cols], preferred_element_type=jnp.float32
            )
            start = stop
        proj_ref[:, cols] = total

    cosine = cos_ref[...]
    sine = sin_ref[...]
    place_k = lax.broadcasted_iota(jnp.int32, (RECLEN, RECLEN), 0)
    place_q = lax.broadcasted_iota(jnp.int32, (RECLEN, RECLEN), 1)
    scaling = math.log2(math.e) / math.sqrt(HS)
    ones = jnp.ones((16, RECLEN), jnp.bfloat16)
    for part in range(2):
        rows = slice(part * RECLEN, (part + 1) * RECLEN)
        allowed = (segq_ref[part] == segk_ref[part]) & (place_k <= place_q)
        key = proj_ref[rows, GROUP * HS : (GROUP + 1) * HS]
        key = key * cosine + pltpu.roll(key, HS // 2, 1) * sine
        key = jnp.concatenate([key, pltpu.roll(key, HS // 2, 1)], axis=1).astype(jnp.bfloat16)
        value = proj_ref[rows, (GROUP + 1) * HS : (GROUP + 2) * HS].T.astype(jnp.bfloat16)
        value = jnp.concatenate([value, ones], axis=0)
        for g in range(GROUP):
            cols = slice(g * HS, (g + 1) * HS)
            query = proj_ref[rows, cols]
            query = jnp.concatenate([query * cosine, -(query * sine)], axis=1).astype(jnp.bfloat16)
            for low in range(0, RECLEN, QBLK):
                high = low + QBLK
                logits = lax.dot_general(
                    key[:high],
                    query[low:high],
                    (((1,), (1,)), ((), ())),
                    preferred_element_type=jnp.float32,
                )
                held = jnp.where(allowed[:high, low:high], logits, -1e30)
                top = jnp.max(held, axis=0, keepdims=True)
                weights = jnp.exp2((held - top) * scaling).astype(jnp.bfloat16)
                mixed = jnp.dot(value[:, :high], weights, preferred_element_type=jnp.float32)
                mixed = mixed[:HS] / mixed[HS : HS + 1]
                out_ref[rows.start + low : rows.start + high, cols] = mixed.T.astype(jnp.bfloat16)


def attend(normed, cosine, sine, segq, segk, pieces, after=()):
    vmem = pl.BlockSpec(memory_space=pltpu.VMEM)
    return pl.pallas_call(
        attend_kernel,
        out_shape=jax.ShapeDtypeStruct((2 * RECLEN, HEADS), jnp.bfloat16),
        in_specs=[vmem] * 15 + [pl.BlockSpec(memory_space=pl.ANY)] * len(after),
        out_specs=vmem,
        scratch_shapes=[pltpu.VMEM((2 * RECLEN, QKV), jnp.float32)],
        compiler_params=pltpu.CompilerParams(vmem_limit_bytes=ATTEND_VMEM),
        cost_estimate=pl.CostEstimate(
            flops=2 * 512 * WIDTH * QKV, bytes_accessed=16 << 20, transcendentals=1 << 20
        ),
        name="attend",
    )(normed, cosine, sine, segq, segk, *pieces, *after)


def arrange_kernel(head, offs_ref, line_ref, one_ref, three_ref, two_ref, out_ref, raw_ref, sems):
    copies = []
    for b, piece in enumerate((line_ref, one_ref, two_ref, three_ref)):
        for a in range(4):
            n = a * 4 + b
            row = a * BLK if b == 2 else (head * 4 + a) * BLK
            to = pl.multiple_of(offs_ref[n], BLK)
            copies.append(
                pltpu.make_async_copy(
                    piece.at[pl.ds(row, BLK)], raw_ref.at[pl.ds(to, BLK)], sems.at[n]
                )
            )
    for copy in copies:
        copy.start()
    for copy in copies:
        copy.wait()

    @pl.loop(0, 2 * COLS // 256)
    def _(n):
        rows = pl.ds(pl.multiple_of(n * 256, 256), 256)
        out_ref[:, rows] = raw_ref[rows, :].T


def arrange(offs, pieces, head):
    line, one, three, two_a, two_b = pieces
    return pl.pallas_call(
        lambda *refs: arrange_kernel(head, *refs),
        out_shape=jax.ShapeDtypeStruct((HEADS, 2 * COLS), jnp.bfloat16),
        in_specs=[pl.BlockSpec(memory_space=pltpu.SMEM)]
        + [pl.BlockSpec(memory_space=pl.ANY)] * 4,
        out_specs=pl.BlockSpec(memory_space=pltpu.VMEM),
        scratch_shapes=[
            pltpu.VMEM((2 * COLS, HEADS), jnp.bfloat16),
            pltpu.SemaphoreType.DMA((16,)),
        ],
        compiler_params=pltpu.CompilerParams(vmem_limit_bytes=SMALL_VMEM),
        cost_estimate=pl.CostEstimate(flops=0, bytes_accessed=8 << 20, transcendentals=0),
        name=f"arrange_{head}",
    )(offs, line, one, three, two_b if head else two_a)


def project_kernel(first, mixed_ref, w_ref, *rest):
    out_refs = rest[-3:-1]
    for part, out_ref in enumerate(out_refs):

        @pl.loop(0, COLS // 256)
        def _(n, part=part, out_ref=out_ref):
            from_cols = pl.ds(pl.multiple_of(part * COLS + n * 256, 256), 256)
            cols = pl.ds(pl.multiple_of(n * 256, 256), 256)
            out_ref[:, cols] = jnp.dot(
                mixed_ref[...], w_ref[:, from_cols], preferred_element_type=jnp.float32
            ).astype(jnp.bfloat16)

    meta_ref, weight_ref, score_ref = rest[0], rest[1], rest[-1]
    token = jnp.zeros((2 * RECLEN, 1), jnp.float32)
    for part, out_ref in enumerate(out_refs):
        terms = out_ref[...].astype(jnp.float32) * weight_ref[part : part + 1, :]
        token += jnp.sum(terms, axis=1, keepdims=True)
    score_ref[...] = row_scores(token, meta_ref, first, 2)


def project(mixed, w, meta, weight, first):
    vmem = pl.BlockSpec(memory_space=pltpu.VMEM)
    tokens = mixed.shape[0]
    return pl.pallas_call(
        lambda *refs: project_kernel(first, *refs),
        out_shape=[jax.ShapeDtypeStruct((tokens, COLS), jnp.bfloat16)] * 2
        + [jax.ShapeDtypeStruct((1, 128), jnp.float32)],
        in_specs=[vmem] * 2 + [pl.BlockSpec(memory_space=pltpu.SMEM), vmem],
        out_specs=[vmem] * 3,
        compiler_params=pltpu.CompilerParams(vmem_limit_bytes=PROJECT_VMEM),
        cost_estimate=pl.CostEstimate(
            flops=2 * tokens * HEADS * 2 * COLS, bytes_accessed=2 << 20, transcendentals=0
        ),
        name="project",
    )(mixed, w, meta, weight)


def row_scores(token, place_ref, first, count):
    slot = lax.broadcasted_iota(jnp.int32, (RECLEN, 1), 0)
    lane = lax.broadcasted_iota(jnp.int32, (1, 128), 1)
    scores = jnp.zeros((1, 128), jnp.float32)
    for i in range(count):
        row, length = place_ref[first + i], place_ref[8 + first + i]
        used = jnp.where(slot < length, token[i * RECLEN : (i + 1) * RECLEN], 0.0)
        scores += jnp.where(lane == row, jnp.sum(used, axis=0, keepdims=True), 0.0)
    return scores


def packed_rows(meta_ref, i, total):
    start, length = meta_ref[4 + i], meta_ref[8 + i]
    token = lax.broadcasted_iota(jnp.int32, (TOK, RECLEN), 0)
    slot = lax.broadcasted_iota(jnp.int32, (TOK, RECLEN), 1)
    pick = ((token - slot == start) & (slot < length)).astype(jnp.bfloat16)
    return jnp.dot(pick, total.astype(jnp.bfloat16), preferred_element_type=jnp.float32)


def finish_kernel(meta_ref, *refs):
    x_refs, kept_refs, in_refs = refs[:4], refs[4:8], refs[8:12]
    hidden_ref, acc_ref = refs[12:]
    for i in range(4):
        mine = slice(i % 2 * RECLEN, (i % 2 + 1) * RECLEN)
        theirs = slice((1 - i % 2) * RECLEN, (2 - i % 2) * RECLEN)
        total = x_refs[i][...].astype(jnp.float32)
        for head in range(2):
            n = i // 2 * 2 + head
            total += kept_refs[n][mine, :].astype(jnp.float32)
            total += in_refs[n][theirs, :].astype(jnp.float32)
        moved = packed_rows(meta_ref, i, total)
        if i == 0:
            acc_ref[...] = moved
        elif i < 3:
            acc_ref[...] += moved
        else:
            hidden_ref[...] = (acc_ref[...] + moved).astype(jnp.bfloat16)


def finish(meta, records, kept, swapped):
    def whole(shape):
        return pl.BlockSpec(shape, lambda i, m: (0,) * len(shape))

    slices = pl.BlockSpec((RECLEN, COLS), lambda i, m: (0, m[12]))
    return pl.pallas_call(
        finish_kernel,
        out_shape=jax.ShapeDtypeStruct((TOK, COLS), jnp.bfloat16),
        grid_spec=pltpu.PrefetchScalarGridSpec(
            num_scalar_prefetch=1,
            grid=(1,),
            in_specs=[slices] * 4 + [whole(v.shape) for v in (*kept, *swapped)],
            out_specs=whole((TOK, COLS)),
            scratch_shapes=[pltpu.VMEM((TOK, COLS), jnp.float32)],
        ),
        compiler_params=pltpu.CompilerParams(vmem_limit_bytes=FINISH_VMEM),
        cost_estimate=pl.CostEstimate(
            flops=2 * TOK * 4 * RECLEN * COLS, bytes_accessed=16 << 20, transcendentals=0
        ),
        name="finish",
    )(meta, *records, *kept, *swapped)


def record_score_kernel(meta_ref, record_ref, weight_ref, score_ref):
    token = jnp.sum(
        record_ref[...].astype(jnp.float32) * weight_ref[...], axis=1, keepdims=True
    )
    score_ref[...] = row_scores(token, meta_ref, 0, 1)


def record_score(meta, record, weight):
    vmem = pl.BlockSpec(memory_space=pltpu.VMEM)
    return pl.pallas_call(
        record_score_kernel,
        out_shape=jax.ShapeDtypeStruct((1, 128), jnp.float32),
        in_specs=[pl.BlockSpec(memory_space=pltpu.SMEM), vmem, vmem],
        out_specs=vmem,
        compiler_params=pltpu.CompilerParams(vmem_limit_bytes=SMALL_VMEM),
        cost_estimate=pl.CostEstimate(flops=2 << 20, bytes_accessed=2 << 20, transcendentals=0),
        name="record_score",
    )(meta, record, weight)


def on_device(records, lengths, assignment, segment_ids, norm_gain, w_qkv, w_out, score_weights):
    xh, co, xl, z, y = (lax.axis_index(a) for a in ("xh", "co", "xl", "z", "y"))
    row_index = xh * 2 + co
    reader_index = xl * 16 + z * 4 + y
    swap_xl, swap_xh, swap_co = ring("xl", 2, 1), ring("xh", 2, 1), ring("co", 2, 1)
    rec_ids = jnp.arange(32, dtype=jnp.int32)

    o_own = w_out.reshape(BLK, HEADS)
    here = xl == xh
    o_peer = swap_xl(o_own)
    o_across = lax.ppermute(o_own, ("xh", "xl"), [(0, 2), (2, 0), (1, 3), (3, 1)])
    o_corner = lax.ppermute(o_own, ("xh", "xl"), [(0, 3), (3, 0), (1, 2), (2, 1)])
    o_both = jnp.concatenate(
        [jnp.where(here, o_own, o_peer), jnp.where(here, o_across, o_corner)], axis=0
    )

    w_own = w_qkv.reshape(BLK, QKV)
    w_peer = swap_xl(w_own)
    own_line = plane_gather_first(w_own, 1)

    own_assign = lax.dynamic_index_in_dim(assignment, row_index, 0, keepdims=False)
    outgoing = jnp.sum(
        jnp.where(own_assign[None, :] == rec_ids[:, None], rec_ids[None, :], 0), axis=1
    )
    send_block = order_records(outgoing, records.reshape(32, 8, WIDTH), [o_both, own_line, w_peer])
    arrived = lax.all_to_all(
        send_block, ("xl", "z", "y"), split_axis=0, concat_axis=0, tiled=True
    )
    own_record = arrived.reshape(RECLEN, WIDTH)
    peer_record = swap_co(own_record)

    own_pieces = plane_gather_second(stack([own_line], [(0, 0, 4 * BLK)], own_record))
    peer_pieces = plane_gather_second(
        plane_gather_first(stack([w_peer], [(0, 0, BLK)], own_record), 1)
    )
    qkv_pieces = own_pieces + peer_pieces
    o_both = stack([o_both], [(0, 0, 2 * BLK)], peer_pieces[3:] + own_pieces[3:])
    out_pieces = plane_gather_second(plane_gather_first(o_both, 2))

    far_record = stack([swap_xh(own_record)], [(0, 0, RECLEN)], peer_pieces[1:3])
    far_peer_record = swap_co(far_record)
    slots = [own_record, peer_record, far_record, far_peer_record]

    chosen = assignment == reader_index
    row_order = jnp.stack(
        [row_index, row_index + 1 - 2 * co, row_index + 2 - 4 * xh, 3 - row_index]
    )
    pick_row = row_order[:, None] == jnp.arange(4, dtype=jnp.int32)[None, :]
    lens = jnp.sum(jnp.where(chosen, lengths, 0), axis=1)
    segs = jnp.sum(jnp.where(chosen[:, :, None], segment_ids, 0), axis=1)
    local_lens = jnp.sum(jnp.where(pick_row, lens[None, :], 0), axis=1)
    before = jnp.arange(4, dtype=jnp.int32)[None, :] < row_order[:, None]
    local_starts = jnp.sum(jnp.where(before, lens[None, :], 0), axis=1)
    local_segs = jnp.sum(jnp.where(pick_row[:, :, None], segs[None], 0), axis=1)
    segq = local_segs[:, :, None]
    segk = local_segs[:, None, :]
    meta = jnp.concatenate([row_order, local_starts, local_lens, row_index[None]])

    inv_freq = ROPE_BASE ** (-(jnp.arange(HS // 2, dtype=jnp.float32) * 2.0 / HS))
    angle = jnp.arange(RECLEN, dtype=jnp.float32)[:, None] * inv_freq[None, :]
    cosine = jnp.cos(angle)
    sine = jnp.sin(angle)
    cosine = jnp.concatenate([cosine, cosine], axis=1)
    sine = jnp.concatenate([-sine, sine], axis=1)


    steps_a = jnp.arange(4, dtype=jnp.int32)[:, None]
    steps_b = jnp.arange(4, dtype=jnp.int32)[None, :]
    src_z = jnp.where(co == 0, z - steps_b, z - steps_a) & 3
    src_y = jnp.where(co == 0, y - steps_a, y - steps_b) & 3
    plane = BLK * (src_z * 4 + src_y)
    plane = jnp.stack([plane[:, b] for b in (0, 1, 3, 2)]).reshape(16)
    qkv_offs = jnp.concatenate([xl * 2048 + plane, (1 - xl) * 2048 + plane])
    kept = ((src_z // 2) == co).astype(jnp.int32)
    out_offs = (kept * COLS + (src_z & 1) * (4 * BLK) + src_y * BLK).reshape(16)

    gain = norm_gain[None, :]
    normed_a = normalize(qkv_offs, slots[0], slots[1], gain)
    normed_b = normalize(qkv_offs, slots[2], slots[3], gain)
    mixed_a = attend(normed_a, cosine, sine, segq[:2], segk[:2], qkv_pieces, [normed_b])
    mixed_b = attend(normed_b, cosine, sine, segq[2:], segk[2:], qkv_pieces)
    far_b = swap_xh(mixed_a)
    far_a = swap_xh(mixed_b)
    weights = score_weights.reshape(4, COLS)
    weight = jnp.stack(
        [
            lax.dynamic_index_in_dim(weights, row_index + 1 - 2 * co, 0, keepdims=False),
            lax.dynamic_index_in_dim(weights, row_index, 0, keepdims=False),
        ]
    )
    w_near, w_far = arrange(out_offs, out_pieces, 0), arrange(out_offs, out_pieces, 1)

    terms = [
        project(mixed_a, w_near, meta, weight, 0),
        project(far_a, w_far, meta, weight, 0),
        project(mixed_b, w_near, meta, weight, 2),
        project(far_b, w_far, meta, weight, 2),
    ]
    hidden_out = finish(meta, slots, [t[1] for t in terms], [swap_co(t[0]) for t in terms])
    partial = record_score(meta, own_record, score_weights[None, :])
    partial += (terms[0][2] + terms[2][2]) + (terms[3][2] + terms[1][2])
    scores = lax.psum(partial[0, :4], ("xh", "co"))
    record_scores = (scores / lens.astype(jnp.float32))[None, :]
    return (hidden_out, record_scores)


def solution(mesh):
    fine = Mesh(mesh.devices.reshape(2, 2, 2, 4, 4), ("xh", "co", "xl", "z", "y"))
    row, reader = ("xh", "co"), ("xl", "z", "y")
    in_specs = (
        P(row, None, reader, None),
        P(),
        P(),
        P(),
        P(),
        P(reader, row, None),
        P(reader, row, None),
        P(),
    )
    out_specs = (P(reader, row), P(reader, None))
    return jax.shard_map(
        on_device, mesh=fine, in_specs=in_specs, out_specs=out_specs, check_vma=False
    )
```

time: 346 us -> 253 us (0.73)
  Pallas kernels: 151 us -> 78.3 us
  waiting for transfers between devices: 101 us -> 60.4 us
  blocking collectives: 6.64 us -> 39.3 us
  local copies, waits for them, and re-layouts: 25.8 us -> 17.8 us
    pallas_call x1, Pallas kernels: 65.6 us -> 3.84 us  [order_records(): pl.pallas_call(order_kernel, out_shape=jax.ShapeDtypeStruct(records.shape...]
    ppermute x11, waiting for transfers between devices: 37.2 us -> 3.77 us  [ring(): lax.ppermute(v, axis, [(i, (i + step) % size) for i in range(size)])]
    all_to_all x0 -> x1, blocking collectives: none -> 32.7 us  [on_device(): lax.all_to_all(send_block, ('xl', 'z', 'y'), split_axis=0, concat_axis=0,...]
    pallas_call x2, Pallas kernels: 48.9 us -> 18.9 us  [attend(): pl.pallas_call(attend_kernel, out_shape=jax.ShapeDtypeStruct((2 * RECLEN,...]
    pallas_call x4 -> x17, Pallas kernels: 36.3 us -> 55.6 us  [the longest x4 22 us: project(): pl.pallas_call(lambda *refs: project_kernel(first, *refs), out_shape=[jax...]
    ppermute x21, waiting for transfers between devices: 63.3 us -> 51.5 us  [plane_perm(): return lambda v: lax.ppermute(v, CORE_ZY, pairs)]
    all_to_all x1 -> x0, starting transfers between devices: 10.1 us -> none  [on_device(): lax.all_to_all(send_block, ('xl', 'z', 'y'), split_axis=0, concat_axis=0,...]
    ppermute x21, starting transfers between devices: 25.7 us -> 31.3 us  [plane_perm(): return lambda v: lax.ppermute(v, CORE_ZY, pairs)]
  transfers between devices with their start and end apart: 33 -> 34, of which waited for: 16 -> 12; matrix products, arithmetic and copies ran while one was open for 7% -> 4% of each run, Pallas kernels for 22% -> 27%
where the time goes in v2:
time: 253 us; the launch traced here: 252 us
  Pallas kernels  78.3 us (31%)
  waiting for transfers between devices  60.4 us (24%)
  starting transfers between devices  49.5 us (20%)
  blocking collectives  39.3 us (16%)
  local copies, waits for them, and re-layouts  17.8 us (7%)
  other arithmetic  5.4 us (2%)
    ppermute x21, waiting for transfers between devices, plane_perm(): return lambda v: lax.ppermute(v, CORE_ZY, pairs)  51.5 us
    all_to_all x1, blocking collectives, on_device(): lax.all_to_all(send_block, ('xl', 'z', 'y'), split_axis=0, concat_axis=0,...  32.7 us
    ppermute x21, starting transfers between devices, plane_perm(): return lambda v: lax.ppermute(v, CORE_ZY, pairs)  31.3 us
    pallas_call x4, Pallas kernels, project(): pl.pallas_call(lambda *refs: project_kernel(first, *refs), out_shape=[jax...  22 us
    pallas_call x2, Pallas kernels, attend(): pl.pallas_call(attend_kernel, out_shape=jax.ShapeDtypeStruct((2 * RECLEN,...  18.9 us
    ppermute x11, starting transfers between devices, ring(): lax.ppermute(v, axis, [(i, (i + step) % size) for i in range(size)])  15.6 us
    unnamed x74, local copies, waits for them, and re-layouts  12 us
    pallas_call x2, Pallas kernels, normalize(): pl.pallas_call(normalize_kernel, out_shape=jax.ShapeDtypeStruct((2 * RECL...  10.1 us
  transfers between devices with their start and end apart: 34, of which 12 were waited for; matrix products, arithmetic and copies ran while one was open for 4% of the time, Pallas kernels for 27%

profile of v2, /device:TPU:1, one launch (start us, length us, event | category | flops | bytes accessed | tf_op | source)
XLA Modules:
  0.0 251.9 jit_solution(1431420949951652055)
XLA Ops:
  0.6 2.1 collective-permute-start
  2.8 2.5 collective-permute-start.1
  5.2 1.8 collective-permute-start.3
  7.0 3.3 %collective-permute-start.4 = (bf16[128,1280]{1,0:T(8,128)(2,1)}, bf16[128,1280]{1,0:T(8,128)(2,1)S(1)}, u32[]{:S(2)}, u32[]{:S(2)}) collective-permute-start(bf16[128,1280]{1,0:T(8,128)(2,1)} %bitcast.33), channel_id=1, source_target_pairs={{0,2},{1,3},{2,0},{3,1},{4,6},{5,7},{6,4},{7,5},{8,10},{9,11},{10,... | collective-permute-start | bytes 983048 | tf_op jit(solution)/shard_map/ppermute | solution.py:41
  13.7 3.1 %collective-permute-done.1 = bf16[128,1024]{1,0:T(8,128)(2,1)S(1)} collective-permute-done((bf16[128,1024]{1,0:T(8,128)(2,1)}, bf16[128,1024]{1,0:T(8,128)(2,1)S(1)}, u32[]{:S(2)}, u32[]{:S(2)}) %collective-permute-start.1) | collective-permute-done | bytes 262176 | tf_op jit(solution)/shard_map/ppermute | solution.py:376
  16.8 2.0 collective-permute-done.2
  20.9 3.7 %collective-permute-done.6.rest_2_.refs_0_ = bf16[128,1280]{1,0:T(8,128)(2,1)S(1)} collective-permute-done((bf16[128,1280]{1,0:T(8,128)(2,1)}, bf16[128,1280]{1,0:T(8,128)(2,1)S(1)}, u32[]{:S(2)}, u32[]{:S(2)}) %collective-permute-start.6) | collective-permute-done | bytes 327712 | tf_op jit(solution)/shard_map/ppermute | solution.py:30
  25.3 3.8 %order_records.1 = bf16[32,8,4096]{2,1,0:T(8,128)(2,1)} custom-call(s32[32]{0:T(128)} %select_reduce_fusion.2.outgoing_ref, bf16[32,8,4096]{2,1,0:T(8,128)(2,1)} %bitcast.40, bf16[256,1024]{1,0:T(8,128)(2,1)} %pad_maximum_fusion.rest_0_.refs_0_, bf16[512,1280]{1,0:T(8,128)(2,1)} %copy-done, bf16[128,1280]{1,0:T(8,128)(2,1)} %copy-done.22), custom_call_target="tpu_custom_call" | custom-call | bytes 4194304 | tf_op jit(solution)/shard_map/order_records/pallas_call | solution.py:97
  29.2 32.7 %all_to_all.5 = bf16[32,8,4096]{2,1,0:T(8,128)(2,1)S(1)} all-to-all(bf16[32,8,4096]{2,1,0:T(8,128)(2,1)} %order_records.1), channel_id=1, replica_groups=mesh['xh'=2,'co'=2,'xl'=2,'z'=4,'y'=4] {'xl','z','y'}, dimensions={0} | all-to-all | bytes 4194304 | tf_op jit(solution)/shard_map/all_to_all | solution.py:391
  62.0 3.7 %collective-permute-start.10 = (bf16[128,1280]{1,0:T(8,128)(2,1)S(1)}, bf16[128,1280]{1,0:T(8,128)(2,1)S(1)}, u32[]{:S(2)}, u32[]{:S(2)}) collective-permute-start(bf16[128,1280]{1,0:T(8,128)(2,1)S(1)} %stack.38.refs_0_), channel_id=1, source_target_pairs={{0,2},{1,3},{2,0},{3,1},{4,6},{5,7},{6,4},{7,5},{8,10},{9,11},{10,... | collective-permute-start | bytes 983048 | tf_op jit(solution)/shard_map/ppermute | solution.py:41
  66.1 2.7 %collective-permute-start.16 = (bf16[512,1280]{1,0:T(8,128)(2,1)S(1)}, bf16[512,1280]{1,0:T(8,128)(2,1)S(1)}, u32[]{:S(2)}, u32[]{:S(2)}) collective-permute-start(bf16[512,1280]{1,0:T(8,128)(2,1)S(1)} %stack.41.rest_0_), channel_id=1, source_target_pairs={{0,12},{1,13},{2,14},{3,15},{4,0},{5,1},{6,2},{7,3},{8,4},{9,5},{1... | collective-permute-start | bytes 3932168 | tf_op jit(solution)/shard_map/ppermute | solution.py:41
  69.2 4.5 %collective-permute-done.10.refs_2_ = bf16[128,1280]{1,0:T(8,128)(2,1)S(1)} collective-permute-done((bf16[128,1280]{1,0:T(8,128)(2,1)S(1)}, bf16[128,1280]{1,0:T(8,128)(2,1)S(1)}, u32[]{:S(2)}, u32[]{:S(2)}) %collective-permute-start.10) | collective-permute-done | bytes 327712 | tf_op jit(solution)/shard_map/ppermute | solution.py:41
  74.9 2.5 collective-permute-start.13
  78.5 12.6 %collective-permute-done.15.rest_1_ = bf16[512,1280]{1,0:T(8,128)(2,1)S(1)} collective-permute-done((bf16[512,1280]{1,0:T(8,128)(2,1)S(1)}, bf16[512,1280]{1,0:T(8,128)(2,1)S(1)}, u32[]{:S(2)}, u32[]{:S(2)}) %collective-permute-start.15) | collective-permute-done | bytes 1310752 | tf_op jit(solution)/shard_map/ppermute | solution.py:41
  92.3 2.7 %collective-permute-start.18 = (bf16[256,1280]{1,0:T(8,128)(2,1)S(1)}, bf16[256,1280]{1,0:T(8,128)(2,1)S(1)}, u32[]{:S(2)}, u32[]{:S(2)}) collective-permute-start(bf16[256,1280]{1,0:T(8,128)(2,1)S(1)} %slice.72), channel_id=1, source_target_pairs={{0,12},{1,13},{2,14},{3,15},{4,0},{5,1},{6,2},{7,3},{8,4},{9,5},{1... | collective-permute-start | bytes 1966088 | tf_op jit(solution)/shard_map/ppermute | solution.py:41
  95.0 10.2 %collective-permute-done.12.refs_1_.rest_6_ = bf16[512,1280]{1,0:T(8,128)(2,1)S(1)} collective-permute-done((bf16[512,1280]{1,0:T(8,128)(2,1)S(1)}, bf16[512,1280]{1,0:T(8,128)(2,1)S(1)}, u32[]{:S(2)}, u32[]{:S(2)}) %collective-permute-start.12) | collective-permute-done | bytes 1310752 | tf_op jit(solution)/shard_map/ppermute | solution.py:41
  106.5 2.7 %collective-permute-start.20 = (bf16[256,1280]{1,0:T(8,128)(2,1)S(1)}, bf16[256,1280]{1,0:T(8,128)(2,1)S(1)}, u32[]{:S(2)}, u32[]{:S(2)}) collective-permute-start(bf16[256,1280]{1,0:T(8,128)(2,1)S(1)} %slice.74), channel_id=1, source_target_pairs={{0,12},{1,13},{2,14},{3,15},{4,0},{5,1},{6,2},{7,3},{8,4},{9,5},{1... | collective-permute-start | bytes 1966088 | tf_op jit(solution)/shard_map/ppermute | solution.py:41
  109.2 3.1 %collective-permute-done.17.rest_3_.refs_3_ = bf16[256,1280]{1,0:T(8,128)(2,1)S(1)} collective-permute-done((bf16[256,1280]{1,0:T(8,128)(2,1)S(1)}, bf16[256,1280]{1,0:T(8,128)(2,1)S(1)}, u32[]{:S(2)}, u32[]{:S(2)}) %collective-permute-start.17) | collective-permute-done | bytes 655392 | tf_op jit(solution)/shard_map/ppermute | solution.py:41
  112.3 7.0 %collective-permute-done.19.rest_8_.refs_1_ = bf16[256,1280]{1,0:T(8,128)(2,1)S(1)} collective-permute-done((bf16[256,1280]{1,0:T(8,128)(2,1)S(1)}, bf16[256,1280]{1,0:T(8,128)(2,1)S(1)}, u32[]{:S(2)}, u32[]{:S(2)}) %collective-permute-start.19) | collective-permute-done | bytes 655392 | tf_op jit(solution)/shard_map/ppermute | solution.py:41
  121.5 2.5 collective-permute-start.23
  124.9 1.3 copy-done.3
  126.2 3.1 %stack.40.xa_ref.refs_2_ = bf16[256,4096]{1,0:T(8,128)(2,1)} custom-call(bf16[256,4096]{1,0:T(8,128)(2,1)} %collective-permute-done.8.refs_0_, bf16[512,1280]{1,0:T(8,128)(2,1)S(1)} %collective-permute-done.12.refs_1_.rest_6_, bf16[512,1280]{1,0:T(8,128)(2,1)S(1)} %copy-done.3), custom_call_target="tpu_custom_call" | custom-call | bytes 1048576 | tf_op jit(solution)/shard_map/stack/pallas_call | solution.py:55
  129.3 2.2 collective-permute-start.14
  131.5 4.2 %collective-permute-done.21.refs_1_ = bf16[256,1024]{1,0:T(8,128)(2,1)} collective-permute-done((bf16[256,1024]{1,0:T(8,128)(2,1)}, bf16[256,1024]{1,0:T(8,128)(2,1)}, u32[]{:S(2)}, u32[]{:S(2)}) %collective-permute-start.21) | collective-permute-done | bytes 524320 | tf_op jit(solution)/shard_map/ppermute | solution.py:41
  136.4 3.0 %stack.43.refs_1_ = bf16[1024,1024]{1,0:T(8,128)(2,1)} custom-call(bf16[256,1024]{1,0:T(8,128)(2,1)} %stack.42.refs_0_, bf16[256,1024]{1,0:T(8,128)(2,1)} %collective-permute-done.21.refs_1_, bf16[256,1024]{1,0:T(8,128)(2,1)} %collective-permute-done.22.refs_2_, bf16[256,1024]{1,0:T(8,128)(2,1)} %collective-permute-done.23.refs_3_), custom_call_target="tpu_custom_call" | custom-call | bytes 1048576 | tf_op jit(solution)/shard_map/stack/pallas_call | solution.py:55
  140.2 2.6 %collective-permute-start.25 = (bf16[1024,1024]{1,0:T(8,128)(2,1)}, bf16[1024,1024]{1,0:T(8,128)(2,1)}, u32[]{:S(2)}, u32[]{:S(2)}) collective-permute-start(bf16[1024,1024]{1,0:T(8,128)(2,1)} %stack.43.refs_1_), channel_id=1, source_target_pairs={{0,12},{1,13},{2,14},{3,15},{4,0},{5,1},{6,2},{7,3},{8,4},{9,5},{1... | collective-permute-start | bytes 6291464 | tf_op jit(solution)/shard_map/ppermute | solution.py:41
  147.1 4.6 %normalize.2.normed_ref = bf16[512,4096]{1,0:T(8,128)(2,1)S(1)} custom-call(s32[32]{0:T(128)S(1)} %pad_add_fusion.2.offs_ref, bf16[256,4096]{1,0:T(8,128)(2,1)S(1)} %bitcast.29, bf16[256,4096]{1,0:T(8,128)(2,1)} %collective-permute-done.7.xb_ref.refs_1_, f32[1,4096]{1,0:T(1,128)S(1)} %bitcast.37), custom_call_target="tpu_custom_call" | custom-call | flops 4194304 | bytes 12582912 | tf_op jit(solution)/shard_map/normalize/pallas_call | solution.py:127
  151.9 5.4 %normalize.3.rest_10_.normed_ref = bf16[512,4096]{1,0:T(8,128)(2,1)S(1)} custom-call(s32[32]{0:T(128)S(1)} %pad_add_fusion.2.offs_ref, bf16[256,4096]{1,0:T(8,128)(2,1)} %stack.40.xa_ref.refs_2_, bf16[256,4096]{1,0:T(8,128)(2,1)} %collective-permute-done.14.xb_ref.refs_3_, f32[1,4096]{1,0:T(1,128)S(1)} %bitcast.38), custom_call_target="tpu_custom_call" | custom-call | flops 4194304 | bytes 12582912 | tf_op jit(solution)/shard_map/normalize/pallas_call | solution.py:127
  157.3 8.8 %collective-permute-done.24.refs_2_ = bf16[1024,1024]{1,0:T(8,128)(2,1)} collective-permute-done((bf16[1024,1024]{1,0:T(8,128)(2,1)}, bf16[1024,1024]{1,0:T(8,128)(2,1)}, u32[]{:S(2)}, u32[]{:S(2)}) %collective-permute-start.24) | collective-permute-done | bytes 2097184 | tf_op jit(solution)/shard_map/ppermute | solution.py:41
  166.1 1.3 slice.75
  167.6 9.5 %attend.3.refs_0_ = bf16[512,1024]{1,0:T(8,128)(2,1)S(1)} custom-call(bf16[512,4096]{1,0:T(8,128)(2,1)S(1)} %normalize.3.rest_10_.normed_ref, f32[256,128]{1,0:T(8,128)S(1)} %get-tuple-element.50.cos_ref, f32[256,128]{1,0:T(8,128)S(1)} %get-tuple-element.51.sin_ref, s32[2,256,1]{2,1,0:T(8,128)S(1)} %copy-done.32, s32[2,1,256]{2,1,0:T(1,128)S(1)} %slice.67.segk_ref, ...), custom_call_target="tpu_custom_call" | custom-call | flops 5368709120 | bytes 16777216 | tf_op jit(solution)/shard_map/attend/pallas_call | solution.py:192
  178.1 1.3 slice.77
  179.4 2.7 %collective-permute-start.28 = (bf16[512,1024]{1,0:T(8,128)(2,1)S(1)}, bf16[512,1024]{1,0:T(8,128)(2,1)S(1)}, u32[]{:S(2)}, u32[]{:S(2)}) collective-permute-start(bf16[512,1024]{1,0:T(8,128)(2,1)S(1)} %slice.77), channel_id=1, source_target_pairs={{0,12},{1,13},{2,14},{3,15},{4,0},{5,1},{6,2},{7,3},{8,4},{9,5},{1... | collective-permute-start | bytes 3145736 | tf_op jit(solution)/shard_map/ppermute | solution.py:41
  182.1 9.4 %attend.2.refs_0_ = bf16[512,1024]{1,0:T(8,128)(2,1)S(1)} custom-call(bf16[512,4096]{1,0:T(8,128)(2,1)S(1)} %normalize.2.normed_ref, f32[256,128]{1,0:T(8,128)S(1)} %get-tuple-element.50.cos_ref, f32[256,128]{1,0:T(8,128)S(1)} %get-tuple-element.51.sin_ref, s32[2,256,1]{2,1,0:T(8,128)S(1)} %copy-done.24, s32[2,1,256]{2,1,0:T(1,128)S(1)} %slice.59.segk_ref, ...), custom_call_target="tpu_custom_call" | custom-call | flops 5368709120 | bytes 16777216 | tf_op jit(solution)/shard_map/attend/pallas_call | solution.py:192
  191.6 2.3 collective-permute-start.29
  193.9 4.1 %arrange_0.1.refs_1_ = bf16[1024,2048]{1,0:T(8,128)(2,1)S(1)} custom-call(s32[16]{0:T(128)S(1)} %fusion.6.refs_0_, bf16[1024,1024]{1,0:T(8,128)(2,1)} %stack.43.refs_1_, bf16[1024,1024]{1,0:T(8,128)(2,1)} %collective-permute-done.24.refs_2_, bf16[1024,1024]{1,0:T(8,128)(2,1)} %collective-permute-done.25.refs_3_, ...), custom_call_target="tpu_custom_call" | custom-call | bytes 8388608 | tf_op jit(solution)/shard_map/arrange_0/pallas_call | solution.py:231
  198.1 5.5 %project.4 = (bf16[512,1024]{1,0:T(8,128)(2,1)}, bf16[512,1024]{1,0:T(8,128)(2,1)S(1)}, f32[1,128]{1,0:T(1,128)S(1)}) custom-call(bf16[512,1024]{1,0:T(8,128)(2,1)S(1)} %attend.2.refs_0_, bf16[1024,2048]{1,0:T(8,128)(2,1)S(1)} %arrange_0.1.refs_1_, s32[13]{0:T(128)S(1)} %concatenate.16.refs_2_.meta_ref, f32[2,1024]{1,0:T(2,128)S(1)} %pad_maximum_fusion.3.refs_3_), custom_call_target="tpu_custom_call" | custom-call | flops 2147483648 | bytes 2097152 | tf_op jit(solution)/shard_map/project/pallas_call | solution.py:270
  203.6 3.1 %collective-permute-start.30 = (bf16[512,1024]{1,0:T(8,128)(2,1)}, bf16[512,1024]{1,0:T(8,128)(2,1)}, u32[]{:S(2)}, u32[]{:S(2)}) collective-permute-start(bf16[512,1024]{1,0:T(8,128)(2,1)} %get-tuple-element.18), channel_id=1, source_target_pairs={{0,32},{32,0},{1,33},{33,1},{2,34},{34,2},{3,35},{35,3},{4,36},{36... | collective-permute-start | bytes 3145736 | tf_op jit(solution)/shard_map/ppermute | solution.py:30
  206.7 4.1 %arrange_1.1.refs_1_ = bf16[1024,2048]{1,0:T(8,128)(2,1)S(1)} custom-call(s32[16]{0:T(128)S(1)} %fusion.6.refs_0_, bf16[1024,1024]{1,0:T(8,128)(2,1)} %stack.43.refs_1_, bf16[1024,1024]{1,0:T(8,128)(2,1)} %collective-permute-done.24.refs_2_, bf16[1024,1024]{1,0:T(8,128)(2,1)} %collective-permute-done.25.refs_3_, ...), custom_call_target="tpu_custom_call" | custom-call | bytes 8388608 | tf_op jit(solution)/shard_map/arrange_1/pallas_call | solution.py:231
  210.9 5.5 %project.5 = (bf16[512,1024]{1,0:T(8,128)(2,1)}, bf16[512,1024]{1,0:T(8,128)(2,1)S(1)}, f32[1,128]{1,0:T(1,128)S(1)}) custom-call(bf16[512,1024]{1,0:T(8,128)(2,1)S(1)} %collective-permute-done.27.refs_0_, bf16[1024,2048]{1,0:T(8,128)(2,1)S(1)} %arrange_1.1.refs_1_, s32[13]{0:T(128)S(1)} %concatenate.16.refs_2_.meta_ref, f32[2,1024]{1,0:T(2,128)S(1)} %pad_maximum_fusion.3.refs_3_), custom_call_target="tpu_custom_call" | custom-call | flops 2147483648 | bytes 2097152 | tf_op jit(solution)/shard_map/project/pallas_call | solution.py:270
  217.4 5.5 %project.6 = (bf16[512,1024]{1,0:T(8,128)(2,1)}, bf16[512,1024]{1,0:T(8,128)(2,1)S(1)}, f32[1,128]{1,0:T(1,128)S(1)}) custom-call(bf16[512,1024]{1,0:T(8,128)(2,1)S(1)} %attend.3.refs_0_, bf16[1024,2048]{1,0:T(8,128)(2,1)S(1)} %arrange_0.1.refs_1_, s32[13]{0:T(128)S(1)} %concatenate.16.refs_2_.meta_ref, f32[2,1024]{1,0:T(2,128)S(1)} %pad_maximum_fusion.3.refs_3_), custom_call_target="tpu_custom_call" | custom-call | flops 2147483648 | bytes 2097152 | tf_op jit(solution)/shard_map/project/pallas_call | solution.py:270
  224.4 5.5 %project.7 = (bf16[512,1024]{1,0:T(8,128)(2,1)}, bf16[512,1024]{1,0:T(8,128)(2,1)S(1)}, f32[1,128]{1,0:T(1,128)S(1)}) custom-call(bf16[512,1024]{1,0:T(8,128)(2,1)S(1)} %collective-permute-done.29.refs_0_, bf16[1024,2048]{1,0:T(8,128)(2,1)S(1)} %arrange_1.1.refs_1_, s32[13]{0:T(128)S(1)} %concatenate.16.refs_2_.meta_ref, f32[2,1024]{1,0:T(2,128)S(1)} %pad_maximum_fusion.3.refs_3_), custom_call_target="tpu_custom_call" | custom-call | flops 2147483648 | bytes 2097152 | tf_op jit(solution)/shard_map/project/pallas_call | solution.py:270
  230.9 2.3 collective-permute-start.33
  234.3 6.6 %psum.7 = f32[4]{0:T(128)S(1)} all-reduce(f32[4]{0:T(128)S(1)} %slice_bitcast_fusion), channel_id=1, replica_groups=mesh['xh'=2,'co'=2,'xl'=2,'z'=4,'y'=4] {'xh','co'}, use_global_device_ids=true, to_apply=%region_6.7 | all-reduce | flops 4 | bytes 32 | tf_op jit(solution)/shard_map/psum | solution.py:467
  241.5 1.2 copy-done.26
  242.7 1.2 copy-done.28
  243.9 1.2 copy-done.30
  245.1 6.8 %finish.1 = bf16[896,1024]{1,0:T(8,128)(2,1)} custom-call(s32[13]{0:T(128)S(1)} %concatenate.16.refs_2_.meta_ref, bf16[256,4096]{1,0:T(8,128)(2,1)S(1)} %bitcast.31, bf16[256,4096]{1,0:T(8,128)(2,1)} %collective-permute-done.7.xb_ref.refs_1_, bf16[256,4096]{1,0:T(8,128)(2,1)} %stack.40.xa_ref.refs_2_, ...), custom_call_target="tpu_custom_call" | custom-call | flops 1879048192 | bytes 16777216 | tf_op jit(solution)/shard_map/finish/pallas_call | solution.py:328
  (158 shorter events, 26.8 us)
Async XLA Ops:
  0.6 19.1 %copy-start.31 = (bf16[128,1,1280]{2,0,1:T(8,128)(2,1)S(1)}, bf16[128,1,1280]{2,0,1:T(8,128)(2,1)}, u32[]{:S(2)}) copy-start(bf16[128,1,1280]{2,0,1:T(8,128)(2,1)} %param.13) | copy-start | bytes 983044
  0.6 11.0 %collective-permute-start = (bf16[128,1024]{1,0:T(8,128)(2,1)}, bf16[128,1024]{1,0:T(8,128)(2,1)S(1)}, u32[]{:S(2)}, u32[]{:S(2)}) collective-permute-start(bf16[128,1024]{1,0:T(8,128)(2,1)} %bitcast.41), channel_id=1, source_target_pairs={{0,16},{16,0},{1,17},{17,1},{2,18},{18,2},{3,19},{19,3},{4,20},{20... | collective-permute-start | bytes 786440 | tf_op jit(solution)/shard_map/ppermute | solution.py:30
  2.8 14.0 %collective-permute-start.1 = (bf16[128,1024]{1,0:T(8,128)(2,1)}, bf16[128,1024]{1,0:T(8,128)(2,1)S(1)}, u32[]{:S(2)}, u32[]{:S(2)}) collective-permute-start(bf16[128,1024]{1,0:T(8,128)(2,1)} %bitcast.42), channel_id=1, source_target_pairs={{0,64},{64,0},{16,80},{80,16},{1,65},{65,1},{17,81},{81,17},{2,66}... | collective-permute-start | bytes 786440 | tf_op jit(solution)/shard_map/ppermute | solution.py:376
  5.2 13.6 %collective-permute-start.2 = (bf16[128,1024]{1,0:T(8,128)(2,1)}, bf16[128,1024]{1,0:T(8,128)(2,1)S(1)}, u32[]{:S(2)}, u32[]{:S(2)}) collective-permute-start(bf16[128,1024]{1,0:T(8,128)(2,1)} %bitcast.43), channel_id=1, source_target_pairs={{0,80},{80,0},{16,64},{64,16},{1,81},{81,1},{17,65},{65,17},{2,82}... | collective-permute-start | bytes 786440 | tf_op jit(solution)/shard_map/ppermute | solution.py:377
  5.2 14.4 %collective-permute-start.3 = (bf16[128,1280]{1,0:T(8,128)(2,1)}, bf16[128,1280]{1,0:T(8,128)(2,1)S(1)}, u32[]{:S(2)}, u32[]{:S(2)}) collective-permute-start(bf16[128,1280]{1,0:T(8,128)(2,1)} %bitcast.32), channel_id=1, source_target_pairs={{0,1},{1,2},{2,3},{3,0},{4,5},{5,6},{6,7},{7,4},{8,9},{9,10},{10,1... | collective-permute-start | bytes 983048 | tf_op jit(solution)/shard_map/ppermute | solution.py:41
  7.0 12.6 %collective-permute-start.4 = (bf16[128,1280]{1,0:T(8,128)(2,1)}, bf16[128,1280]{1,0:T(8,128)(2,1)S(1)}, u32[]{:S(2)}, u32[]{:S(2)}) collective-permute-start(bf16[128,1280]{1,0:T(8,128)(2,1)} %bitcast.33), channel_id=1, source_target_pairs={{0,2},{1,3},{2,0},{3,1},{4,6},{5,7},{6,4},{7,5},{8,10},{9,11},{10,... | collective-permute-start | bytes 983048 | tf_op jit(solution)/shard_map/ppermute | solution.py:41
  11.7 8.0 %collective-permute-start.5 = (bf16[128,1280]{1,0:T(8,128)(2,1)}, bf16[128,1280]{1,0:T(8,128)(2,1)S(1)}, u32[]{:S(2)}, u32[]{:S(2)}) collective-permute-start(bf16[128,1280]{1,0:T(8,128)(2,1)} %bitcast.34), channel_id=1, source_target_pairs={{0,3},{1,0},{2,1},{3,2},{4,7},{5,4},{6,5},{7,6},{8,11},{9,8},{10,9... | collective-permute-start | bytes 983048 | tf_op jit(solution)/shard_map/ppermute | solution.py:41
  16.8 7.8 %collective-permute-start.6 = (bf16[128,1280]{1,0:T(8,128)(2,1)}, bf16[128,1280]{1,0:T(8,128)(2,1)S(1)}, u32[]{:S(2)}, u32[]{:S(2)}) collective-permute-start(bf16[128,1280]{1,0:T(8,128)(2,1)} %bitcast.35), channel_id=1, source_target_pairs={{0,16},{16,0},{1,17},{17,1},{2,18},{18,2},{3,19},{19,3},{4,20},{20... | collective-permute-start | bytes 983048 | tf_op jit(solution)/shard_map/ppermute | solution.py:30
  29.2 32.7 %copy-start.23 = (bf16[128,1280]{1,0:T(8,128)(2,1)S(1)}, bf16[128,1280]{1,0:T(8,128)(2,1)}, u32[]{:S(2)}) copy-start(bf16[128,1280]{1,0:T(8,128)(2,1)} %copy-done.22) | copy-start | bytes 983044
  61.9 7.3 %collective-permute-start.9 = (bf16[128,1280]{1,0:T(8,128)(2,1)S(1)}, bf16[128,1280]{1,0:T(8,128)(2,1)S(1)}, u32[]{:S(2)}, u32[]{:S(2)}) collective-permute-start(bf16[128,1280]{1,0:T(8,128)(2,1)S(1)} %stack.38.refs_0_), channel_id=1, source_target_pairs={{0,1},{1,2},{2,3},{3,0},{4,5},{5,6},{6,7},{7,4},{8,9},{9,10},{10,1... | collective-permute-start | bytes 983048 | tf_op jit(solution)/shard_map/ppermute | solution.py:41
  62.0 11.6 %collective-permute-start.10 = (bf16[128,1280]{1,0:T(8,128)(2,1)S(1)}, bf16[128,1280]{1,0:T(8,128)(2,1)S(1)}, u32[]{:S(2)}, u32[]{:S(2)}) collective-permute-start(bf16[128,1280]{1,0:T(8,128)(2,1)S(1)} %stack.38.refs_0_), channel_id=1, source_target_pairs={{0,2},{1,3},{2,0},{3,1},{4,6},{5,7},{6,4},{7,5},{8,10},{9,11},{10,... | collective-permute-start | bytes 983048 | tf_op jit(solution)/shard_map/ppermute | solution.py:41
  65.7 8.0 %collective-permute-start.11 = (bf16[128,1280]{1,0:T(8,128)(2,1)S(1)}, bf16[128,1280]{1,0:T(8,128)(2,1)S(1)}, u32[]{:S(2)}, u32[]{:S(2)}) collective-permute-start(bf16[128,1280]{1,0:T(8,128)(2,1)S(1)} %stack.38.refs_0_), channel_id=1, source_target_pairs={{0,3},{1,0},{2,1},{3,2},{4,7},{5,4},{6,5},{7,6},{8,11},{9,8},{10,9... | collective-permute-start | bytes 983048 | tf_op jit(solution)/shard_map/ppermute | solution.py:41
  66.0 26.2 %copy-start.5 = (bf16[512,1280]{1,0:T(8,128)(2,1)}, bf16[512,1280]{1,0:T(8,128)(2,1)S(1)}, u32[]{:S(2)}) copy-start(bf16[512,1280]{1,0:T(8,128)(2,1)S(1)} %stack.41.rest_0_) | copy-start | bytes 3932164
  66.0 25.1 %collective-permute-start.15 = (bf16[512,1280]{1,0:T(8,128)(2,1)S(1)}, bf16[512,1280]{1,0:T(8,128)(2,1)S(1)}, u32[]{:S(2)}, u32[]{:S(2)}) collective-permute-start(bf16[512,1280]{1,0:T(8,128)(2,1)S(1)} %stack.41.rest_0_), channel_id=1, source_target_pairs={{0,4},{1,5},{2,6},{3,7},{4,8},{5,9},{6,10},{7,11},{8,12},{9,13},{1... | collective-permute-start | bytes 3932168 | tf_op jit(solution)/shard_map/ppermute | solution.py:41
  66.1 26.1 %collective-permute-start.16 = (bf16[512,1280]{1,0:T(8,128)(2,1)S(1)}, bf16[512,1280]{1,0:T(8,128)(2,1)S(1)}, u32[]{:S(2)}, u32[]{:S(2)}) collective-permute-start(bf16[512,1280]{1,0:T(8,128)(2,1)S(1)} %stack.41.rest_0_), channel_id=1, source_target_pairs={{0,12},{1,13},{2,14},{3,15},{4,0},{5,1},{6,2},{7,3},{8,4},{9,5},{1... | collective-permute-start | bytes 3932168 | tf_op jit(solution)/shard_map/ppermute | solution.py:41
  73.7 31.7 %copy-start.7 = (bf16[512,1280]{1,0:T(8,128)(2,1)}, bf16[512,1280]{1,0:T(8,128)(2,1)S(1)}, u32[]{:S(2)}) copy-start(bf16[512,1280]{1,0:T(8,128)(2,1)S(1)} %stack.39.rest_5_) | copy-start | bytes 3932164
  73.8 31.5 %collective-permute-start.12 = (bf16[512,1280]{1,0:T(8,128)(2,1)S(1)}, bf16[512,1280]{1,0:T(8,128)(2,1)S(1)}, u32[]{:S(2)}, u32[]{:S(2)}) collective-permute-start(bf16[512,1280]{1,0:T(8,128)(2,1)S(1)} %stack.39.rest_5_), channel_id=1, source_target_pairs={{0,4},{1,5},{2,6},{3,7},{4,8},{5,9},{6,10},{7,11},{8,12},{9,13},{1... | collective-permute-start | bytes 3932168 | tf_op jit(solution)/shard_map/ppermute | solution.py:41
  74.9 30.4 %collective-permute-start.13 = (bf16[512,1280]{1,0:T(8,128)(2,1)S(1)}, bf16[512,1280]{1,0:T(8,128)(2,1)S(1)}, u32[]{:S(2)}, u32[]{:S(2)}) collective-permute-start(bf16[512,1280]{1,0:T(8,128)(2,1)S(1)} %stack.39.rest_5_), channel_id=1, source_target_pairs={{0,12},{1,13},{2,14},{3,15},{4,0},{5,1},{6,2},{7,3},{8,4},{9,5},{1... | collective-permute-start | bytes 3932168 | tf_op jit(solution)/shard_map/ppermute | solution.py:41
  77.4 47.5 %collective-permute-start.8 = (bf16[256,4096]{1,0:T(8,128)(2,1)S(1)}, bf16[256,4096]{1,0:T(8,128)(2,1)}, u32[]{:S(2)}, u32[]{:S(2)}) collective-permute-start(bf16[256,4096]{1,0:T(8,128)(2,1)S(1)} %bitcast.27), channel_id=1, source_target_pairs={{0,64},{64,0},{1,65},{65,1},{2,66},{66,2},{3,67},{67,3},{4,68},{68... | collective-permute-start | bytes 6291464 | tf_op jit(solution)/shard_map/ppermute | solution.py:30
  92.2 27.1 %copy-start.9 = (bf16[256,1024]{1,0:T(8,128)(2,1)S(1)}, bf16[256,1024]{1,0:T(8,128)(2,1)}, u32[]{:S(2)}) copy-start(bf16[256,1024]{1,0:T(8,128)(2,1)} %pad_maximum_fusion.rest_0_.refs_0_) | copy-start | bytes 1572868
  92.2 20.1 %collective-permute-start.17 = (bf16[256,1280]{1,0:T(8,128)(2,1)S(1)}, bf16[256,1280]{1,0:T(8,128)(2,1)S(1)}, u32[]{:S(2)}, u32[]{:S(2)}) collective-permute-start(bf16[256,1280]{1,0:T(8,128)(2,1)S(1)} %slice.71), channel_id=1, source_target_pairs={{0,4},{1,5},{2,6},{3,7},{4,8},{5,9},{6,10},{7,11},{8,12},{9,13},{1... | collective-permute-start | bytes 1966088 | tf_op jit(solution)/shard_map/ppermute | solution.py:41
  92.2 28.0 %copy-start.12 = (bf16[512,1280]{1,0:T(8,128)(2,1)}, bf16[512,1280]{1,0:T(8,128)(2,1)S(1)}, u32[]{:S(2)}) copy-start(bf16[512,1280]{1,0:T(8,128)(2,1)S(1)} %collective-permute-done.16.rest_2_) | copy-start | bytes 3932164
  92.3 20.0 %collective-permute-start.18 = (bf16[256,1280]{1,0:T(8,128)(2,1)S(1)}, bf16[256,1280]{1,0:T(8,128)(2,1)S(1)}, u32[]{:S(2)}, u32[]{:S(2)}) collective-permute-start(bf16[256,1280]{1,0:T(8,128)(2,1)S(1)} %slice.72), channel_id=1, source_target_pairs={{0,12},{1,13},{2,14},{3,15},{4,0},{5,1},{6,2},{7,3},{8,4},{9,5},{1... | collective-permute-start | bytes 1966088 | tf_op jit(solution)/shard_map/ppermute | solution.py:41
  105.3 14.0 %collective-permute-start.19 = (bf16[256,1280]{1,0:T(8,128)(2,1)S(1)}, bf16[256,1280]{1,0:T(8,128)(2,1)S(1)}, u32[]{:S(2)}, u32[]{:S(2)}) collective-permute-start(bf16[256,1280]{1,0:T(8,128)(2,1)S(1)} %slice.73), channel_id=1, source_target_pairs={{0,4},{1,5},{2,6},{3,7},{4,8},{5,9},{6,10},{7,11},{8,12},{9,13},{1... | collective-permute-start | bytes 1966088 | tf_op jit(solution)/shard_map/ppermute | solution.py:41
  106.5 12.8 %collective-permute-start.20 = (bf16[256,1280]{1,0:T(8,128)(2,1)S(1)}, bf16[256,1280]{1,0:T(8,128)(2,1)S(1)}, u32[]{:S(2)}, u32[]{:S(2)}) collective-permute-start(bf16[256,1280]{1,0:T(8,128)(2,1)S(1)} %slice.74), channel_id=1, source_target_pairs={{0,12},{1,13},{2,14},{3,15},{4,0},{5,1},{6,2},{7,3},{8,4},{9,5},{1... | collective-permute-start | bytes 1966088 | tf_op jit(solution)/shard_map/ppermute | solution.py:41
  120.3 15.5 %collective-permute-start.21 = (bf16[256,1024]{1,0:T(8,128)(2,1)}, bf16[256,1024]{1,0:T(8,128)(2,1)}, u32[]{:S(2)}, u32[]{:S(2)}) collective-permute-start(bf16[256,1024]{1,0:T(8,128)(2,1)} %stack.42.refs_0_), channel_id=1, source_target_pairs={{0,1},{1,2},{2,3},{3,0},{4,5},{5,6},{6,7},{7,4},{8,9},{9,10},{10,1... | collective-permute-start | bytes 1572872 | tf_op jit(solution)/shard_map/ppermute | solution.py:41
  121.4 14.3 %collective-permute-start.22 = (bf16[256,1024]{1,0:T(8,128)(2,1)}, bf16[256,1024]{1,0:T(8,128)(2,1)}, u32[]{:S(2)}, u32[]{:S(2)}) collective-permute-start(bf16[256,1024]{1,0:T(8,128)(2,1)} %stack.42.refs_0_), channel_id=1, source_target_pairs={{0,2},{1,3},{2,0},{3,1},{4,6},{5,7},{6,4},{7,5},{8,10},{9,11},{10,... | collective-permute-start | bytes 1572872 | tf_op jit(solution)/shard_map/ppermute | solution.py:41
  121.5 14.9 %collective-permute-start.23 = (bf16[256,1024]{1,0:T(8,128)(2,1)}, bf16[256,1024]{1,0:T(8,128)(2,1)}, u32[]{:S(2)}, u32[]{:S(2)}) collective-permute-start(bf16[256,1024]{1,0:T(8,128)(2,1)} %stack.42.refs_0_), channel_id=1, source_target_pairs={{0,3},{1,0},{2,1},{3,2},{4,7},{5,4},{6,5},{7,6},{8,11},{9,8},{10,9... | collective-permute-start | bytes 1572872 | tf_op jit(solution)/shard_map/ppermute | solution.py:41
  124.0 23.1 %collective-permute-start.7 = (bf16[256,4096]{1,0:T(8,128)(2,1)S(1)}, bf16[256,4096]{1,0:T(8,128)(2,1)}, u32[]{:S(2)}, u32[]{:S(2)}) collective-permute-start(bf16[256,4096]{1,0:T(8,128)(2,1)S(1)} %bitcast.28), channel_id=1, source_target_pairs={{0,32},{32,0},{1,33},{33,1},{2,34},{34,2},{3,35},{35,3},{4,36},{36... | collective-permute-start | bytes 6291464 | tf_op jit(solution)/shard_map/ppermute | solution.py:30
  129.3 15.9 %copy-start.34 = (f32[4096]{0:T(1024)S(1)}, f32[4096]{0:T(1024)}, u32[]{:S(2)}) copy-start(f32[4096]{0:T(1024)} %param.15) | copy-start | bytes 49156
  129.3 17.8 %copy-start.33 = (f32[4096]{0:T(1024)S(1)}, f32[4096]{0:T(1024)}, u32[]{:S(2)}) copy-start(f32[4096]{0:T(1024)} %param.12) | copy-start | bytes 49156
  129.3 22.5 %collective-permute-start.14 = (bf16[256,4096]{1,0:T(8,128)(2,1)}, bf16[256,4096]{1,0:T(8,128)(2,1)}, u32[]{:S(2)}, u32[]{:S(2)}) collective-permute-start(bf16[256,4096]{1,0:T(8,128)(2,1)} %stack.40.xa_ref.refs_2_), channel_id=1, source_target_pairs={{0,32},{32,0},{1,33},{33,1},{2,34},{34,2},{3,35},{35,3},{4,36},{36... | collective-permute-start | bytes 6291464 | tf_op jit(solution)/shard_map/ppermute | solution.py:30
  139.4 26.7 %collective-permute-start.24 = (bf16[1024,1024]{1,0:T(8,128)(2,1)}, bf16[1024,1024]{1,0:T(8,128)(2,1)}, u32[]{:S(2)}, u32[]{:S(2)}) collective-permute-start(bf16[1024,1024]{1,0:T(8,128)(2,1)} %stack.43.refs_1_), channel_id=1, source_target_pairs={{0,4},{1,5},{2,6},{3,7},{4,8},{5,9},{6,10},{7,11},{8,12},{9,13},{1... | collective-permute-start | bytes 6291464 | tf_op jit(solution)/shard_map/ppermute | solution.py:41
  140.2 37.9 %collective-permute-start.25 = (bf16[1024,1024]{1,0:T(8,128)(2,1)}, bf16[1024,1024]{1,0:T(8,128)(2,1)}, u32[]{:S(2)}, u32[]{:S(2)}) collective-permute-start(bf16[1024,1024]{1,0:T(8,128)(2,1)} %stack.43.refs_1_), channel_id=1, source_target_pairs={{0,12},{1,13},{2,14},{3,15},{4,0},{5,1},{6,2},{7,3},{8,4},{9,5},{1... | collective-permute-start | bytes 6291464 | tf_op jit(solution)/shard_map/ppermute | solution.py:41
  151.8 15.7 %copy-start.6 = (bf16[512,1280]{1,0:T(8,128)(2,1)S(1)}, bf16[512,1280]{1,0:T(8,128)(2,1)}, u32[]{:S(2)}) copy-start(bf16[512,1280]{1,0:T(8,128)(2,1)} %copy-done.5) | copy-start | bytes 3932164
  151.8 15.7 %copy-start.8 = (bf16[512,1280]{1,0:T(8,128)(2,1)S(1)}, bf16[512,1280]{1,0:T(8,128)(2,1)}, u32[]{:S(2)}) copy-start(bf16[512,1280]{1,0:T(8,128)(2,1)} %copy-done.7) | copy-start | bytes 3932164
  151.8 15.7 %copy-start.11 = (bf16[512,1280]{1,0:T(8,128)(2,1)S(1)}, bf16[512,1280]{1,0:T(8,128)(2,1)}, u32[]{:S(2)}) copy-start(bf16[512,1280]{1,0:T(8,128)(2,1)} %copy-done.10) | copy-start | bytes 3932164
  151.8 15.7 %copy-start.13 = (bf16[512,1280]{1,0:T(8,128)(2,1)S(1)}, bf16[512,1280]{1,0:T(8,128)(2,1)}, u32[]{:S(2)}) copy-start(bf16[512,1280]{1,0:T(8,128)(2,1)} %copy-done.12) | copy-start | bytes 3932164
  151.8 15.7 %copy-start.17 = (bf16[256,1280]{1,0:T(8,128)(2,1)S(1)}, bf16[256,1280]{1,0:T(8,128)(2,1)}, u32[]{:S(2)}) copy-start(bf16[256,1280]{1,0:T(8,128)(2,1)} %copy-done.16) | copy-start | bytes 1966084
  151.8 15.7 %copy-start.19 = (bf16[256,1280]{1,0:T(8,128)(2,1)S(1)}, bf16[256,1280]{1,0:T(8,128)(2,1)}, u32[]{:S(2)}) copy-start(bf16[256,1280]{1,0:T(8,128)(2,1)} %copy-done.18) | copy-start | bytes 1966084
  167.4 26.5 %collective-permute-start.26 = (bf16[512,1024]{1,0:T(8,128)(2,1)S(1)}, bf16[512,1024]{1,0:T(8,128)(2,1)S(1)}, u32[]{:S(2)}, u32[]{:S(2)}) collective-permute-start(bf16[512,1024]{1,0:T(8,128)(2,1)S(1)} %slice.75), channel_id=1, source_target_pairs={{0,4},{1,5},{2,6},{3,7},{4,8},{5,9},{6,10},{7,11},{8,12},{9,13},{1... | collective-permute-start | bytes 3145736 | tf_op jit(solution)/shard_map/ppermute | solution.py:41
  177.1 33.8 %collective-permute-start.27 = (bf16[512,1024]{1,0:T(8,128)(2,1)S(1)}, bf16[512,1024]{1,0:T(8,128)(2,1)S(1)}, u32[]{:S(2)}, u32[]{:S(2)}) collective-permute-start(bf16[512,1024]{1,0:T(8,128)(2,1)S(1)} %attend.3.refs_0_), channel_id=1, source_target_pairs={{0,64},{64,0},{1,65},{65,1},{2,66},{66,2},{3,67},{67,3},{4,68},{68... | collective-permute-start | bytes 3145736 | tf_op jit(solution)/shard_map/ppermute | solution.py:30
  179.4 27.3 %collective-permute-start.28 = (bf16[512,1024]{1,0:T(8,128)(2,1)S(1)}, bf16[512,1024]{1,0:T(8,128)(2,1)S(1)}, u32[]{:S(2)}, u32[]{:S(2)}) collective-permute-start(bf16[512,1024]{1,0:T(8,128)(2,1)S(1)} %slice.77), channel_id=1, source_target_pairs={{0,12},{1,13},{2,14},{3,15},{4,0},{5,1},{6,2},{7,3},{8,4},{9,5},{1... | collective-permute-start | bytes 3145736 | tf_op jit(solution)/shard_map/ppermute | solution.py:41
  191.6 32.9 %collective-permute-start.29 = (bf16[512,1024]{1,0:T(8,128)(2,1)S(1)}, bf16[512,1024]{1,0:T(8,128)(2,1)S(1)}, u32[]{:S(2)}, u32[]{:S(2)}) collective-permute-start(bf16[512,1024]{1,0:T(8,128)(2,1)S(1)} %attend.2.refs_0_), channel_id=1, source_target_pairs={{0,64},{64,0},{1,65},{65,1},{2,66},{66,2},{3,67},{67,3},{4,68},{68... | collective-permute-start | bytes 3145736 | tf_op jit(solution)/shard_map/ppermute | solution.py:30
  203.6 37.8 %collective-permute-start.30 = (bf16[512,1024]{1,0:T(8,128)(2,1)}, bf16[512,1024]{1,0:T(8,128)(2,1)}, u32[]{:S(2)}, u32[]{:S(2)}) collective-permute-start(bf16[512,1024]{1,0:T(8,128)(2,1)} %get-tuple-element.18), channel_id=1, source_target_pairs={{0,32},{32,0},{1,33},{33,1},{2,34},{34,2},{3,35},{35,3},{4,36},{36... | collective-permute-start | bytes 3145736 | tf_op jit(solution)/shard_map/ppermute | solution.py:30
  217.4 24.1 %collective-permute-start.31 = (bf16[512,1024]{1,0:T(8,128)(2,1)}, bf16[512,1024]{1,0:T(8,128)(2,1)}, u32[]{:S(2)}, u32[]{:S(2)}) collective-permute-start(bf16[512,1024]{1,0:T(8,128)(2,1)} %get-tuple-element.19), channel_id=1, source_target_pairs={{0,32},{32,0},{1,33},{33,1},{2,34},{34,2},{3,35},{35,3},{4,36},{36... | collective-permute-start | bytes 3145736 | tf_op jit(solution)/shard_map/ppermute | solution.py:30
  223.9 17.5 %collective-permute-start.32 = (bf16[512,1024]{1,0:T(8,128)(2,1)}, bf16[512,1024]{1,0:T(8,128)(2,1)}, u32[]{:S(2)}, u32[]{:S(2)}) collective-permute-start(bf16[512,1024]{1,0:T(8,128)(2,1)} %get-tuple-element.20), channel_id=1, source_target_pairs={{0,32},{32,0},{1,33},{33,1},{2,34},{34,2},{3,35},{35,3},{4,36},{36... | collective-permute-start | bytes 3145736 | tf_op jit(solution)/shard_map/ppermute | solution.py:30
  230.9 10.5 %collective-permute-start.33 = (bf16[512,1024]{1,0:T(8,128)(2,1)}, bf16[512,1024]{1,0:T(8,128)(2,1)}, u32[]{:S(2)}, u32[]{:S(2)}) collective-permute-start(bf16[512,1024]{1,0:T(8,128)(2,1)} %get-tuple-element.21), channel_id=1, source_target_pairs={{0,32},{32,0},{1,33},{33,1},{2,34},{34,2},{3,35},{35,3},{4,36},{36... | collective-permute-start | bytes 3145736 | tf_op jit(solution)/shard_map/ppermute | solution.py:30
  (23 other events, 122.8 us)

commit v3 on v2

--- a/solution.py
+++ b/solution.py
@@ -244,41 +244,45 @@
     )(offs, line, one, three, two_b if head else two_a)
 
 
-def project_kernel(first, mixed_ref, w_ref, *rest):
-    out_refs = rest[-3:-1]
-    for part, out_ref in enumerate(out_refs):
+def project_kernel(mixed_a_ref, mixed_b_ref, w_ref, meta_ref, weight_ref, *outs):
+    score_ref = outs[-1]
+    for part, out_ref in enumerate(outs[:2]):
 
         @pl.loop(0, COLS // 256)
         def _(n, part=part, out_ref=out_ref):
             from_cols = pl.ds(pl.multiple_of(part * COLS + n * 256, 256), 256)
             cols = pl.ds(pl.multiple_of(n * 256, 256), 256)
-            out_ref[:, cols] = jnp.dot(
-                mixed_ref[...], w_ref[:, from_cols], preferred_element_type=jnp.float32
-            ).astype(jnp.bfloat16)
-
-    meta_ref, weight_ref, score_ref = rest[0], rest[1], rest[-1]
-    token = jnp.zeros((2 * RECLEN, 1), jnp.float32)
-    for part, out_ref in enumerate(out_refs):
-        terms = out_ref[...].astype(jnp.float32) * weight_ref[part : part + 1, :]
-        token += jnp.sum(terms, axis=1, keepdims=True)
-    score_ref[...] = row_scores(token, meta_ref, first, 2)
-
-
-def project(mixed, w, meta, weight, first):
+            for pair, mixed_ref in enumerate((mixed_a_ref, mixed_b_ref)):
+                rows = slice(pair * 2 * RECLEN, (pair + 1) * 2 * RECLEN)
+                out_ref[rows, cols] = jnp.dot(
+                    mixed_ref[...], w_ref[:, from_cols], preferred_element_type=jnp.float32
+                ).astype(jnp.bfloat16)
+
+    scores = jnp.zeros((1, 128), jnp.float32)
+    for i in range(4):
+        rows = slice(i * RECLEN, (i + 1) * RECLEN)
+        token = jnp.zeros((RECLEN, 1), jnp.float32)
+        for part, out_ref in enumerate(outs[:2]):
+            terms = out_ref[rows, :].astype(jnp.float32) * weight_ref[part : part + 1, :]
+            token += jnp.sum(terms, axis=1, keepdims=True)
+        scores += row_scores(token, meta_ref, i, 1)
+    score_ref[...] = scores
+
+
+def project(mixed_a, mixed_b, w, meta, weight):
     vmem = pl.BlockSpec(memory_space=pltpu.VMEM)
-    tokens = mixed.shape[0]
-    return pl.pallas_call(
-        lambda *refs: project_kernel(first, *refs),
-        out_shape=[jax.ShapeDtypeStruct((tokens, COLS), jnp.bfloat16)] * 2
+    return pl.pallas_call(
+        project_kernel,
+        out_shape=[jax.ShapeDtypeStruct((4 * RECLEN, COLS), jnp.bfloat16)] * 2
         + [jax.ShapeDtypeStruct((1, 128), jnp.float32)],
-        in_specs=[vmem] * 2 + [pl.BlockSpec(memory_space=pltpu.SMEM), vmem],
+        in_specs=[vmem] * 3 + [pl.BlockSpec(memory_space=pltpu.SMEM), vmem],
         out_specs=[vmem] * 3,
         compiler_params=pltpu.CompilerParams(vmem_limit_bytes=PROJECT_VMEM),
         cost_estimate=pl.CostEstimate(
-            flops=2 * tokens * HEADS * 2 * COLS, bytes_accessed=2 << 20, transcendentals=0
+            flops=2 * 4 * RECLEN * HEADS * 2 * COLS, bytes_accessed=2 << 20, transcendentals=0
         ),
         name="project",
-    )(mixed, w, meta, weight)
+    )(mixed_a, mixed_b, w, meta, weight)
 
 
 def row_scores(token, place_ref, first, count):
@@ -301,16 +305,15 @@
 
 
 def finish_kernel(meta_ref, *refs):
-    x_refs, kept_refs, in_refs = refs[:4], refs[4:8], refs[8:12]
-    hidden_ref, acc_ref = refs[12:]
+    x_refs, kept_refs, in_refs = refs[:4], refs[4:6], refs[6:8]
+    hidden_ref, acc_ref = refs[8:]
     for i in range(4):
-        mine = slice(i % 2 * RECLEN, (i % 2 + 1) * RECLEN)
-        theirs = slice((1 - i % 2) * RECLEN, (2 - i % 2) * RECLEN)
+        mine = slice(i * RECLEN, (i + 1) * RECLEN)
+        theirs = slice((i ^ 1) * RECLEN, ((i ^ 1) + 1) * RECLEN)
         total = x_refs[i][...].astype(jnp.float32)
         for head in range(2):
-            n = i // 2 * 2 + head
-            total += kept_refs[n][mine, :].astype(jnp.float32)
-            total += in_refs[n][theirs, :].astype(jnp.float32)
+            total += kept_refs[head][mine, :].astype(jnp.float32)
+            total += in_refs[head][theirs, :].astype(jnp.float32)
         moved = packed_rows(meta_ref, i, total)
         if i == 0:
             acc_ref[...] = moved
@@ -456,15 +459,15 @@
     w_near, w_far = arrange(out_offs, out_pieces, 0), arrange(out_offs, out_pieces, 1)
 
     terms = [
-        project(mixed_a, w_near, meta, weight, 0),
-        project(far_a, w_far, meta, weight, 0),
-        project(mixed_b, w_near, meta, weight, 2),
-        project(far_b, w_far, meta, weight, 2),
+        project(mixed_a, mixed_b, w_near, meta, weight),
+        project(far_a, far_b, w_far, meta, weight),
     ]
     hidden_out = finish(meta, slots, [t[1] for t in terms], [swap_co(t[0]) for t in terms])
-    partial = record_score(meta, own_record, score_weights[None, :])
-    partial += (terms[0][2] + terms[2][2]) + (terms[3][2] + terms[1][2])
-    scores = lax.psum(partial[0, :4], ("xh", "co"))
+    scores = record_score(meta, own_record, score_weights[None, :])
+    scores += terms[0][2] + terms[1][2]
+    scores += swap_co(scores)
+    scores += stack([swap_xh(scores)], [(0, 0, 1)], hidden_out)
+    scores = scores[0, :4]
     record_scores = (scores / lens.astype(jnp.float32))[None, :]
     return (hidden_out, record_scores)
 

time: 253 us -> 241 us (0.953)
  waiting for transfers between devices: 60.4 us -> 53 us
  blocking collectives: 39.3 us -> 32.7 us
  starting transfers between devices: 49.5 us -> 54.5 us
    ppermute x21, waiting for transfers between devices: 51.5 us -> 41.5 us  [plane_perm(): return lambda v: lax.ppermute(v, CORE_ZY, pairs)]
    ppermute x11, starting transfers between devices: 15.6 us -> 22.9 us  [ring(): lax.ppermute(v, axis, [(i, (i + step) % size) for i in range(size)])]
    psum x1 -> x0, blocking collectives: 6.63 us -> none  [on_device(): scores = lax.psum(partial[0, :4], ('xh', 'co'))]
    unnamed x74 -> x50, local copies, waits for them, and re-layouts: 12 us -> 5.74 us
    pallas_call x4 -> x2, Pallas kernels: 22 us -> 16 us  [project(): pl.pallas_call(project_kernel, out_shape=[jax.ShapeDtypeStruct((4 * RECLE...]
    pallas_call x2, Pallas kernels: 18.9 us -> 24.2 us  [attend(): pl.pallas_call(attend_kernel, out_shape=jax.ShapeDtypeStruct((2 * RECLEN,...]
    slice x3, local copies, waits for them, and re-layouts: 1.38 us -> 4.15 us  [plane_gather_second(): two_b = plane_perm(-1, False)(three[half:])]
    slice x3, local copies, waits for them, and re-layouts: 1.38 us -> 4.11 us  [plane_gather_second(): two_a = plane_perm(1, False)(one[:half])]
  transfers between devices with their start and end apart: 34 -> 34, of which waited for: 12 -> 11; matrix products, arithmetic and copies ran while one was open for 4% -> 6% of each run, Pallas kernels for 27% -> 30%
where the time goes in v3:
time: 241 us; the launch traced here: 240 us
  Pallas kernels  76.9 us (32%)
  starting transfers between devices  54.5 us (23%)
  waiting for transfers between devices  53 us (22%)
  blocking collectives  32.7 us (14%)
  local copies, waits for them, and re-layouts  17.1 us (7%)
  other arithmetic  4.62 us (2%)
    ppermute x21, waiting for transfers between devices, plane_perm(): return lambda v: lax.ppermute(v, CORE_ZY, pairs)  41.5 us
    all_to_all x1, blocking collectives, on_device(): lax.all_to_all(send_block, ('xl', 'z', 'y'), split_axis=0, concat_axis=0,...  32.7 us
    ppermute x21, starting transfers between devices, plane_perm(): return lambda v: lax.ppermute(v, CORE_ZY, pairs)  29.2 us
    pallas_call x2, Pallas kernels, attend(): pl.pallas_call(attend_kernel, out_shape=jax.ShapeDtypeStruct((2 * RECLEN,...  24.2 us
    ppermute x11, starting transfers between devices, ring(): lax.ppermute(v, axis, [(i, (i + step) % size) for i in range(size)])  22.9 us
    pallas_call x2, Pallas kernels, project(): pl.pallas_call(project_kernel, out_shape=[jax.ShapeDtypeStruct((4 * RECLE...  16 us
    pallas_call x2, Pallas kernels, normalize(): pl.pallas_call(normalize_kernel, out_shape=jax.ShapeDtypeStruct((2 * RECL...  10.1 us
    pallas_call x2, Pallas kernels, arrange(): pl.pallas_call(lambda *refs: arrange_kernel(head, *refs), out_shape=jax.S...  8.87 us
  transfers between devices with their start and end apart: 34, of which 11 were waited for; matrix products, arithmetic and copies ran while one was open for 6% of the time, Pallas kernels for 30%

profile of v3, /device:TPU:1, one launch (start us, length us, event | category | flops | bytes accessed | tf_op | source)
XLA Modules:
  0.0 239.9 jit_solution(15792758506791874020)
XLA Ops:
  0.6 2.1 collective-permute-start
  2.8 2.5 %collective-permute-start.1 = (bf16[128,1024]{1,0:T(8,128)(2,1)}, bf16[128,1024]{1,0:T(8,128)(2,1)S(1)}, u32[]{:S(2)}, u32[]{:S(2)}) collective-permute-start(bf16[128,1024]{1,0:T(8,128)(2,1)} %bitcast.40), channel_id=1, source_target_pairs={{0,64},{64,0},{16,80},{80,16},{1,65},{65,1},{17,81},{81,17},{2,66}... | collective-permute-start | bytes 786440 | tf_op jit(solution)/shard_map/ppermute | solution.py:379
  5.2 1.8 collective-permute-start.3
  7.0 3.3 %collective-permute-start.4 = (bf16[128,1280]{1,0:T(8,128)(2,1)}, bf16[128,1280]{1,0:T(8,128)(2,1)S(1)}, u32[]{:S(2)}, u32[]{:S(2)}) collective-permute-start(bf16[128,1280]{1,0:T(8,128)(2,1)} %bitcast.31), channel_id=1, source_target_pairs={{0,2},{1,3},{2,0},{3,1},{4,6},{5,7},{6,4},{7,5},{8,10},{9,11},{10,... | collective-permute-start | bytes 983048 | tf_op jit(solution)/shard_map/ppermute | solution.py:41
  13.7 3.1 %collective-permute-done.1 = bf16[128,1024]{1,0:T(8,128)(2,1)S(1)} collective-permute-done((bf16[128,1024]{1,0:T(8,128)(2,1)}, bf16[128,1024]{1,0:T(8,128)(2,1)S(1)}, u32[]{:S(2)}, u32[]{:S(2)}) %collective-permute-start.1) | collective-permute-done | bytes 262176 | tf_op jit(solution)/shard_map/ppermute | solution.py:379
  16.8 2.0 collective-permute-done.2
  20.9 3.7 %collective-permute-done.6.rest_2_.refs_0_ = bf16[128,1280]{1,0:T(8,128)(2,1)S(1)} collective-permute-done((bf16[128,1280]{1,0:T(8,128)(2,1)}, bf16[128,1280]{1,0:T(8,128)(2,1)S(1)}, u32[]{:S(2)}, u32[]{:S(2)}) %collective-permute-start.6) | collective-permute-done | bytes 327712 | tf_op jit(solution)/shard_map/ppermute | solution.py:30
  25.3 3.9 %order_records.1 = bf16[32,8,4096]{2,1,0:T(8,128)(2,1)} custom-call(s32[32]{0:T(128)} %select_reduce_fusion.2.outgoing_ref, bf16[32,8,4096]{2,1,0:T(8,128)(2,1)} %bitcast.38, bf16[256,1024]{1,0:T(8,128)(2,1)} %pad_maximum_fusion.rest_0_.refs_0_, bf16[512,1280]{1,0:T(8,128)(2,1)} %copy-done, bf16[128,1280]{1,0:T(8,128)(2,1)} %copy-done.15), custom_call_target="tpu_custom_call" | custom-call | bytes 4194304 | tf_op jit(solution)/shard_map/order_records/pallas_call | solution.py:97
  29.2 32.7 %all_to_all.5 = bf16[32,8,4096]{2,1,0:T(8,128)(2,1)S(1)} all-to-all(bf16[32,8,4096]{2,1,0:T(8,128)(2,1)} %order_records.1), channel_id=1, replica_groups=mesh['xh'=2,'co'=2,'xl'=2,'z'=4,'y'=4] {'xl','z','y'}, dimensions={0} | all-to-all | bytes 4194304 | tf_op jit(solution)/shard_map/all_to_all | solution.py:394
  62.0 3.7 %collective-permute-start.10 = (bf16[128,1280]{1,0:T(8,128)(2,1)S(1)}, bf16[128,1280]{1,0:T(8,128)(2,1)S(1)}, u32[]{:S(2)}, u32[]{:S(2)}) collective-permute-start(bf16[128,1280]{1,0:T(8,128)(2,1)S(1)} %stack.39.refs_0_), channel_id=1, source_target_pairs={{0,2},{1,3},{2,0},{3,1},{4,6},{5,7},{6,4},{7,5},{8,10},{9,11},{10,... | collective-permute-start | bytes 983048 | tf_op jit(solution)/shard_map/ppermute | solution.py:41
  66.0 1.1 collective-permute-start.8
  67.2 2.0 collective-permute-done.9.refs_1_
  69.2 2.1 collective-permute-start.16
  71.3 2.3 collective-permute-done.10.refs_2_
  73.8 1.2 collective-permute-start.12
  74.9 1.7 collective-permute-start.13
  76.7 15.4 %collective-permute-done.15.rest_1_ = bf16[512,1280]{1,0:T(8,128)(2,1)S(1)} collective-permute-done((bf16[512,1280]{1,0:T(8,128)(2,1)S(1)}, bf16[512,1280]{1,0:T(8,128)(2,1)S(1)}, u32[]{:S(2)}, u32[]{:S(2)}) %collective-permute-start.15) | collective-permute-done | bytes 1310752 | tf_op jit(solution)/shard_map/ppermute | solution.py:41
  94.0 2.7 %collective-permute-start.18 = (bf16[256,1280]{1,0:T(8,128)(2,1)}, bf16[256,1280]{1,0:T(8,128)(2,1)}, u32[]{:S(2)}, u32[]{:S(2)}) collective-permute-start(bf16[256,1280]{1,0:T(8,128)(2,1)} %slice.72), channel_id=1, source_target_pairs={{0,12},{1,13},{2,14},{3,15},{4,0},{5,1},{6,2},{7,3},{8,4},{9,5},{1... | collective-permute-start | bytes 1966088 | tf_op jit(solution)/shard_map/ppermute | solution.py:41
  96.7 9.5 %collective-permute-done.12.refs_1_.rest_6_ = bf16[512,1280]{1,0:T(8,128)(2,1)S(1)} collective-permute-done((bf16[512,1280]{1,0:T(8,128)(2,1)S(1)}, bf16[512,1280]{1,0:T(8,128)(2,1)S(1)}, u32[]{:S(2)}, u32[]{:S(2)}) %collective-permute-start.12) | collective-permute-done | bytes 1310752 | tf_op jit(solution)/shard_map/ppermute | solution.py:41
  109.1 2.7 %collective-permute-start.20 = (bf16[256,1280]{1,0:T(8,128)(2,1)}, bf16[256,1280]{1,0:T(8,128)(2,1)}, u32[]{:S(2)}, u32[]{:S(2)}) collective-permute-start(bf16[256,1280]{1,0:T(8,128)(2,1)} %slice.74), channel_id=1, source_target_pairs={{0,12},{1,13},{2,14},{3,15},{4,0},{5,1},{6,2},{7,3},{8,4},{9,5},{1... | collective-permute-start | bytes 1966088 | tf_op jit(solution)/shard_map/ppermute | solution.py:41
  111.7 5.0 %collective-permute-start.7 = (bf16[256,4096]{1,0:T(8,128)(2,1)S(1)}, bf16[256,4096]{1,0:T(8,128)(2,1)}, u32[]{:S(2)}, u32[]{:S(2)}) collective-permute-start(bf16[256,4096]{1,0:T(8,128)(2,1)S(1)} %bitcast.26), channel_id=1, source_target_pairs={{0,32},{32,0},{1,33},{33,1},{2,34},{34,2},{3,35},{35,3},{4,36},{36... | collective-permute-start | bytes 6291464 | tf_op jit(solution)/shard_map/ppermute | solution.py:30
  116.7 1.3 copy-done.3
  118.0 3.1 %stack.41.xa_ref.refs_2_ = bf16[256,4096]{1,0:T(8,128)(2,1)} custom-call(bf16[256,4096]{1,0:T(8,128)(2,1)} %collective-permute-done.8.refs_0_, bf16[512,1280]{1,0:T(8,128)(2,1)S(1)} %collective-permute-done.12.refs_1_.rest_6_, bf16[512,1280]{1,0:T(8,128)(2,1)S(1)} %copy-done.3), custom_call_target="tpu_custom_call" | custom-call | bytes 1048576 | tf_op jit(solution)/shard_map/stack/pallas_call | solution.py:55
  122.1 2.9 %collective-permute-start.22 = (bf16[256,1024]{1,0:T(8,128)(2,1)}, bf16[256,1024]{1,0:T(8,128)(2,1)}, u32[]{:S(2)}, u32[]{:S(2)}) collective-permute-start(bf16[256,1024]{1,0:T(8,128)(2,1)} %stack.43.refs_0_), channel_id=1, source_target_pairs={{0,2},{1,3},{2,0},{3,1},{4,6},{5,7},{6,4},{7,5},{8,10},{9,11},{10,... | collective-permute-start | bytes 1572872 | tf_op jit(solution)/shard_map/ppermute | solution.py:41
  125.8 6.0 %collective-permute-done.21.refs_1_ = bf16[256,1024]{1,0:T(8,128)(2,1)} collective-permute-done((bf16[256,1024]{1,0:T(8,128)(2,1)}, bf16[256,1024]{1,0:T(8,128)(2,1)}, u32[]{:S(2)}, u32[]{:S(2)}) %collective-permute-start.21) | collective-permute-done | bytes 524320 | tf_op jit(solution)/shard_map/ppermute | solution.py:41
  131.9 5.9 %collective-permute-done.22.refs_2_ = bf16[256,1024]{1,0:T(8,128)(2,1)} collective-permute-done((bf16[256,1024]{1,0:T(8,128)(2,1)}, bf16[256,1024]{1,0:T(8,128)(2,1)}, u32[]{:S(2)}, u32[]{:S(2)}) %collective-permute-start.22) | collective-permute-done | bytes 524320 | tf_op jit(solution)/shard_map/ppermute | solution.py:41
  138.1 3.1 %stack.44.refs_1_ = bf16[1024,1024]{1,0:T(8,128)(2,1)} custom-call(bf16[256,1024]{1,0:T(8,128)(2,1)} %stack.43.refs_0_, bf16[256,1024]{1,0:T(8,128)(2,1)} %collective-permute-done.21.refs_1_, bf16[256,1024]{1,0:T(8,128)(2,1)} %collective-permute-done.22.refs_2_, bf16[256,1024]{1,0:T(8,128)(2,1)} %collective-permute-done.23.refs_3_), custom_call_target="tpu_custom_call" | custom-call | bytes 1048576 | tf_op jit(solution)/shard_map/stack/pallas_call | solution.py:55
  141.2 1.1 collective-permute-start.24
  142.3 1.6 collective-permute-start.25
  146.8 4.6 %normalize.2.normed_ref = bf16[512,4096]{1,0:T(8,128)(2,1)S(1)} custom-call(s32[32]{0:T(128)S(1)} %pad_add_fusion.2.offs_ref, bf16[256,4096]{1,0:T(8,128)(2,1)S(1)} %bitcast.27, bf16[256,4096]{1,0:T(8,128)(2,1)} %collective-permute-done.7.xb_ref.refs_1_, f32[1,4096]{1,0:T(1,128)S(1)} %bitcast.35), custom_call_target="tpu_custom_call" | custom-call | flops 4194304 | bytes 12582912 | tf_op jit(solution)/shard_map/normalize/pallas_call | solution.py:127
  151.6 5.4 %normalize.3.rest_10_.normed_ref = bf16[512,4096]{1,0:T(8,128)(2,1)S(1)} custom-call(s32[32]{0:T(128)S(1)} %pad_add_fusion.2.offs_ref, bf16[256,4096]{1,0:T(8,128)(2,1)} %stack.41.xa_ref.refs_2_, bf16[256,4096]{1,0:T(8,128)(2,1)} %collective-permute-done.14.xb_ref.refs_3_, f32[1,4096]{1,0:T(1,128)S(1)} %bitcast.36), custom_call_target="tpu_custom_call" | custom-call | flops 4194304 | bytes 12582912 | tf_op jit(solution)/shard_map/normalize/pallas_call | solution.py:127
  157.0 12.1 %attend.3.mixed_b_ref = bf16[512,1024]{1,0:T(8,128)(2,1)} custom-call(bf16[512,4096]{1,0:T(8,128)(2,1)S(1)} %normalize.3.rest_10_.normed_ref, f32[256,128]{1,0:T(8,128)S(1)} %get-tuple-element.38.cos_ref, f32[256,128]{1,0:T(8,128)S(1)} %get-tuple-element.39.sin_ref, s32[2,256,1]{2,1,0:T(8,128)S(1)} %copy-done.19, s32[2,1,256]{2,1,0:T(1,128)S(1)} %slice.66.segk_ref, ...), custom_call_target="tpu_custom_call" | custom-call | flops 5368709120 | bytes 16777216 | tf_op jit(solution)/shard_map/attend/pallas_call | solution.py:192
  169.2 1.7 collective-permute-start.27
  170.8 2.3 slice.76
  173.1 2.3 slice.77
  175.4 2.7 %collective-permute-start.29 = (bf16[512,1024]{1,0:T(8,128)(2,1)}, bf16[512,1024]{1,0:T(8,128)(2,1)}, u32[]{:S(2)}, u32[]{:S(2)}) collective-permute-start(bf16[512,1024]{1,0:T(8,128)(2,1)} %slice.77), channel_id=1, source_target_pairs={{0,12},{1,13},{2,14},{3,15},{4,0},{5,1},{6,2},{7,3},{8,4},{9,5},{1... | collective-permute-start | bytes 3145736 | tf_op jit(solution)/shard_map/ppermute | solution.py:41
  178.1 12.1 %attend.2.mixed_a_ref = bf16[512,1024]{1,0:T(8,128)(2,1)} custom-call(bf16[512,4096]{1,0:T(8,128)(2,1)S(1)} %normalize.2.normed_ref, f32[256,128]{1,0:T(8,128)S(1)} %get-tuple-element.38.cos_ref, f32[256,128]{1,0:T(8,128)S(1)} %get-tuple-element.39.sin_ref, s32[2,256,1]{2,1,0:T(8,128)S(1)} %copy-done.17, s32[2,1,256]{2,1,0:T(1,128)S(1)} %slice.59.segk_ref, ...), custom_call_target="tpu_custom_call" | custom-call | flops 5368709120 | bytes 16777216 | tf_op jit(solution)/shard_map/attend/pallas_call | solution.py:192
  190.2 1.3 collective-permute-start.28
  192.0 4.4 %arrange_0.1.w_ref = bf16[1024,2048]{1,0:T(8,128)(2,1)S(1)} custom-call(s32[16]{0:T(128)S(1)} %fusion.6.refs_0_, bf16[1024,1024]{1,0:T(8,128)(2,1)} %stack.44.refs_1_, bf16[1024,1024]{1,0:T(8,128)(2,1)} %collective-permute-done.24.refs_2_, bf16[1024,1024]{1,0:T(8,128)(2,1)} %collective-permute-done.25.refs_3_, bf16[512,1024]{1,0:T(8,128)(2,1)} %collective-permute-done.26.refs_4_), custom_call_target="tpu_custom_call" | custom-call | bytes 8388608 | tf_op jit(solution)/shard_map/arrange_0/pallas_call | solution.py:231
  196.4 8.2 %project.2 = (bf16[1024,1024]{1,0:T(8,128)(2,1)S(1)}, bf16[1024,1024]{1,0:T(8,128)(2,1)S(1)}, f32[1,128]{1,0:T(1,128)S(1)}) custom-call(bf16[512,1024]{1,0:T(8,128)(2,1)} %attend.2.mixed_a_ref, bf16[512,1024]{1,0:T(8,128)(2,1)} %attend.3.mixed_b_ref, bf16[1024,2048]{1,0:T(8,128)(2,1)S(1)} %arrange_0.1.w_ref, s32[13]{0:T(128)S(1)} %concatenate.16.meta_ref, ...), custom_call_target="tpu_custom_call" | custom-call | flops 4294967296 | bytes 2097152 | tf_op jit(solution)/shard_map/project/pallas_call | solution.py:274
  204.6 7.3 %collective-permute-start.30 = (bf16[1024,1024]{1,0:T(8,128)(2,1)S(1)}, bf16[1024,1024]{1,0:T(8,128)(2,1)S(1)}, u32[]{:S(2)}, u32[]{:S(2)}) collective-permute-start(bf16[1024,1024]{1,0:T(8,128)(2,1)S(1)} %get-tuple-element.10), channel_id=1, source_target_pairs={{0,32},{32,0},{1,33},{33,1},{2,34},{34,2},{3,35},{35,3},{4,36},{36... | collective-permute-start | bytes 6291464 | tf_op jit(solution)/shard_map/ppermute | solution.py:30
  211.9 4.4 %arrange_1.1.w_ref = bf16[1024,2048]{1,0:T(8,128)(2,1)S(1)} custom-call(s32[16]{0:T(128)S(1)} %fusion.6.refs_0_, bf16[1024,1024]{1,0:T(8,128)(2,1)} %stack.44.refs_1_, bf16[1024,1024]{1,0:T(8,128)(2,1)} %collective-permute-done.24.refs_2_, bf16[1024,1024]{1,0:T(8,128)(2,1)} %collective-permute-done.25.refs_3_, bf16[512,1024]{1,0:T(8,128)(2,1)} %collective-permute-done.29.refs_4_), custom_call_target="tpu_custom_call" | custom-call | bytes 8388608 | tf_op jit(solution)/shard_map/arrange_1/pallas_call | solution.py:231
  216.3 7.8 %project.3 = (bf16[1024,1024]{1,0:T(8,128)(2,1)S(1)}, bf16[1024,1024]{1,0:T(8,128)(2,1)S(1)}, f32[1,128]{1,0:T(1,128)S(1)}) custom-call(bf16[512,1024]{1,0:T(8,128)(2,1)} %collective-permute-done.27.mixed_a_ref, bf16[512,1024]{1,0:T(8,128)(2,1)S(1)} %collective-permute-done.28.mixed_b_ref, bf16[1024,2048]{1,0:T(8,128)(2,1)S(1)} %arrange_1.1.w_ref, ...), custom_call_target="tpu_custom_call" | custom-call | flops 4294967296 | bytes 2097152 | tf_op jit(solution)/shard_map/project/pallas_call | solution.py:274
  224.2 2.7 %collective-permute-start.31 = (bf16[1024,1024]{1,0:T(8,128)(2,1)S(1)}, bf16[1024,1024]{1,0:T(8,128)(2,1)S(1)}, u32[]{:S(2)}, u32[]{:S(2)}) collective-permute-start(bf16[1024,1024]{1,0:T(8,128)(2,1)S(1)} %get-tuple-element.11), channel_id=1, source_target_pairs={{0,32},{32,0},{1,33},{33,1},{2,34},{34,2},{3,35},{35,3},{4,36},{36... | collective-permute-start | bytes 6291464 | tf_op jit(solution)/shard_map/ppermute | solution.py:30
  228.0 2.6 %collective-permute-done.32 = f32[1,128]{1,0:T(1,128)S(1)} collective-permute-done((f32[1,128]{1,0:T(1,128)S(1)}, f32[1,128]{1,0:T(1,128)S(1)}, u32[]{:S(2)}, u32[]{:S(2)}) %collective-permute-start.32) | collective-permute-done | bytes 544 | tf_op jit(solution)/shard_map/ppermute | solution.py:30
  230.6 1.7 collective-permute-start.33
  232.3 5.5 %finish.1.refs_1_ = bf16[896,1024]{1,0:T(8,128)(2,1)} custom-call(s32[13]{0:T(128)S(1)} %concatenate.16.meta_ref, bf16[256,4096]{1,0:T(8,128)(2,1)S(1)} %bitcast.29, bf16[256,4096]{1,0:T(8,128)(2,1)} %collective-permute-done.7.xb_ref.refs_1_, bf16[256,4096]{1,0:T(8,128)(2,1)} %stack.41.xa_ref.refs_2_, ...), custom_call_target="tpu_custom_call" | custom-call | flops 1879048192 | bytes 16777216 | tf_op jit(solution)/shard_map/finish/pallas_call | solution.py:331
  237.8 1.5 copy-done.5
  (133 shorter events, 18.9 us)
Async XLA Ops:
  0.6 19.1 %copy-start.18 = (bf16[128,1,1280]{2,0,1:T(8,128)(2,1)S(1)}, bf16[128,1,1280]{2,0,1:T(8,128)(2,1)}, u32[]{:S(2)}) copy-start(bf16[128,1,1280]{2,0,1:T(8,128)(2,1)} %param.13) | copy-start | bytes 983044
  0.6 11.1 %collective-permute-start = (bf16[128,1024]{1,0:T(8,128)(2,1)}, bf16[128,1024]{1,0:T(8,128)(2,1)S(1)}, u32[]{:S(2)}, u32[]{:S(2)}) collective-permute-start(bf16[128,1024]{1,0:T(8,128)(2,1)} %bitcast.39), channel_id=1, source_target_pairs={{0,16},{16,0},{1,17},{17,1},{2,18},{18,2},{3,19},{19,3},{4,20},{20... | collective-permute-start | bytes 786440 | tf_op jit(solution)/shard_map/ppermute | solution.py:30
  2.8 14.0 %collective-permute-start.1 = (bf16[128,1024]{1,0:T(8,128)(2,1)}, bf16[128,1024]{1,0:T(8,128)(2,1)S(1)}, u32[]{:S(2)}, u32[]{:S(2)}) collective-permute-start(bf16[128,1024]{1,0:T(8,128)(2,1)} %bitcast.40), channel_id=1, source_target_pairs={{0,64},{64,0},{16,80},{80,16},{1,65},{65,1},{17,81},{81,17},{2,66}... | collective-permute-start | bytes 786440 | tf_op jit(solution)/shard_map/ppermute | solution.py:379
  5.2 13.6 %collective-permute-start.2 = (bf16[128,1024]{1,0:T(8,128)(2,1)}, bf16[128,1024]{1,0:T(8,128)(2,1)S(1)}, u32[]{:S(2)}, u32[]{:S(2)}) collective-permute-start(bf16[128,1024]{1,0:T(8,128)(2,1)} %bitcast.41), channel_id=1, source_target_pairs={{0,80},{80,0},{16,64},{64,16},{1,81},{81,1},{17,65},{65,17},{2,82}... | collective-permute-start | bytes 786440 | tf_op jit(solution)/shard_map/ppermute | solution.py:380
  5.2 14.5 %collective-permute-start.3 = (bf16[128,1280]{1,0:T(8,128)(2,1)}, bf16[128,1280]{1,0:T(8,128)(2,1)S(1)}, u32[]{:S(2)}, u32[]{:S(2)}) collective-permute-start(bf16[128,1280]{1,0:T(8,128)(2,1)} %bitcast.30), channel_id=1, source_target_pairs={{0,1},{1,2},{2,3},{3,0},{4,5},{5,6},{6,7},{7,4},{8,9},{9,10},{10,1... | collective-permute-start | bytes 983048 | tf_op jit(solution)/shard_map/ppermute | solution.py:41
  7.0 12.7 %collective-permute-start.4 = (bf16[128,1280]{1,0:T(8,128)(2,1)}, bf16[128,1280]{1,0:T(8,128)(2,1)S(1)}, u32[]{:S(2)}, u32[]{:S(2)}) collective-permute-start(bf16[128,1280]{1,0:T(8,128)(2,1)} %bitcast.31), channel_id=1, source_target_pairs={{0,2},{1,3},{2,0},{3,1},{4,6},{5,7},{6,4},{7,5},{8,10},{9,11},{10,... | collective-permute-start | bytes 983048 | tf_op jit(solution)/shard_map/ppermute | solution.py:41
  11.7 8.0 %collective-permute-start.5 = (bf16[128,1280]{1,0:T(8,128)(2,1)}, bf16[128,1280]{1,0:T(8,128)(2,1)S(1)}, u32[]{:S(2)}, u32[]{:S(2)}) collective-permute-start(bf16[128,1280]{1,0:T(8,128)(2,1)} %bitcast.32), channel_id=1, source_target_pairs={{0,3},{1,0},{2,1},{3,2},{4,7},{5,4},{6,5},{7,6},{8,11},{9,8},{10,9... | collective-permute-start | bytes 983048 | tf_op jit(solution)/shard_map/ppermute | solution.py:41
  16.8 7.8 %collective-permute-start.6 = (bf16[128,1280]{1,0:T(8,128)(2,1)}, bf16[128,1280]{1,0:T(8,128)(2,1)S(1)}, u32[]{:S(2)}, u32[]{:S(2)}) collective-permute-start(bf16[128,1280]{1,0:T(8,128)(2,1)} %bitcast.33), channel_id=1, source_target_pairs={{0,16},{16,0},{1,17},{17,1},{2,18},{18,2},{3,19},{19,3},{4,20},{20... | collective-permute-start | bytes 983048 | tf_op jit(solution)/shard_map/ppermute | solution.py:30
  29.2 32.7 %copy-start.16 = (bf16[128,1280]{1,0:T(8,128)(2,1)S(1)}, bf16[128,1280]{1,0:T(8,128)(2,1)}, u32[]{:S(2)}) copy-start(bf16[128,1280]{1,0:T(8,128)(2,1)} %copy-done.15) | copy-start | bytes 983044
  61.9 7.3 %collective-permute-start.9 = (bf16[128,1280]{1,0:T(8,128)(2,1)S(1)}, bf16[128,1280]{1,0:T(8,128)(2,1)S(1)}, u32[]{:S(2)}, u32[]{:S(2)}) collective-permute-start(bf16[128,1280]{1,0:T(8,128)(2,1)S(1)} %stack.39.refs_0_), channel_id=1, source_target_pairs={{0,1},{1,2},{2,3},{3,0},{4,5},{5,6},{6,7},{7,4},{8,9},{9,10},{10,1... | collective-permute-start | bytes 983048 | tf_op jit(solution)/shard_map/ppermute | solution.py:41
  62.0 11.6 %collective-permute-start.10 = (bf16[128,1280]{1,0:T(8,128)(2,1)S(1)}, bf16[128,1280]{1,0:T(8,128)(2,1)S(1)}, u32[]{:S(2)}, u32[]{:S(2)}) collective-permute-start(bf16[128,1280]{1,0:T(8,128)(2,1)S(1)} %stack.39.refs_0_), channel_id=1, source_target_pairs={{0,2},{1,3},{2,0},{3,1},{4,6},{5,7},{6,4},{7,5},{8,10},{9,11},{10,... | collective-permute-start | bytes 983048 | tf_op jit(solution)/shard_map/ppermute | solution.py:41
  65.7 8.0 %collective-permute-start.11 = (bf16[128,1280]{1,0:T(8,128)(2,1)S(1)}, bf16[128,1280]{1,0:T(8,128)(2,1)S(1)}, u32[]{:S(2)}, u32[]{:S(2)}) collective-permute-start(bf16[128,1280]{1,0:T(8,128)(2,1)S(1)} %stack.39.refs_0_), channel_id=1, source_target_pairs={{0,3},{1,0},{2,1},{3,2},{4,7},{5,4},{6,5},{7,6},{8,11},{9,8},{10,9... | collective-permute-start | bytes 983048 | tf_op jit(solution)/shard_map/ppermute | solution.py:41
  66.0 45.8 %collective-permute-start.8 = (bf16[256,4096]{1,0:T(8,128)(2,1)S(1)}, bf16[256,4096]{1,0:T(8,128)(2,1)}, u32[]{:S(2)}, u32[]{:S(2)}) collective-permute-start(bf16[256,4096]{1,0:T(8,128)(2,1)S(1)} %bitcast.24), channel_id=1, source_target_pairs={{0,64},{64,0},{1,65},{65,1},{2,66},{66,2},{3,67},{67,3},{4,68},{68... | collective-permute-start | bytes 6291464 | tf_op jit(solution)/shard_map/ppermute | solution.py:30
  67.1 26.9 %copy-start.6 = (bf16[512,1280]{1,0:T(8,128)(2,1)}, bf16[512,1280]{1,0:T(8,128)(2,1)S(1)}, u32[]{:S(2)}) copy-start(bf16[512,1280]{1,0:T(8,128)(2,1)S(1)} %stack.42.rest_0_) | copy-start | bytes 3932164
  67.1 25.0 %collective-permute-start.15 = (bf16[512,1280]{1,0:T(8,128)(2,1)S(1)}, bf16[512,1280]{1,0:T(8,128)(2,1)S(1)}, u32[]{:S(2)}, u32[]{:S(2)}) collective-permute-start(bf16[512,1280]{1,0:T(8,128)(2,1)S(1)} %stack.42.rest_0_), channel_id=1, source_target_pairs={{0,4},{1,5},{2,6},{3,7},{4,8},{5,9},{6,10},{7,11},{8,12},{9,13},{1... | collective-permute-start | bytes 3932168 | tf_op jit(solution)/shard_map/ppermute | solution.py:41
  69.2 23.9 %collective-permute-start.16 = (bf16[512,1280]{1,0:T(8,128)(2,1)S(1)}, bf16[512,1280]{1,0:T(8,128)(2,1)S(1)}, u32[]{:S(2)}, u32[]{:S(2)}) collective-permute-start(bf16[512,1280]{1,0:T(8,128)(2,1)S(1)} %stack.42.rest_0_), channel_id=1, source_target_pairs={{0,12},{1,13},{2,14},{3,15},{4,0},{5,1},{6,2},{7,3},{8,4},{9,5},{1... | collective-permute-start | bytes 3932168 | tf_op jit(solution)/shard_map/ppermute | solution.py:41
  73.8 34.2 %copy-start.8 = (bf16[512,1280]{1,0:T(8,128)(2,1)}, bf16[512,1280]{1,0:T(8,128)(2,1)S(1)}, u32[]{:S(2)}) copy-start(bf16[512,1280]{1,0:T(8,128)(2,1)S(1)} %stack.40.rest_5_) | copy-start | bytes 3932164
  73.8 32.4 %collective-permute-start.12 = (bf16[512,1280]{1,0:T(8,128)(2,1)S(1)}, bf16[512,1280]{1,0:T(8,128)(2,1)S(1)}, u32[]{:S(2)}, u32[]{:S(2)}) collective-permute-start(bf16[512,1280]{1,0:T(8,128)(2,1)S(1)} %stack.40.rest_5_), channel_id=1, source_target_pairs={{0,4},{1,5},{2,6},{3,7},{4,8},{5,9},{6,10},{7,11},{8,12},{9,13},{1... | collective-permute-start | bytes 3932168 | tf_op jit(solution)/shard_map/ppermute | solution.py:41
  74.9 32.1 %collective-permute-start.13 = (bf16[512,1280]{1,0:T(8,128)(2,1)S(1)}, bf16[512,1280]{1,0:T(8,128)(2,1)S(1)}, u32[]{:S(2)}, u32[]{:S(2)}) collective-permute-start(bf16[512,1280]{1,0:T(8,128)(2,1)S(1)} %stack.40.rest_5_), channel_id=1, source_target_pairs={{0,12},{1,13},{2,14},{3,15},{4,0},{5,1},{6,2},{7,3},{8,4},{9,5},{1... | collective-permute-start | bytes 3932168 | tf_op jit(solution)/shard_map/ppermute | solution.py:41
  92.1 15.9 %copy-start.11 = (bf16[512,1280]{1,0:T(8,128)(2,1)}, bf16[512,1280]{1,0:T(8,128)(2,1)S(1)}, u32[]{:S(2)}) copy-start(bf16[512,1280]{1,0:T(8,128)(2,1)S(1)} %collective-permute-done.15.rest_1_) | copy-start | bytes 3932164
  93.1 28.1 %collective-permute-start.17 = (bf16[256,1280]{1,0:T(8,128)(2,1)}, bf16[256,1280]{1,0:T(8,128)(2,1)}, u32[]{:S(2)}, u32[]{:S(2)}) collective-permute-start(bf16[256,1280]{1,0:T(8,128)(2,1)} %slice.71), channel_id=1, source_target_pairs={{0,4},{1,5},{2,6},{3,7},{4,8},{5,9},{6,10},{7,11},{8,12},{9,13},{1... | collective-permute-start | bytes 1966088 | tf_op jit(solution)/shard_map/ppermute | solution.py:41
  93.1 14.9 %copy-start.13 = (bf16[512,1280]{1,0:T(8,128)(2,1)}, bf16[512,1280]{1,0:T(8,128)(2,1)S(1)}, u32[]{:S(2)}) copy-start(bf16[512,1280]{1,0:T(8,128)(2,1)S(1)} %collective-permute-done.16.rest_2_) | copy-start | bytes 3932164
  94.0 27.1 %collective-permute-start.18 = (bf16[256,1280]{1,0:T(8,128)(2,1)}, bf16[256,1280]{1,0:T(8,128)(2,1)}, u32[]{:S(2)}, u32[]{:S(2)}) collective-permute-start(bf16[256,1280]{1,0:T(8,128)(2,1)} %slice.72), channel_id=1, source_target_pairs={{0,12},{1,13},{2,14},{3,15},{4,0},{5,1},{6,2},{7,3},{8,4},{9,5},{1... | collective-permute-start | bytes 1966088 | tf_op jit(solution)/shard_map/ppermute | solution.py:41
  107.0 14.1 %collective-permute-start.19 = (bf16[256,1280]{1,0:T(8,128)(2,1)}, bf16[256,1280]{1,0:T(8,128)(2,1)}, u32[]{:S(2)}, u32[]{:S(2)}) collective-permute-start(bf16[256,1280]{1,0:T(8,128)(2,1)} %slice.73), channel_id=1, source_target_pairs={{0,4},{1,5},{2,6},{3,7},{4,8},{5,9},{6,10},{7,11},{8,12},{9,13},{1... | collective-permute-start | bytes 1966088 | tf_op jit(solution)/shard_map/ppermute | solution.py:41
  109.1 12.1 %collective-permute-start.20 = (bf16[256,1280]{1,0:T(8,128)(2,1)}, bf16[256,1280]{1,0:T(8,128)(2,1)}, u32[]{:S(2)}, u32[]{:S(2)}) collective-permute-start(bf16[256,1280]{1,0:T(8,128)(2,1)} %slice.74), channel_id=1, source_target_pairs={{0,12},{1,13},{2,14},{3,15},{4,0},{5,1},{6,2},{7,3},{8,4},{9,5},{1... | collective-permute-start | bytes 1966088 | tf_op jit(solution)/shard_map/ppermute | solution.py:41
  111.7 35.1 %collective-permute-start.7 = (bf16[256,4096]{1,0:T(8,128)(2,1)S(1)}, bf16[256,4096]{1,0:T(8,128)(2,1)}, u32[]{:S(2)}, u32[]{:S(2)}) collective-permute-start(bf16[256,4096]{1,0:T(8,128)(2,1)S(1)} %bitcast.26), channel_id=1, source_target_pairs={{0,32},{32,0},{1,33},{33,1},{2,34},{34,2},{3,35},{35,3},{4,36},{36... | collective-permute-start | bytes 6291464 | tf_op jit(solution)/shard_map/ppermute | solution.py:30
  121.2 30.4 %collective-permute-start.14 = (bf16[256,4096]{1,0:T(8,128)(2,1)}, bf16[256,4096]{1,0:T(8,128)(2,1)}, u32[]{:S(2)}, u32[]{:S(2)}) collective-permute-start(bf16[256,4096]{1,0:T(8,128)(2,1)} %stack.41.xa_ref.refs_2_), channel_id=1, source_target_pairs={{0,32},{32,0},{1,33},{33,1},{2,34},{34,2},{3,35},{35,3},{4,36},{36... | collective-permute-start | bytes 6291464 | tf_op jit(solution)/shard_map/ppermute | solution.py:30
  122.0 9.9 %collective-permute-start.21 = (bf16[256,1024]{1,0:T(8,128)(2,1)}, bf16[256,1024]{1,0:T(8,128)(2,1)}, u32[]{:S(2)}, u32[]{:S(2)}) collective-permute-start(bf16[256,1024]{1,0:T(8,128)(2,1)} %stack.43.refs_0_), channel_id=1, source_target_pairs={{0,1},{1,2},{2,3},{3,0},{4,5},{5,6},{6,7},{7,4},{8,9},{9,10},{10,1... | collective-permute-start | bytes 1572872 | tf_op jit(solution)/shard_map/ppermute | solution.py:41
  122.1 15.7 %collective-permute-start.22 = (bf16[256,1024]{1,0:T(8,128)(2,1)}, bf16[256,1024]{1,0:T(8,128)(2,1)}, u32[]{:S(2)}, u32[]{:S(2)}) collective-permute-start(bf16[256,1024]{1,0:T(8,128)(2,1)} %stack.43.refs_0_), channel_id=1, source_target_pairs={{0,2},{1,3},{2,0},{3,1},{4,6},{5,7},{6,4},{7,5},{8,10},{9,11},{10,... | collective-permute-start | bytes 1572872 | tf_op jit(solution)/shard_map/ppermute | solution.py:41
  125.0 13.1 %collective-permute-start.23 = (bf16[256,1024]{1,0:T(8,128)(2,1)}, bf16[256,1024]{1,0:T(8,128)(2,1)}, u32[]{:S(2)}, u32[]{:S(2)}) collective-permute-start(bf16[256,1024]{1,0:T(8,128)(2,1)} %stack.43.refs_0_), channel_id=1, source_target_pairs={{0,3},{1,0},{2,1},{3,2},{4,7},{5,4},{6,5},{7,6},{8,11},{9,8},{10,9... | collective-permute-start | bytes 1572872 | tf_op jit(solution)/shard_map/ppermute | solution.py:41
  125.8 18.1 %copy-start.23 = (s32[4,32]{1,0:T(4,128)S(1)}, s32[4,32]{1,0:T(4,128)}, u32[]{:S(2)}) copy-start(s32[4,32]{1,0:T(4,128)} %param.9) | copy-start | bytes 1540
  125.8 18.1 %copy-start.24 = (s32[4,32]{1,0:T(4,128)S(1)}, s32[4,32]{1,0:T(4,128)}, u32[]{:S(2)}) copy-start(s32[4,32]{1,0:T(4,128)} %param.10) | copy-start | bytes 1540
  125.8 18.2 %copy-start.22 = (s32[4,32,256]{2,1,0:T(8,128)S(1)}, s32[4,32,256]{2,1,0:T(8,128)}, u32[]{:S(2)}) copy-start(s32[4,32,256]{2,1,0:T(8,128)} %param.11) | copy-start | bytes 393220
  125.8 21.0 %copy-start.20 = (f32[4096]{0:T(1024)S(1)}, f32[4096]{0:T(1024)}, u32[]{:S(2)}) copy-start(f32[4096]{0:T(1024)} %param.12) | copy-start | bytes 49156
  141.2 29.7 %collective-permute-start.24 = (bf16[1024,1024]{1,0:T(8,128)(2,1)}, bf16[1024,1024]{1,0:T(8,128)(2,1)}, u32[]{:S(2)}, u32[]{:S(2)}) collective-permute-start(bf16[1024,1024]{1,0:T(8,128)(2,1)} %stack.44.refs_1_), channel_id=1, source_target_pairs={{0,4},{1,5},{2,6},{3,7},{4,8},{5,9},{6,10},{7,11},{8,12},{9,13},{1... | collective-permute-start | bytes 6291464 | tf_op jit(solution)/shard_map/ppermute | solution.py:41
  142.3 30.8 %collective-permute-start.25 = (bf16[1024,1024]{1,0:T(8,128)(2,1)}, bf16[1024,1024]{1,0:T(8,128)(2,1)}, u32[]{:S(2)}, u32[]{:S(2)}) collective-permute-start(bf16[1024,1024]{1,0:T(8,128)(2,1)} %stack.44.refs_1_), channel_id=1, source_target_pairs={{0,12},{1,13},{2,14},{3,15},{4,0},{5,1},{6,2},{7,3},{8,4},{9,5},{1... | collective-permute-start | bytes 6291464 | tf_op jit(solution)/shard_map/ppermute | solution.py:41
  151.5 5.5 %copy-start.4 = (bf16[512,1280]{1,0:T(8,128)(2,1)S(1)}, bf16[512,1280]{1,0:T(8,128)(2,1)}, u32[]{:S(2)}) copy-start(bf16[512,1280]{1,0:T(8,128)(2,1)} %copy-done.2) | copy-start | bytes 3932164
  151.5 5.5 %copy-start.7 = (bf16[512,1280]{1,0:T(8,128)(2,1)S(1)}, bf16[512,1280]{1,0:T(8,128)(2,1)}, u32[]{:S(2)}) copy-start(bf16[512,1280]{1,0:T(8,128)(2,1)} %copy-done.6) | copy-start | bytes 3932164
  169.2 8.9 %copy-start.17 = (s32[2,256,1]{2,1,0:T(8,128)S(1)}, s32[2,256,1]{2,1,0:T(8,128)}, u32[]{:S(2)}) copy-start(s32[2,256,1]{2,1,0:T(8,128)} %copy.16.segq_ref) | copy-start | bytes 6148
  169.2 47.2 %collective-permute-start.27 = (bf16[512,1024]{1,0:T(8,128)(2,1)}, bf16[512,1024]{1,0:T(8,128)(2,1)}, u32[]{:S(2)}, u32[]{:S(2)}) collective-permute-start(bf16[512,1024]{1,0:T(8,128)(2,1)} %attend.3.mixed_b_ref), channel_id=1, source_target_pairs={{0,64},{64,0},{1,65},{65,1},{2,66},{66,2},{3,67},{67,3},{4,68},{68... | collective-permute-start | bytes 3145736 | tf_op jit(solution)/shard_map/ppermute | solution.py:30
  173.1 18.9 %collective-permute-start.26 = (bf16[512,1024]{1,0:T(8,128)(2,1)}, bf16[512,1024]{1,0:T(8,128)(2,1)}, u32[]{:S(2)}, u32[]{:S(2)}) collective-permute-start(bf16[512,1024]{1,0:T(8,128)(2,1)} %slice.76), channel_id=1, source_target_pairs={{0,4},{1,5},{2,6},{3,7},{4,8},{5,9},{6,10},{7,11},{8,12},{9,13},{1... | collective-permute-start | bytes 3145736 | tf_op jit(solution)/shard_map/ppermute | solution.py:41
  175.4 16.3 %copy-start.21 = (f32[4096]{0:T(1024)S(1)}, f32[4096]{0:T(1024)}, u32[]{:S(2)}) copy-start(f32[4096]{0:T(1024)} %param.15) | copy-start | bytes 49156
  175.4 36.5 %collective-permute-start.29 = (bf16[512,1024]{1,0:T(8,128)(2,1)}, bf16[512,1024]{1,0:T(8,128)(2,1)}, u32[]{:S(2)}, u32[]{:S(2)}) collective-permute-start(bf16[512,1024]{1,0:T(8,128)(2,1)} %slice.77), channel_id=1, source_target_pairs={{0,12},{1,13},{2,14},{3,15},{4,0},{5,1},{6,2},{7,3},{8,4},{9,5},{1... | collective-permute-start | bytes 3145736 | tf_op jit(solution)/shard_map/ppermute | solution.py:41
  190.2 26.2 %collective-permute-start.28 = (bf16[512,1024]{1,0:T(8,128)(2,1)}, bf16[512,1024]{1,0:T(8,128)(2,1)S(1)}, u32[]{:S(2)}, u32[]{:S(2)}) collective-permute-start(bf16[512,1024]{1,0:T(8,128)(2,1)} %attend.2.mixed_a_ref), channel_id=1, source_target_pairs={{0,64},{64,0},{1,65},{65,1},{2,66},{66,2},{3,67},{67,3},{4,68},{68... | collective-permute-start | bytes 3145736 | tf_op jit(solution)/shard_map/ppermute | solution.py:30
  204.6 27.7 %collective-permute-start.30 = (bf16[1024,1024]{1,0:T(8,128)(2,1)S(1)}, bf16[1024,1024]{1,0:T(8,128)(2,1)S(1)}, u32[]{:S(2)}, u32[]{:S(2)}) collective-permute-start(bf16[1024,1024]{1,0:T(8,128)(2,1)S(1)} %get-tuple-element.10), channel_id=1, source_target_pairs={{0,32},{32,0},{1,33},{33,1},{2,34},{34,2},{3,35},{35,3},{4,36},{36... | collective-permute-start | bytes 6291464 | tf_op jit(solution)/shard_map/ppermute | solution.py:30
  224.2 8.1 %collective-permute-start.31 = (bf16[1024,1024]{1,0:T(8,128)(2,1)S(1)}, bf16[1024,1024]{1,0:T(8,128)(2,1)S(1)}, u32[]{:S(2)}, u32[]{:S(2)}) collective-permute-start(bf16[1024,1024]{1,0:T(8,128)(2,1)S(1)} %get-tuple-element.11), channel_id=1, source_target_pairs={{0,32},{32,0},{1,33},{33,1},{2,34},{34,2},{3,35},{35,3},{4,36},{36... | collective-permute-start | bytes 6291464 | tf_op jit(solution)/shard_map/ppermute | solution.py:30
  227.9 2.7 %collective-permute-start.32 = (f32[1,128]{1,0:T(1,128)S(1)}, f32[1,128]{1,0:T(1,128)S(1)}, u32[]{:S(2)}, u32[]{:S(2)}) collective-permute-start(f32[1,128]{1,0:T(1,128)S(1)} %add_add_fusion), channel_id=1, source_target_pairs={{0,32},{32,0},{1,33},{33,1},{2,34},{34,2},{3,35},{35,3},{4,36},{36... | collective-permute-start | bytes 1544 | tf_op jit(solution)/shard_map/ppermute | solution.py:30
  230.6 7.2 %collective-permute-start.33 = (f32[1,128]{1,0:T(1,128)S(1)}, f32[1,128]{1,0:T(1,128)S(1)}, u32[]{:S(2)}, u32[]{:S(2)}) collective-permute-start(f32[1,128]{1,0:T(1,128)S(1)} %add.86), channel_id=1, source_target_pairs={{0,64},{64,0},{1,65},{65,1},{2,66},{66,2},{3,67},{67,3},{4,68},{68... | collective-permute-start | bytes 1544 | tf_op jit(solution)/shard_map/ppermute | solution.py:30
  (11 other events, 35.9 us)

commit v4 on v3

--- a/solution.py
+++ b/solution.py
@@ -402,8 +402,6 @@
         plane_gather_first(stack([w_peer], [(0, 0, BLK)], own_record), 1)
     )
     qkv_pieces = own_pieces + peer_pieces
-    o_both = stack([o_both], [(0, 0, 2 * BLK)], peer_pieces[3:] + own_pieces[3:])
-    out_pieces = plane_gather_second(plane_gather_first(o_both, 2))
 
     far_record = stack([swap_xh(own_record)], [(0, 0, RECLEN)], peer_pieces[1:3])
     far_peer_record = swap_co(far_record)
@@ -445,6 +443,8 @@
     gain = norm_gain[None, :]
     normed_a = normalize(qkv_offs, slots[0], slots[1], gain)
     normed_b = normalize(qkv_offs, slots[2], slots[3], gain)
+    o_both = stack([o_both], [(0, 0, 2 * BLK)], peer_pieces[3:] + own_pieces[3:] + [normed_a])
+    out_pieces = plane_gather_second(plane_gather_first(o_both, 2))
     mixed_a = attend(normed_a, cosine, sine, segq[:2], segk[:2], qkv_pieces, [normed_b])
     mixed_b = attend(normed_b, cosine, sine, segq[2:], segk[2:], qkv_pieces)
     far_b = swap_xh(mixed_a)

time: 241 us -> 247 us (1.025)
  Pallas kernels: 76.9 us -> 80.6 us
  waiting for transfers between devices: 53 us -> 56 us
    pallas_call x2, Pallas kernels: 24.2 us -> 28.2 us  [attend(): pl.pallas_call(attend_kernel, out_shape=jax.ShapeDtypeStruct((2 * RECLEN,...]
    ppermute x21, waiting for transfers between devices: 41.5 us -> 44.4 us  [plane_perm(): return lambda v: lax.ppermute(v, CORE_ZY, pairs)]
    unnamed x50 -> x30, local copies, waits for them, and re-layouts: 5.74 us -> 3.32 us
  transfers between devices with their start and end apart: 34 -> 34, of which waited for: 11 -> 13; matrix products, arithmetic and copies ran while one was open for 6% -> 8% of each run, Pallas kernels for 30% -> 31%
where the time goes in v4:
time: 247 us
  Pallas kernels  80.6 us (33%)
  waiting for transfers between devices  56 us (23%)
  starting transfers between devices  53.1 us (21%)
  blocking collectives  32.7 us (13%)
  local copies, waits for them, and re-layouts  17.9 us (7%)
  other arithmetic  5.39 us (2%)
    ppermute x21, waiting for transfers between devices, plane_perm(): return lambda v: lax.ppermute(v, CORE_ZY, pairs)  44.4 us
    all_to_all x1, blocking collectives, on_device(): lax.all_to_all(send_block, ('xl', 'z', 'y'), split_axis=0, concat_axis=0,...  32.7 us
    ppermute x21, starting transfers between devices, plane_perm(): return lambda v: lax.ppermute(v, CORE_ZY, pairs)  28.6 us
    pallas_call x2, Pallas kernels, attend(): pl.pallas_call(attend_kernel, out_shape=jax.ShapeDtypeStruct((2 * RECLEN,...  28.2 us
    ppermute x11, starting transfers between devices, ring(): lax.ppermute(v, axis, [(i, (i + step) % size) for i in range(size)])  22 us
    pallas_call x2, Pallas kernels, project(): pl.pallas_call(project_kernel, out_shape=[jax.ShapeDtypeStruct((4 * RECLE...  16 us
    pallas_call x2, Pallas kernels, normalize(): pl.pallas_call(normalize_kernel, out_shape=jax.ShapeDtypeStruct((2 * RECL...  10 us
    pallas_call x2, Pallas kernels, arrange(): pl.pallas_call(lambda *refs: arrange_kernel(head, *refs), out_shape=jax.S...  8.87 us
  transfers between devices with their start and end apart: 34, of which 13 were waited for; matrix products, arithmetic and copies ran while one was open for 8% of the time, Pallas kernels for 31%

profile of v4, /device:TPU:1, one launch (start us, length us, event | category | flops | bytes accessed | tf_op | source)
XLA Modules:
  0.0 246.6 jit_solution(9129497831615691207)
XLA Ops:
  0.6 2.1 collective-permute-start
  2.8 2.5 collective-permute-start.1
  5.2 1.8 collective-permute-start.3
  7.0 3.3 %collective-permute-start.4 = (bf16[128,1280]{1,0:T(8,128)(2,1)}, bf16[128,1280]{1,0:T(8,128)(2,1)S(1)}, u32[]{:S(2)}, u32[]{:S(2)}) collective-permute-start(bf16[128,1280]{1,0:T(8,128)(2,1)} %bitcast.31), channel_id=1, source_target_pairs={{0,2},{1,3},{2,0},{3,1},{4,6},{5,7},{6,4},{7,5},{8,10},{9,11},{10,... | collective-permute-start | bytes 983048 | tf_op jit(solution)/shard_map/ppermute | solution.py:41
  13.7 3.1 %collective-permute-done.1 = bf16[128,1024]{1,0:T(8,128)(2,1)S(1)} collective-permute-done((bf16[128,1024]{1,0:T(8,128)(2,1)}, bf16[128,1024]{1,0:T(8,128)(2,1)S(1)}, u32[]{:S(2)}, u32[]{:S(2)}) %collective-permute-start.1) | collective-permute-done | bytes 262176 | tf_op jit(solution)/shard_map/ppermute | solution.py:379
  16.8 2.0 collective-permute-done.2
  20.8 3.8 %collective-permute-done.6.rest_2_.refs_0_ = bf16[128,1280]{1,0:T(8,128)(2,1)S(1)} collective-permute-done((bf16[128,1280]{1,0:T(8,128)(2,1)}, bf16[128,1280]{1,0:T(8,128)(2,1)S(1)}, u32[]{:S(2)}, u32[]{:S(2)}) %collective-permute-start.6) | collective-permute-done | bytes 327712 | tf_op jit(solution)/shard_map/ppermute | solution.py:30
  25.3 3.8 %order_records.1 = bf16[32,8,4096]{2,1,0:T(8,128)(2,1)} custom-call(s32[32]{0:T(128)} %select_reduce_fusion.2.outgoing_ref, bf16[32,8,4096]{2,1,0:T(8,128)(2,1)} %bitcast.38, bf16[256,1024]{1,0:T(8,128)(2,1)} %pad_maximum_fusion.rest_0_.refs_0_, bf16[512,1280]{1,0:T(8,128)(2,1)} %copy-done.2, bf16[128,1280]{1,0:T(8,128)(2,1)} %copy-done.6), custom_call_target="tpu_custom_call" | custom-call | bytes 4194304 | tf_op jit(solution)/shard_map/order_records/pallas_call | solution.py:97
  29.2 32.7 %all_to_all.5 = bf16[32,8,4096]{2,1,0:T(8,128)(2,1)S(1)} all-to-all(bf16[32,8,4096]{2,1,0:T(8,128)(2,1)} %order_records.1), channel_id=1, replica_groups=mesh['xh'=2,'co'=2,'xl'=2,'z'=4,'y'=4] {'xl','z','y'}, dimensions={0} | all-to-all | bytes 4194304 | tf_op jit(solution)/shard_map/all_to_all | solution.py:394
  63.1 1.2 collective-permute-start.15
  64.3 3.9 %collective-permute-start.7 = (bf16[256,4096]{1,0:T(8,128)(2,1)S(1)}, bf16[256,4096]{1,0:T(8,128)(2,1)}, u32[]{:S(2)}, u32[]{:S(2)}) collective-permute-start(bf16[256,4096]{1,0:T(8,128)(2,1)S(1)} %bitcast.24), channel_id=1, source_target_pairs={{0,32},{32,0},{1,33},{33,1},{2,34},{34,2},{3,35},{35,3},{4,36},{36... | collective-permute-start | bytes 6291464 | tf_op jit(solution)/shard_map/ppermute | solution.py:30
  69.0 2.9 %collective-permute-start.10 = (bf16[128,1280]{1,0:T(8,128)(2,1)S(1)}, bf16[128,1280]{1,0:T(8,128)(2,1)S(1)}, u32[]{:S(2)}, u32[]{:S(2)}) collective-permute-start(bf16[128,1280]{1,0:T(8,128)(2,1)S(1)} %stack.39.refs_0_), channel_id=1, source_target_pairs={{0,2},{1,3},{2,0},{3,1},{4,6},{5,7},{6,4},{7,5},{8,10},{9,11},{10,... | collective-permute-start | bytes 983048 | tf_op jit(solution)/shard_map/ppermute | solution.py:41
  71.8 1.3 collective-permute-start.11
  73.1 6.2 %collective-permute-done.9.refs_1_ = bf16[128,1280]{1,0:T(8,128)(2,1)S(1)} collective-permute-done((bf16[128,1280]{1,0:T(8,128)(2,1)S(1)}, bf16[128,1280]{1,0:T(8,128)(2,1)S(1)}, u32[]{:S(2)}, u32[]{:S(2)}) %collective-permute-start.9) | collective-permute-done | bytes 327712 | tf_op jit(solution)/shard_map/ppermute | solution.py:41
  80.4 6.7 %collective-permute-done.10.refs_2_ = bf16[128,1280]{1,0:T(8,128)(2,1)S(1)} collective-permute-done((bf16[128,1280]{1,0:T(8,128)(2,1)S(1)}, bf16[128,1280]{1,0:T(8,128)(2,1)S(1)}, u32[]{:S(2)}, u32[]{:S(2)}) %collective-permute-start.10) | collective-permute-done | bytes 327712 | tf_op jit(solution)/shard_map/ppermute | solution.py:41
  89.8 2.4 collective-permute-start.13
  92.2 2.0 slice.71
  94.2 10.1 %collective-permute-done.16.rest_2_ = bf16[512,1280]{1,0:T(8,128)(2,1)} collective-permute-done((bf16[512,1280]{1,0:T(8,128)(2,1)}, bf16[512,1280]{1,0:T(8,128)(2,1)}, u32[]{:S(2)}, u32[]{:S(2)}) %collective-permute-start.16) | collective-permute-done | bytes 1310752 | tf_op jit(solution)/shard_map/ppermute | solution.py:41
  104.8 2.0 slice.72
  109.8 8.5 %collective-permute-done.13.refs_2_.rest_7_ = bf16[512,1280]{1,0:T(8,128)(2,1)} collective-permute-done((bf16[512,1280]{1,0:T(8,128)(2,1)}, bf16[512,1280]{1,0:T(8,128)(2,1)}, u32[]{:S(2)}, u32[]{:S(2)}) %collective-permute-start.13) | collective-permute-done | bytes 1310752 | tf_op jit(solution)/shard_map/ppermute | solution.py:41
  118.9 2.0 slice.74
  120.9 2.1 collective-permute-start.20
  123.5 4.7 %normalize.2.normed_ref.refs_5_ = bf16[512,4096]{1,0:T(8,128)(2,1)S(1)} custom-call(s32[32]{0:T(128)S(1)} %pad_add_fusion.2.offs_ref, bf16[256,4096]{1,0:T(8,128)(2,1)S(1)} %bitcast.27, bf16[256,4096]{1,0:T(8,128)(2,1)} %collective-permute-done.7.xb_ref.refs_1_, f32[1,4096]{1,0:T(1,128)S(1)} %bitcast.35), custom_call_target="tpu_custom_call" | custom-call | flops 4194304 | bytes 12582912 | tf_op jit(solution)/shard_map/normalize/pallas_call | solution.py:127
  128.3 1.3 collective-permute-done.19.rest_8_.refs_1_
  129.5 2.8 %collective-permute-done.20.rest_9_.refs_2_ = bf16[256,1280]{1,0:T(8,128)(2,1)} collective-permute-done((bf16[256,1280]{1,0:T(8,128)(2,1)}, bf16[256,1280]{1,0:T(8,128)(2,1)}, u32[]{:S(2)}, u32[]{:S(2)}) %collective-permute-start.20) | collective-permute-done | bytes 655392 | tf_op jit(solution)/shard_map/ppermute | solution.py:41
  132.6 2.6 %collective-permute-start.23 = (bf16[256,1024]{1,0:T(8,128)(2,1)S(1)}, bf16[256,1024]{1,0:T(8,128)(2,1)S(1)}, u32[]{:S(2)}, u32[]{:S(2)}) collective-permute-start(bf16[256,1024]{1,0:T(8,128)(2,1)S(1)} %stack.43.refs_0_), channel_id=1, source_target_pairs={{0,3},{1,0},{2,1},{3,2},{4,7},{5,4},{6,5},{7,6},{8,11},{9,8},{10,9... | collective-permute-start | bytes 1572872 | tf_op jit(solution)/shard_map/ppermute | solution.py:41
  135.1 3.1 %stack.41.xa_ref.refs_2_ = bf16[256,4096]{1,0:T(8,128)(2,1)} custom-call(bf16[256,4096]{1,0:T(8,128)(2,1)} %collective-permute-done.8.refs_0_, bf16[512,1280]{1,0:T(8,128)(2,1)S(1)} %collective-permute-done.12.refs_1_.rest_6_, bf16[512,1280]{1,0:T(8,128)(2,1)} %collective-permute-done.13.refs_2_.rest_7_), custom_call_target="tpu_custom_call" | custom-call | bytes 1048576 | tf_op jit(solution)/shard_map/stack/pallas_call | solution.py:55
  138.3 2.1 collective-permute-start.14
  140.3 7.3 %collective-permute-done.21.refs_1_ = bf16[256,1024]{1,0:T(8,128)(2,1)S(1)} collective-permute-done((bf16[256,1024]{1,0:T(8,128)(2,1)S(1)}, bf16[256,1024]{1,0:T(8,128)(2,1)S(1)}, u32[]{:S(2)}, u32[]{:S(2)}) %collective-permute-start.21) | collective-permute-done | bytes 524320 | tf_op jit(solution)/shard_map/ppermute | solution.py:41
  148.2 1.5 stack.44.refs_1_
  150.0 2.4 collective-permute-start.25
  156.2 5.3 %normalize.3.rest_10_.normed_ref = bf16[512,4096]{1,0:T(8,128)(2,1)S(1)} custom-call(s32[32]{0:T(128)S(1)} %pad_add_fusion.2.offs_ref, bf16[256,4096]{1,0:T(8,128)(2,1)} %stack.41.xa_ref.refs_2_, bf16[256,4096]{1,0:T(8,128)(2,1)} %collective-permute-done.14.xb_ref.refs_3_, f32[1,4096]{1,0:T(1,128)S(1)} %bitcast.36), custom_call_target="tpu_custom_call" | custom-call | flops 4194304 | bytes 12582912 | tf_op jit(solution)/shard_map/normalize/pallas_call | solution.py:127
  161.5 14.2 %attend.3.mixed_b_ref = bf16[512,1024]{1,0:T(8,128)(2,1)} custom-call(bf16[512,4096]{1,0:T(8,128)(2,1)S(1)} %normalize.3.rest_10_.normed_ref, f32[256,128]{1,0:T(8,128)S(1)} %get-tuple-element.38.cos_ref, f32[256,128]{1,0:T(8,128)S(1)} %get-tuple-element.39.sin_ref, s32[2,256,1]{2,1,0:T(8,128)S(1)} %copy-done.10, s32[2,1,256]{2,1,0:T(1,128)S(1)} %slice.66.segk_ref, ...), custom_call_target="tpu_custom_call" | custom-call | flops 5368709120 | bytes 16777216 | tf_op jit(solution)/shard_map/attend/pallas_call | solution.py:192
  176.4 2.3 slice.76
  178.7 2.3 slice.77
  181.0 2.7 %collective-permute-start.29 = (bf16[512,1024]{1,0:T(8,128)(2,1)}, bf16[512,1024]{1,0:T(8,128)(2,1)}, u32[]{:S(2)}, u32[]{:S(2)}) collective-permute-start(bf16[512,1024]{1,0:T(8,128)(2,1)} %slice.77), channel_id=1, source_target_pairs={{0,12},{1,13},{2,14},{3,15},{4,0},{5,1},{6,2},{7,3},{8,4},{9,5},{1... | collective-permute-start | bytes 3145736 | tf_op jit(solution)/shard_map/ppermute | solution.py:41
  183.7 14.1 %attend.2.mixed_a_ref = bf16[512,1024]{1,0:T(8,128)(2,1)} custom-call(bf16[512,4096]{1,0:T(8,128)(2,1)S(1)} %copy-done.1, f32[256,128]{1,0:T(8,128)S(1)} %get-tuple-element.38.cos_ref, f32[256,128]{1,0:T(8,128)S(1)} %get-tuple-element.39.sin_ref, s32[2,256,1]{2,1,0:T(8,128)S(1)} %copy-done.8, s32[2,1,256]{2,1,0:T(1,128)S(1)} %slice.59.segk_ref, ...), custom_call_target="tpu_custom_call" | custom-call | flops 5368709120 | bytes 16777216 | tf_op jit(solution)/shard_map/attend/pallas_call | solution.py:192
  197.8 2.3 collective-permute-start.28
  200.5 4.4 %arrange_0.1.w_ref = bf16[1024,2048]{1,0:T(8,128)(2,1)S(1)} custom-call(s32[16]{0:T(128)S(1)} %fusion.6.refs_0_, bf16[1024,1024]{1,0:T(8,128)(2,1)} %stack.44.refs_1_, bf16[1024,1024]{1,0:T(8,128)(2,1)} %collective-permute-done.24.refs_2_, bf16[1024,1024]{1,0:T(8,128)(2,1)} %collective-permute-done.25.refs_3_, bf16[512,1024]{1,0:T(8,128)(2,1)} %collective-permute-done.26.refs_4_), custom_call_target="tpu_custom_call" | custom-call | bytes 8388608 | tf_op jit(solution)/shard_map/arrange_0/pallas_call | solution.py:231
  205.0 8.2 %project.2 = (bf16[1024,1024]{1,0:T(8,128)(2,1)S(1)}, bf16[1024,1024]{1,0:T(8,128)(2,1)S(1)}, f32[1,128]{1,0:T(1,128)S(1)}) custom-call(bf16[512,1024]{1,0:T(8,128)(2,1)} %attend.2.mixed_a_ref, bf16[512,1024]{1,0:T(8,128)(2,1)} %attend.3.mixed_b_ref, bf16[1024,2048]{1,0:T(8,128)(2,1)S(1)} %arrange_0.1.w_ref, s32[13]{0:T(128)S(1)} %concatenate.16.meta_ref, ...), custom_call_target="tpu_custom_call" | custom-call | flops 4294967296 | bytes 2097152 | tf_op jit(solution)/shard_map/project/pallas_call | solution.py:274
  213.1 4.1 %collective-permute-start.30 = (bf16[1024,1024]{1,0:T(8,128)(2,1)S(1)}, bf16[1024,1024]{1,0:T(8,128)(2,1)S(1)}, u32[]{:S(2)}, u32[]{:S(2)}) collective-permute-start(bf16[1024,1024]{1,0:T(8,128)(2,1)S(1)} %get-tuple-element.10), channel_id=1, source_target_pairs={{0,32},{32,0},{1,33},{33,1},{2,34},{34,2},{3,35},{35,3},{4,36},{36... | collective-permute-start | bytes 6291464 | tf_op jit(solution)/shard_map/ppermute | solution.py:30
  217.2 4.4 %arrange_1.1.w_ref = bf16[1024,2048]{1,0:T(8,128)(2,1)S(1)} custom-call(s32[16]{0:T(128)S(1)} %fusion.6.refs_0_, bf16[1024,1024]{1,0:T(8,128)(2,1)} %stack.44.refs_1_, bf16[1024,1024]{1,0:T(8,128)(2,1)} %collective-permute-done.24.refs_2_, bf16[1024,1024]{1,0:T(8,128)(2,1)} %collective-permute-done.25.refs_3_, bf16[512,1024]{1,0:T(8,128)(2,1)} %collective-permute-done.29.refs_4_), custom_call_target="tpu_custom_call" | custom-call | bytes 8388608 | tf_op jit(solution)/shard_map/arrange_1/pallas_call | solution.py:231
  221.7 7.8 %project.3 = (bf16[1024,1024]{1,0:T(8,128)(2,1)S(1)}, bf16[1024,1024]{1,0:T(8,128)(2,1)S(1)}, f32[1,128]{1,0:T(1,128)S(1)}) custom-call(bf16[512,1024]{1,0:T(8,128)(2,1)} %collective-permute-done.27.mixed_a_ref, bf16[512,1024]{1,0:T(8,128)(2,1)S(1)} %collective-permute-done.28.mixed_b_ref, bf16[1024,2048]{1,0:T(8,128)(2,1)S(1)} %arrange_1.1.w_ref, ...), custom_call_target="tpu_custom_call" | custom-call | flops 4294967296 | bytes 2097152 | tf_op jit(solution)/shard_map/project/pallas_call | solution.py:274
  229.5 3.9 %collective-permute-start.31 = (bf16[1024,1024]{1,0:T(8,128)(2,1)S(1)}, bf16[1024,1024]{1,0:T(8,128)(2,1)S(1)}, u32[]{:S(2)}, u32[]{:S(2)}) collective-permute-start(bf16[1024,1024]{1,0:T(8,128)(2,1)S(1)} %get-tuple-element.11), channel_id=1, source_target_pairs={{0,32},{32,0},{1,33},{33,1},{2,34},{34,2},{3,35},{35,3},{4,36},{36... | collective-permute-start | bytes 6291464 | tf_op jit(solution)/shard_map/ppermute | solution.py:30
  234.5 2.6 %collective-permute-done.32 = f32[1,128]{1,0:T(1,128)S(1)} collective-permute-done((f32[1,128]{1,0:T(1,128)S(1)}, f32[1,128]{1,0:T(1,128)S(1)}, u32[]{:S(2)}, u32[]{:S(2)}) %collective-permute-start.32) | collective-permute-done | bytes 544 | tf_op jit(solution)/shard_map/ppermute | solution.py:30
  237.2 1.8 collective-permute-start.33
  239.0 5.5 %finish.1.refs_1_ = bf16[896,1024]{1,0:T(8,128)(2,1)} custom-call(s32[13]{0:T(128)S(1)} %concatenate.16.meta_ref, bf16[256,4096]{1,0:T(8,128)(2,1)S(1)} %bitcast.29, bf16[256,4096]{1,0:T(8,128)(2,1)} %collective-permute-done.7.xb_ref.refs_1_, bf16[256,4096]{1,0:T(8,128)(2,1)} %stack.41.xa_ref.refs_2_, ...), custom_call_target="tpu_custom_call" | custom-call | flops 1879048192 | bytes 16777216 | tf_op jit(solution)/shard_map/finish/pallas_call | solution.py:331
  244.6 1.5 copy-done.4
  (113 shorter events, 24.3 us)
Async XLA Ops:
  0.6 19.1 %copy-start.9 = (bf16[128,1,1280]{2,0,1:T(8,128)(2,1)S(1)}, bf16[128,1,1280]{2,0,1:T(8,128)(2,1)}, u32[]{:S(2)}) copy-start(bf16[128,1,1280]{2,0,1:T(8,128)(2,1)} %param.13) | copy-start | bytes 983044
  0.6 11.0 %collective-permute-start = (bf16[128,1024]{1,0:T(8,128)(2,1)}, bf16[128,1024]{1,0:T(8,128)(2,1)S(1)}, u32[]{:S(2)}, u32[]{:S(2)}) collective-permute-start(bf16[128,1024]{1,0:T(8,128)(2,1)} %bitcast.39), channel_id=1, source_target_pairs={{0,16},{16,0},{1,17},{17,1},{2,18},{18,2},{3,19},{19,3},{4,20},{20... | collective-permute-start | bytes 786440 | tf_op jit(solution)/shard_map/ppermute | solution.py:30
  2.8 14.0 %collective-permute-start.1 = (bf16[128,1024]{1,0:T(8,128)(2,1)}, bf16[128,1024]{1,0:T(8,128)(2,1)S(1)}, u32[]{:S(2)}, u32[]{:S(2)}) collective-permute-start(bf16[128,1024]{1,0:T(8,128)(2,1)} %bitcast.40), channel_id=1, source_target_pairs={{0,64},{64,0},{16,80},{80,16},{1,65},{65,1},{17,81},{81,17},{2,66}... | collective-permute-start | bytes 786440 | tf_op jit(solution)/shard_map/ppermute | solution.py:379
  5.2 13.6 %collective-permute-start.2 = (bf16[128,1024]{1,0:T(8,128)(2,1)}, bf16[128,1024]{1,0:T(8,128)(2,1)S(1)}, u32[]{:S(2)}, u32[]{:S(2)}) collective-permute-start(bf16[128,1024]{1,0:T(8,128)(2,1)} %bitcast.41), channel_id=1, source_target_pairs={{0,80},{80,0},{16,64},{64,16},{1,81},{81,1},{17,65},{65,17},{2,82}... | collective-permute-start | bytes 786440 | tf_op jit(solution)/shard_map/ppermute | solution.py:380
  5.2 14.4 %collective-permute-start.3 = (bf16[128,1280]{1,0:T(8,128)(2,1)}, bf16[128,1280]{1,0:T(8,128)(2,1)S(1)}, u32[]{:S(2)}, u32[]{:S(2)}) collective-permute-start(bf16[128,1280]{1,0:T(8,128)(2,1)} %bitcast.30), channel_id=1, source_target_pairs={{0,1},{1,2},{2,3},{3,0},{4,5},{5,6},{6,7},{7,4},{8,9},{9,10},{10,1... | collective-permute-start | bytes 983048 | tf_op jit(solution)/shard_map/ppermute | solution.py:41
  7.0 12.6 %collective-permute-start.4 = (bf16[128,1280]{1,0:T(8,128)(2,1)}, bf16[128,1280]{1,0:T(8,128)(2,1)S(1)}, u32[]{:S(2)}, u32[]{:S(2)}) collective-permute-start(bf16[128,1280]{1,0:T(8,128)(2,1)} %bitcast.31), channel_id=1, source_target_pairs={{0,2},{1,3},{2,0},{3,1},{4,6},{5,7},{6,4},{7,5},{8,10},{9,11},{10,... | collective-permute-start | bytes 983048 | tf_op jit(solution)/shard_map/ppermute | solution.py:41
  11.7 8.0 %collective-permute-start.5 = (bf16[128,1280]{1,0:T(8,128)(2,1)}, bf16[128,1280]{1,0:T(8,128)(2,1)S(1)}, u32[]{:S(2)}, u32[]{:S(2)}) collective-permute-start(bf16[128,1280]{1,0:T(8,128)(2,1)} %bitcast.32), channel_id=1, source_target_pairs={{0,3},{1,0},{2,1},{3,2},{4,7},{5,4},{6,5},{7,6},{8,11},{9,8},{10,9... | collective-permute-start | bytes 983048 | tf_op jit(solution)/shard_map/ppermute | solution.py:41
  16.8 7.8 %collective-permute-start.6 = (bf16[128,1280]{1,0:T(8,128)(2,1)}, bf16[128,1280]{1,0:T(8,128)(2,1)S(1)}, u32[]{:S(2)}, u32[]{:S(2)}) collective-permute-start(bf16[128,1280]{1,0:T(8,128)(2,1)} %bitcast.33), channel_id=1, source_target_pairs={{0,16},{16,0},{1,17},{17,1},{2,18},{18,2},{3,19},{19,3},{4,20},{20... | collective-permute-start | bytes 983048 | tf_op jit(solution)/shard_map/ppermute | solution.py:30
  19.8 1.1 copy-start.2
  29.2 32.7 %copy-start.3 = (bf16[512,1280]{1,0:T(8,128)(2,1)S(1)}, bf16[512,1280]{1,0:T(8,128)(2,1)}, u32[]{:S(2)}) copy-start(bf16[512,1280]{1,0:T(8,128)(2,1)} %copy-done.2) | copy-start | bytes 3932164
  61.9 6.3 %copy-start.7 = (bf16[128,1280]{1,0:T(8,128)(2,1)S(1)}, bf16[128,1280]{1,0:T(8,128)(2,1)}, u32[]{:S(2)}) copy-start(bf16[128,1280]{1,0:T(8,128)(2,1)} %copy-done.6) | copy-start | bytes 983044
  63.1 26.7 %collective-permute-start.15 = (bf16[512,1280]{1,0:T(8,128)(2,1)}, bf16[512,1280]{1,0:T(8,128)(2,1)}, u32[]{:S(2)}, u32[]{:S(2)}) collective-permute-start(bf16[512,1280]{1,0:T(8,128)(2,1)} %stack.42.rest_0_), channel_id=1, source_target_pairs={{0,4},{1,5},{2,6},{3,7},{4,8},{5,9},{6,10},{7,11},{8,12},{9,13},{1... | collective-permute-start | bytes 3932168 | tf_op jit(solution)/shard_map/ppermute | solution.py:41
  64.3 56.6 %collective-permute-start.7 = (bf16[256,4096]{1,0:T(8,128)(2,1)S(1)}, bf16[256,4096]{1,0:T(8,128)(2,1)}, u32[]{:S(2)}, u32[]{:S(2)}) collective-permute-start(bf16[256,4096]{1,0:T(8,128)(2,1)S(1)} %bitcast.24), channel_id=1, source_target_pairs={{0,32},{32,0},{1,33},{33,1},{2,34},{34,2},{3,35},{35,3},{4,36},{36... | collective-permute-start | bytes 6291464 | tf_op jit(solution)/shard_map/ppermute | solution.py:30
  68.2 11.1 %collective-permute-start.9 = (bf16[128,1280]{1,0:T(8,128)(2,1)S(1)}, bf16[128,1280]{1,0:T(8,128)(2,1)S(1)}, u32[]{:S(2)}, u32[]{:S(2)}) collective-permute-start(bf16[128,1280]{1,0:T(8,128)(2,1)S(1)} %stack.39.refs_0_), channel_id=1, source_target_pairs={{0,1},{1,2},{2,3},{3,0},{4,5},{5,6},{6,7},{7,4},{8,9},{9,10},{10,1... | collective-permute-start | bytes 983048 | tf_op jit(solution)/shard_map/ppermute | solution.py:41
  69.0 18.2 %collective-permute-start.10 = (bf16[128,1280]{1,0:T(8,128)(2,1)S(1)}, bf16[128,1280]{1,0:T(8,128)(2,1)S(1)}, u32[]{:S(2)}, u32[]{:S(2)}) collective-permute-start(bf16[128,1280]{1,0:T(8,128)(2,1)S(1)} %stack.39.refs_0_), channel_id=1, source_target_pairs={{0,2},{1,3},{2,0},{3,1},{4,6},{5,7},{6,4},{7,5},{8,10},{9,11},{10,... | collective-permute-start | bytes 983048 | tf_op jit(solution)/shard_map/ppermute | solution.py:41
  71.8 16.5 %collective-permute-start.11 = (bf16[128,1280]{1,0:T(8,128)(2,1)S(1)}, bf16[128,1280]{1,0:T(8,128)(2,1)S(1)}, u32[]{:S(2)}, u32[]{:S(2)}) collective-permute-start(bf16[128,1280]{1,0:T(8,128)(2,1)S(1)} %stack.39.refs_0_), channel_id=1, source_target_pairs={{0,3},{1,0},{2,1},{3,2},{4,7},{5,4},{6,5},{7,6},{8,11},{9,8},{10,9... | collective-permute-start | bytes 983048 | tf_op jit(solution)/shard_map/ppermute | solution.py:41
  79.3 55.8 %collective-permute-start.8 = (bf16[256,4096]{1,0:T(8,128)(2,1)S(1)}, bf16[256,4096]{1,0:T(8,128)(2,1)}, u32[]{:S(2)}, u32[]{:S(2)}) collective-permute-start(bf16[256,4096]{1,0:T(8,128)(2,1)S(1)} %bitcast.26), channel_id=1, source_target_pairs={{0,64},{64,0},{1,65},{65,1},{2,66},{66,2},{3,67},{67,3},{4,68},{68... | collective-permute-start | bytes 6291464 | tf_op jit(solution)/shard_map/ppermute | solution.py:30
  87.2 17.1 %collective-permute-start.16 = (bf16[512,1280]{1,0:T(8,128)(2,1)}, bf16[512,1280]{1,0:T(8,128)(2,1)}, u32[]{:S(2)}, u32[]{:S(2)}) collective-permute-start(bf16[512,1280]{1,0:T(8,128)(2,1)} %stack.42.rest_0_), channel_id=1, source_target_pairs={{0,12},{1,13},{2,14},{3,15},{4,0},{5,1},{6,2},{7,3},{8,4},{9,5},{1... | collective-permute-start | bytes 3932168 | tf_op jit(solution)/shard_map/ppermute | solution.py:41
  89.5 18.3 %collective-permute-start.12 = (bf16[512,1280]{1,0:T(8,128)(2,1)}, bf16[512,1280]{1,0:T(8,128)(2,1)S(1)}, u32[]{:S(2)}, u32[]{:S(2)}) collective-permute-start(bf16[512,1280]{1,0:T(8,128)(2,1)} %stack.40.rest_5_), channel_id=1, source_target_pairs={{0,4},{1,5},{2,6},{3,7},{4,8},{5,9},{6,10},{7,11},{8,12},{9,13},{1... | collective-permute-start | bytes 3932168 | tf_op jit(solution)/shard_map/ppermute | solution.py:41
  89.8 28.5 %collective-permute-start.13 = (bf16[512,1280]{1,0:T(8,128)(2,1)}, bf16[512,1280]{1,0:T(8,128)(2,1)}, u32[]{:S(2)}, u32[]{:S(2)}) collective-permute-start(bf16[512,1280]{1,0:T(8,128)(2,1)} %stack.40.rest_5_), channel_id=1, source_target_pairs={{0,12},{1,13},{2,14},{3,15},{4,0},{5,1},{6,2},{7,3},{8,4},{9,5},{1... | collective-permute-start | bytes 3932168 | tf_op jit(solution)/shard_map/ppermute | solution.py:41
  94.2 29.4 %copy-start.11 = (f32[4096]{0:T(1024)S(1)}, f32[4096]{0:T(1024)}, u32[]{:S(2)}) copy-start(f32[4096]{0:T(1024)} %param.12) | copy-start | bytes 49156
  104.2 24.0 %collective-permute-start.17 = (bf16[256,1280]{1,0:T(8,128)(2,1)}, bf16[256,1280]{1,0:T(8,128)(2,1)}, u32[]{:S(2)}, u32[]{:S(2)}) collective-permute-start(bf16[256,1280]{1,0:T(8,128)(2,1)} %slice.71), channel_id=1, source_target_pairs={{0,4},{1,5},{2,6},{3,7},{4,8},{5,9},{6,10},{7,11},{8,12},{9,13},{1... | collective-permute-start | bytes 1966088 | tf_op jit(solution)/shard_map/ppermute | solution.py:41
  107.8 20.5 %collective-permute-start.18 = (bf16[256,1280]{1,0:T(8,128)(2,1)}, bf16[256,1280]{1,0:T(8,128)(2,1)}, u32[]{:S(2)}, u32[]{:S(2)}) collective-permute-start(bf16[256,1280]{1,0:T(8,128)(2,1)} %slice.72), channel_id=1, source_target_pairs={{0,12},{1,13},{2,14},{3,15},{4,0},{5,1},{6,2},{7,3},{8,4},{9,5},{1... | collective-permute-start | bytes 1966088 | tf_op jit(solution)/shard_map/ppermute | solution.py:41
  118.3 11.3 %collective-permute-start.19 = (bf16[256,1280]{1,0:T(8,128)(2,1)}, bf16[256,1280]{1,0:T(8,128)(2,1)}, u32[]{:S(2)}, u32[]{:S(2)}) collective-permute-start(bf16[256,1280]{1,0:T(8,128)(2,1)} %slice.73), channel_id=1, source_target_pairs={{0,4},{1,5},{2,6},{3,7},{4,8},{5,9},{6,10},{7,11},{8,12},{9,13},{1... | collective-permute-start | bytes 1966088 | tf_op jit(solution)/shard_map/ppermute | solution.py:41
  120.9 11.5 %collective-permute-start.20 = (bf16[256,1280]{1,0:T(8,128)(2,1)}, bf16[256,1280]{1,0:T(8,128)(2,1)}, u32[]{:S(2)}, u32[]{:S(2)}) collective-permute-start(bf16[256,1280]{1,0:T(8,128)(2,1)} %slice.74), channel_id=1, source_target_pairs={{0,12},{1,13},{2,14},{3,15},{4,0},{5,1},{6,2},{7,3},{8,4},{9,5},{1... | collective-permute-start | bytes 1966088 | tf_op jit(solution)/shard_map/ppermute | solution.py:41
  123.5 8.8 %copy-start.5 = (bf16[256,1024]{1,0:T(8,128)(2,1)S(1)}, bf16[256,1024]{1,0:T(8,128)(2,1)}, u32[]{:S(2)}) copy-start(bf16[256,1024]{1,0:T(8,128)(2,1)} %pad_maximum_fusion.rest_0_.refs_0_) | copy-start | bytes 1572868
  128.2 4.1 %copy-start = (bf16[512,4096]{1,0:T(8,128)(2,1)}, bf16[512,4096]{1,0:T(8,128)(2,1)S(1)}, u32[]{:S(2)}) copy-start(bf16[512,4096]{1,0:T(8,128)(2,1)S(1)} %normalize.2.normed_ref.refs_5_) | copy-start | bytes 12582916
  132.4 15.2 %collective-permute-start.21 = (bf16[256,1024]{1,0:T(8,128)(2,1)S(1)}, bf16[256,1024]{1,0:T(8,128)(2,1)S(1)}, u32[]{:S(2)}, u32[]{:S(2)}) collective-permute-start(bf16[256,1024]{1,0:T(8,128)(2,1)S(1)} %stack.43.refs_0_), channel_id=1, source_target_pairs={{0,1},{1,2},{2,3},{3,0},{4,5},{5,6},{6,7},{7,4},{8,9},{9,10},{10,1... | collective-permute-start | bytes 1572872 | tf_op jit(solution)/shard_map/ppermute | solution.py:41
  132.5 15.1 %collective-permute-start.22 = (bf16[256,1024]{1,0:T(8,128)(2,1)S(1)}, bf16[256,1024]{1,0:T(8,128)(2,1)S(1)}, u32[]{:S(2)}, u32[]{:S(2)}) collective-permute-start(bf16[256,1024]{1,0:T(8,128)(2,1)S(1)} %stack.43.refs_0_), channel_id=1, source_target_pairs={{0,2},{1,3},{2,0},{3,1},{4,6},{5,7},{6,4},{7,5},{8,10},{9,11},{10,... | collective-permute-start | bytes 1572872 | tf_op jit(solution)/shard_map/ppermute | solution.py:41
  132.6 15.7 %collective-permute-start.23 = (bf16[256,1024]{1,0:T(8,128)(2,1)S(1)}, bf16[256,1024]{1,0:T(8,128)(2,1)S(1)}, u32[]{:S(2)}, u32[]{:S(2)}) collective-permute-start(bf16[256,1024]{1,0:T(8,128)(2,1)S(1)} %stack.43.refs_0_), channel_id=1, source_target_pairs={{0,3},{1,0},{2,1},{3,2},{4,7},{5,4},{6,5},{7,6},{8,11},{9,8},{10,9... | collective-permute-start | bytes 1572872 | tf_op jit(solution)/shard_map/ppermute | solution.py:41
  138.2 14.2 %copy-start.13 = (s32[4,32]{1,0:T(4,128)S(1)}, s32[4,32]{1,0:T(4,128)}, u32[]{:S(2)}) copy-start(s32[4,32]{1,0:T(4,128)} %param.9) | copy-start | bytes 1540
  138.2 14.2 %copy-start.14 = (s32[4,32]{1,0:T(4,128)S(1)}, s32[4,32]{1,0:T(4,128)}, u32[]{:S(2)}) copy-start(s32[4,32]{1,0:T(4,128)} %param.10) | copy-start | bytes 1540
  138.3 17.9 %collective-permute-start.14 = (bf16[256,4096]{1,0:T(8,128)(2,1)}, bf16[256,4096]{1,0:T(8,128)(2,1)}, u32[]{:S(2)}, u32[]{:S(2)}) collective-permute-start(bf16[256,4096]{1,0:T(8,128)(2,1)} %stack.41.xa_ref.refs_2_), channel_id=1, source_target_pairs={{0,32},{32,0},{1,33},{33,1},{2,34},{34,2},{3,35},{35,3},{4,36},{36... | collective-permute-start | bytes 6291464 | tf_op jit(solution)/shard_map/ppermute | solution.py:30
  149.7 26.7 %collective-permute-start.24 = (bf16[1024,1024]{1,0:T(8,128)(2,1)}, bf16[1024,1024]{1,0:T(8,128)(2,1)}, u32[]{:S(2)}, u32[]{:S(2)}) collective-permute-start(bf16[1024,1024]{1,0:T(8,128)(2,1)} %stack.44.refs_1_), channel_id=1, source_target_pairs={{0,4},{1,5},{2,6},{3,7},{4,8},{5,9},{6,10},{7,11},{8,12},{9,13},{1... | collective-permute-start | bytes 6291464 | tf_op jit(solution)/shard_map/ppermute | solution.py:41
  150.0 28.8 %collective-permute-start.25 = (bf16[1024,1024]{1,0:T(8,128)(2,1)}, bf16[1024,1024]{1,0:T(8,128)(2,1)}, u32[]{:S(2)}, u32[]{:S(2)}) collective-permute-start(bf16[1024,1024]{1,0:T(8,128)(2,1)} %stack.44.refs_1_), channel_id=1, source_target_pairs={{0,12},{1,13},{2,14},{3,15},{4,0},{5,1},{6,2},{7,3},{8,4},{9,5},{1... | collective-permute-start | bytes 6291464 | tf_op jit(solution)/shard_map/ppermute | solution.py:41
  156.2 5.3 %copy-start.10 = (s32[2,256,1]{2,1,0:T(8,128)S(1)}, s32[2,256,1]{2,1,0:T(8,128)}, u32[]{:S(2)}) copy-start(s32[2,256,1]{2,1,0:T(8,128)} %copy.17.segq_ref) | copy-start | bytes 6148
  161.5 22.2 %copy-start.1 = (bf16[512,4096]{1,0:T(8,128)(2,1)S(1)}, bf16[512,4096]{1,0:T(8,128)(2,1)}, u32[]{:S(2)}) copy-start(bf16[512,4096]{1,0:T(8,128)(2,1)} %copy-done) | copy-start | bytes 12582916
  175.7 8.0 %copy-start.8 = (s32[2,256,1]{2,1,0:T(8,128)S(1)}, s32[2,256,1]{2,1,0:T(8,128)}, u32[]{:S(2)}) copy-start(s32[2,256,1]{2,1,0:T(8,128)} %copy.16.segq_ref) | copy-start | bytes 6148
  175.7 46.0 %collective-permute-start.27 = (bf16[512,1024]{1,0:T(8,128)(2,1)}, bf16[512,1024]{1,0:T(8,128)(2,1)}, u32[]{:S(2)}, u32[]{:S(2)}) collective-permute-start(bf16[512,1024]{1,0:T(8,128)(2,1)} %attend.3.mixed_b_ref), channel_id=1, source_target_pairs={{0,64},{64,0},{1,65},{65,1},{2,66},{66,2},{3,67},{67,3},{4,68},{68... | collective-permute-start | bytes 3145736 | tf_op jit(solution)/shard_map/ppermute | solution.py:30
  178.7 21.8 %collective-permute-start.26 = (bf16[512,1024]{1,0:T(8,128)(2,1)}, bf16[512,1024]{1,0:T(8,128)(2,1)}, u32[]{:S(2)}, u32[]{:S(2)}) collective-permute-start(bf16[512,1024]{1,0:T(8,128)(2,1)} %slice.76), channel_id=1, source_target_pairs={{0,4},{1,5},{2,6},{3,7},{4,8},{5,9},{6,10},{7,11},{8,12},{9,13},{1... | collective-permute-start | bytes 3145736 | tf_op jit(solution)/shard_map/ppermute | solution.py:41
  181.0 19.2 %copy-start.12 = (f32[4096]{0:T(1024)S(1)}, f32[4096]{0:T(1024)}, u32[]{:S(2)}) copy-start(f32[4096]{0:T(1024)} %param.15) | copy-start | bytes 49156
  181.0 36.2 %collective-permute-start.29 = (bf16[512,1024]{1,0:T(8,128)(2,1)}, bf16[512,1024]{1,0:T(8,128)(2,1)}, u32[]{:S(2)}, u32[]{:S(2)}) collective-permute-start(bf16[512,1024]{1,0:T(8,128)(2,1)} %slice.77), channel_id=1, source_target_pairs={{0,12},{1,13},{2,14},{3,15},{4,0},{5,1},{6,2},{7,3},{8,4},{9,5},{1... | collective-permute-start | bytes 3145736 | tf_op jit(solution)/shard_map/ppermute | solution.py:41
  197.8 23.9 %collective-permute-start.28 = (bf16[512,1024]{1,0:T(8,128)(2,1)}, bf16[512,1024]{1,0:T(8,128)(2,1)S(1)}, u32[]{:S(2)}, u32[]{:S(2)}) collective-permute-start(bf16[512,1024]{1,0:T(8,128)(2,1)} %attend.2.mixed_a_ref), channel_id=1, source_target_pairs={{0,64},{64,0},{1,65},{65,1},{2,66},{66,2},{3,67},{67,3},{4,68},{68... | collective-permute-start | bytes 3145736 | tf_op jit(solution)/shard_map/ppermute | solution.py:30
  213.1 25.9 %collective-permute-start.30 = (bf16[1024,1024]{1,0:T(8,128)(2,1)S(1)}, bf16[1024,1024]{1,0:T(8,128)(2,1)S(1)}, u32[]{:S(2)}, u32[]{:S(2)}) collective-permute-start(bf16[1024,1024]{1,0:T(8,128)(2,1)S(1)} %get-tuple-element.10), channel_id=1, source_target_pairs={{0,32},{32,0},{1,33},{33,1},{2,34},{34,2},{3,35},{35,3},{4,36},{36... | collective-permute-start | bytes 6291464 | tf_op jit(solution)/shard_map/ppermute | solution.py:30
  229.5 9.5 %collective-permute-start.31 = (bf16[1024,1024]{1,0:T(8,128)(2,1)S(1)}, bf16[1024,1024]{1,0:T(8,128)(2,1)S(1)}, u32[]{:S(2)}, u32[]{:S(2)}) collective-permute-start(bf16[1024,1024]{1,0:T(8,128)(2,1)S(1)} %get-tuple-element.11), channel_id=1, source_target_pairs={{0,32},{32,0},{1,33},{33,1},{2,34},{34,2},{3,35},{35,3},{4,36},{36... | collective-permute-start | bytes 6291464 | tf_op jit(solution)/shard_map/ppermute | solution.py:30
  234.4 2.7 %collective-permute-start.32 = (f32[1,128]{1,0:T(1,128)S(1)}, f32[1,128]{1,0:T(1,128)S(1)}, u32[]{:S(2)}, u32[]{:S(2)}) collective-permute-start(f32[1,128]{1,0:T(1,128)S(1)} %add_add_fusion), channel_id=1, source_target_pairs={{0,32},{32,0},{1,33},{33,1},{2,34},{34,2},{3,35},{35,3},{4,36},{36... | collective-permute-start | bytes 1544 | tf_op jit(solution)/shard_map/ppermute | solution.py:30
  237.2 7.4 %collective-permute-start.33 = (f32[1,128]{1,0:T(1,128)S(1)}, f32[1,128]{1,0:T(1,128)S(1)}, u32[]{:S(2)}, u32[]{:S(2)}) collective-permute-start(f32[1,128]{1,0:T(1,128)S(1)} %add.86), channel_id=1, source_target_pairs={{0,64},{64,0},{1,65},{65,1},{2,66},{66,2},{3,67},{67,3},{4,68},{68... | collective-permute-start | bytes 1544 | tf_op jit(solution)/shard_map/ppermute | solution.py:30
  244.6 1.5 copy-start.4
  (1 other events, 0.7 us)
